TPU v7x, 32 devices: a whole 2x2x4 slice. The times are simulated.
32 devices in a mesh: row: 8 (over y, x, core), col: 4 (over z).
Axes of the slice: x: 2, y: 2, z: 4, core: 2. Of those that a mesh axis runs over, the one named last changes fastest.
Arguments:
- tokens: bfloat16 [16384, 2048], P('row', 'col'), may hold values from -6 to 6
- segment_ids: int32 [16, 1024], P('row'), may hold values from 0 to 7, never falling along the last dimension, each value on 1 to 512 neighbouring positions
- norm_gain: float32 [2048], P('col'), may hold values from 0.5 to 1.5
- in_zx: bfloat16 [2048, 2, 4096], P('row', None, 'col'), may hold values from -0.125 to 0.125
- in_dt: bfloat16 [2048, 64], P('row', 'col'), may hold values from -0.125 to 0.125
- in_bc: bfloat16 [2048, 256], P('row', 'col'), may hold values from -0.125 to 0.125
- conv_x: float32 [4, 4096], P(None, 'col'), may hold values from -3 to 3
- conv_x_bias: float32 [4096], P('col'), may hold values from -3 to 3
- conv_bc: float32 [4, 256], P(None, 'col'), may hold values from -3 to 3
- conv_bc_bias: float32 [256], P('col'), may hold values from -3 to 3
- dt_bias: float32 [64], P('col'), may hold values from -5 to -1.5
- a_log: float32 [64], P('col'), may hold values from 0 to 2.77
- d_skip: float32 [64], P('col'), may hold values from 0.5 to 1.5
- inner_gain: float32 [4096], P('col'), may hold values from 0.5 to 1.5
- out_proj: bfloat16 [2048, 4096], P('row', 'col'), may hold values from -0.09375 to 0.09375
- cotangent: bfloat16 [16384, 2048], P('row', 'col'), may hold values from -6 to 6
Outputs:
- output: bfloat16 [16384, 2048], P('row', 'col')
- tokens_grad: bfloat16 [16384, 2048], P('row', 'col')
- norm_gain_grad: float32 [2048], P('col')
- in_zx_grad: float32 [2048, 2, 4096], P('row', None, 'col')
- in_dt_grad: float32 [2048, 64], P('row', 'col')
- in_bc_grad: float32 [2048, 256], P('row', 'col')
- conv_x_grad: float32 [4, 4096], P(None, 'col')
- conv_x_bias_grad: float32 [4096], P('col')
- conv_bc_grad: float32 [4, 256], P(None, 'col')
- conv_bc_bias_grad: float32 [256], P('col')
- dt_bias_grad: float32 [64], P('col')
- a_log_grad: float32 [64], P('col')
- d_skip_grad: float32 [64], P('col')
- inner_gain_grad: float32 [4096], P('col')
- out_proj_grad: float32 [2048, 4096], P('row', 'col')
Inputs may be any that keep to these rules, and one draw needn't show every extreme that they name: `segment_ids`: within each row (one packed sequence) ids never fall; each document covers at most 512 tokens, and some document exactly that many.
All inputs are finite; a program needn't handle non-finite values.
Results may differ from a plain program's by a relative error of at most 0.012.
Values may be sent and summed in bfloat16 or wider, within the bound.
A program may use at most 320 MiB of HBM per device.

v0:
```python
import jax
import jax.numpy as jnp
from jax import lax
from jax.sharding import PartitionSpec as P

D = 2048
HEADDIM = 64
STATE = 128
SPAN = 256
SEQLEN = 1024
INNER = 4096


EPS = 1e-05


def causal_conv(values, weight, shift_add, seg_rows):
    taps = weight.shape[0]
    length = values.shape[1]
    total = shift_add + weight[taps - 1] * values
    for lag_step in range(1, taps):
        earlier = jnp.pad(values, ((0, 0), (lag_step, 0), (0, 0)))[:, :length]
        earlier_seg = jnp.pad(seg_rows, ((0, 0), (lag_step, 0)), constant_values=-1)[:, :length]
        keeper = (earlier_seg == seg_rows).astype(values.dtype)
        total = total + weight[taps - 1 - lag_step] * earlier * keeper[..., None]
    return total


def span_scan(x_heads, b_rows, c_rows, dt_step, decay_rate, seg_line):
    highest = lax.Precision.HIGHEST
    length, heads, hdim = x_heads.shape
    nstate = b_rows.shape[1]
    blocks = length // SPAN
    x_blocks = x_heads.reshape(blocks, SPAN, heads, hdim)
    b_blocks = b_rows.reshape(blocks, SPAN, nstate)
    c_blocks = c_rows.reshape(blocks, SPAN, nstate)
    dt_blocks = dt_step.reshape(blocks, SPAN, heads)
    seg_blocks = seg_line.reshape(blocks, SPAN)
    log_decay = jnp.cumsum(-dt_blocks * decay_rate, axis=1)
    positions = jnp.arange(SPAN)
    causal = positions[:, None] >= positions[None, :]
    same_doc = (seg_blocks[:, :, None] == seg_blocks[:, None, :]) & causal[None]
    same_mask = same_doc[..., None]
    log_gap = log_decay[:, :, None, :] - log_decay[:, None, :, :]
    decays = jnp.where(same_mask, jnp.exp(jnp.where(same_mask, log_gap, 0.0)), 0.0)
    scores = jnp.einsum("ctn,csn->cts", c_blocks, b_blocks, precision=highest)
    weights = scores[..., None] * decays * dt_blocks[:, None, :, :]
    intra_out = jnp.einsum("ctsh,cshp->cthp", weights, x_blocks, precision=highest)
    last_seg = seg_blocks[:, -1]
    tail_mask = (seg_blocks == last_seg[:, None]).astype(x_heads.dtype)
    to_end = jnp.exp(log_decay[:, -1:, :] - log_decay) * dt_blocks * tail_mask[..., None]
    local_state = jnp.einsum("csh,cshp,csn->chpn", to_end, x_blocks, b_blocks, precision=highest)
    prev_last = jnp.concatenate([jnp.full((1,), -1, jnp.int32), last_seg[:-1]])
    carry_on = (last_seg == prev_last).astype(x_heads.dtype)
    span_decay = jnp.exp(log_decay[:, -1, :])

    def advance(state, items):
        block_state, keeping, factor = items
        return (keeping * factor[:, None, None] * state + block_state, state)

    zero_state = jnp.zeros((heads, hdim, nstate), x_heads.dtype)
    _, entering = lax.scan(advance, zero_state, (local_state, carry_on, span_decay))
    head_mask = (seg_blocks == prev_last[:, None]).astype(x_heads.dtype)
    from_prev = jnp.einsum("ctn,chpn->cthp", c_blocks, entering, precision=highest)
    from_prev = from_prev * (jnp.exp(log_decay) * head_mask[..., None])[..., None]
    return (intra_out + from_prev).reshape(length, heads, hdim)


def contract_rows(left, right):
    return lax.dot_general(
        left, right, (((0,), (0,)), ((), ())), preferred_element_type=jnp.float32
    )


def contract_cols(left, right):
    return lax.dot_general(
        left, right, (((1,), (1,)), ((), ())), preferred_element_type=jnp.float32
    )


def per_device(
    tokens,
    segment_ids,
    norm_gain,
    in_zx,
    in_dt,
    in_bc,
    conv_x,
    conv_x_bias,
    conv_bc,
    conv_bc_bias,
    dt_bias,
    a_log,
    d_skip,
    inner_gain,
    out_proj,
    cotangent,
):
    row_count = tokens.shape[0]
    seq_count = segment_ids.shape[0]
    heads_here = dt_bias.shape[0]
    inner_here = inner_gain.shape[0]
    bc_here = conv_bc_bias.shape[0]
    x_full = tokens.astype(jnp.float32)
    sum_sq = lax.psum(jnp.sum(x_full * x_full, axis=1), "col")
    inv_root = lax.rsqrt(sum_sq / D + EPS)[:, None]
    normed_here = (x_full * inv_root * norm_gain).astype(jnp.bfloat16)
    normed = lax.all_gather(normed_here, "col", axis=1, tiled=True)
    proj_zx, proj_dt, proj_bc, proj_out = (
        lax.all_gather(in_zx, "row", axis=0, tiled=True),
        lax.all_gather(in_dt, "row", axis=0, tiled=True),
        lax.all_gather(in_bc, "row", axis=0, tiled=True),
        lax.all_gather(out_proj, "row", axis=0, tiled=True),
    )
    flat_zx = proj_zx.reshape(D, 2 * inner_here)
    zx_raw = jnp.dot(normed, flat_zx, preferred_element_type=jnp.float32)
    gate_raw = zx_raw[:, :inner_here]
    x_raw = zx_raw[:, inner_here:]
    dt_raw = jnp.dot(normed, proj_dt, preferred_element_type=jnp.float32)
    bc_raw = jnp.dot(normed, proj_bc, preferred_element_type=jnp.float32)

    def conv_piece(x_in, bc_in, taps_x, shift_x, taps_bc, shift_bc):
        x_out = jax.nn.silu(
            causal_conv(x_in.reshape(seq_count, SEQLEN, inner_here), taps_x, shift_x, segment_ids)
        )
        bc_out = jax.nn.silu(
            causal_conv(bc_in.reshape(seq_count, SEQLEN, bc_here), taps_bc, shift_bc, segment_ids)
        )
        return (x_out.reshape(row_count, inner_here), bc_out.reshape(row_count, bc_here))

    (x_conv, bc_conv), conv_pull = jax.vjp(
        conv_piece, x_raw, bc_raw, conv_x, conv_x_bias, conv_bc, conv_bc_bias
    )
    x_low = x_conv.astype(jnp.bfloat16)
    bc_low = bc_conv.astype(jnp.bfloat16)
    bc_all = lax.all_gather(bc_low, "col", axis=1, tiled=True)

    def scan_piece(x_in, bc_in, dt_in, gate_in, bias_dt, log_rate, skip_coef):
        dt_step = jax.nn.softplus(dt_in + bias_dt).reshape(seq_count, SEQLEN, heads_here)
        decay_rate = jnp.exp(log_rate)
        x_seq = x_in.reshape(seq_count, SEQLEN, heads_here, HEADDIM)
        b_seq = bc_in[:, :STATE].reshape(seq_count, SEQLEN, STATE)
        c_seq = bc_in[:, STATE:].reshape(seq_count, SEQLEN, STATE)
        scanned = jax.vmap(span_scan, in_axes=(0, 0, 0, 0, None, 0))(
            x_seq, b_seq, c_seq, dt_step, decay_rate, segment_ids
        )
        y_out = scanned.reshape(row_count, heads_here, HEADDIM) + skip_coef[:, None] * x_in.reshape(
            row_count, heads_here, HEADDIM
        )
        return y_out.reshape(row_count, inner_here) * jax.nn.silu(gate_in)

    gated, scan_pull = jax.vjp(
        scan_piece,
        x_low.astype(jnp.float32),
        bc_all.astype(jnp.float32),
        dt_raw,
        gate_raw,
        dt_bias,
        a_log,
        d_skip,
    )
    gate_sq = lax.psum(jnp.sum(gated * gated, axis=1), "col")
    inner_root = lax.rsqrt(gate_sq / INNER + EPS)[:, None]
    hidden = (gated * inner_root * inner_gain).astype(jnp.bfloat16)
    partial_out = contract_cols(hidden, proj_out)
    out_share = lax.psum_scatter(partial_out, "col", scatter_dimension=1, tiled=True)
    output = (out_share + x_full).astype(jnp.bfloat16)
    back_full = lax.all_gather(cotangent, "col", axis=1, tiled=True)
    proj_zx, proj_dt, proj_bc, proj_out = (
        lax.all_gather(in_zx, "row", axis=0, tiled=True),
        lax.all_gather(in_dt, "row", axis=0, tiled=True),
        lax.all_gather(in_bc, "row", axis=0, tiled=True),
        lax.all_gather(out_proj, "row", axis=0, tiled=True),
    )
    flat_zx = proj_zx.reshape(D, 2 * inner_here)
    d_hidden = jnp.dot(back_full, proj_out, preferred_element_type=jnp.float32)
    grad_out = contract_rows(back_full, hidden)
    scaled = d_hidden * inner_gain
    gate_dot = lax.psum(jnp.sum(scaled * gated, axis=1), "col")
    d_gated = inner_root * scaled - gated * inner_root**3 / INNER * gate_dot[:, None]
    grad_igain = jnp.sum(d_hidden * gated * inner_root, axis=0)
    dx_conv, dbc_all, ddt_raw, d_gate, grad_dtb, grad_alog, grad_dskip = scan_pull(d_gated)
    dbc_here = lax.psum_scatter(dbc_all, "col", scatter_dimension=1, tiled=True)
    dx_raw, dbc_raw, grad_cx, grad_cxb, grad_cb, grad_cbb = conv_pull((dx_conv, dbc_here))
    d_zx = jnp.concatenate([d_gate, dx_raw], axis=1).astype(jnp.bfloat16)
    d_dtr = ddt_raw.astype(jnp.bfloat16)
    d_bcr = dbc_raw.astype(jnp.bfloat16)
    grad_zx = contract_rows(normed, d_zx).reshape(D, 2, inner_here)
    grad_dt = contract_rows(normed, d_dtr)
    grad_bc = contract_rows(normed, d_bcr)
    d_normed = (
        contract_cols(d_zx, flat_zx) + contract_cols(d_dtr, proj_dt) + contract_cols(d_bcr, proj_bc)
    )
    d_here = lax.psum_scatter(d_normed, "col", scatter_dimension=1, tiled=True)
    norm_dot = lax.psum(jnp.sum(d_here * norm_gain * x_full, axis=1), "col")
    tokens_grad = (
        cotangent.astype(jnp.float32)
        + inv_root * norm_gain * d_here
        - x_full * inv_root**3 / D * norm_dot[:, None]
    ).astype(jnp.bfloat16)
    grad_gain = jnp.sum(d_here * x_full * inv_root, axis=0)
    g_zx, g_dt, g_bc, g_out = (
        lax.psum_scatter(grad_zx, "row", scatter_dimension=0, tiled=True),
        lax.psum_scatter(grad_dt, "row", scatter_dimension=0, tiled=True),
        lax.psum_scatter(grad_bc, "row", scatter_dimension=0, tiled=True),
        lax.psum_scatter(grad_out, "row", scatter_dimension=0, tiled=True),
    )
    summed_small = lax.psum(
        (
            grad_gain,
            grad_cx,
            grad_cxb,
            grad_cb,
            grad_cbb,
            grad_dtb,
            grad_alog,
            grad_dskip,
            grad_igain,
        ),
        "row",
    )
    return (
        output,
        tokens_grad,
        summed_small[0],
        g_zx,
        g_dt,
        g_bc,
        summed_small[1],
        summed_small[2],
        summed_small[3],
        summed_small[4],
        summed_small[5],
        summed_small[6],
        summed_small[7],
        summed_small[8],
        g_out,
    )


def solution(mesh):
    in_specs = (
        P("row", "col"),
        P("row", None),
        P("col"),
        P("row", None, "col"),
        P("row", "col"),
        P("row", "col"),
        P(None, "col"),
        P("col"),
        P(None, "col"),
        P("col"),
        P("col"),
        P("col"),
        P("col"),
        P("col"),
        P("row", "col"),
        P("row", "col"),
    )
    out_specs = (
        P("row", "col"),
        P("row", "col"),
        P("col"),
        P("row", None, "col"),
        P("row", "col"),
        P("row", "col"),
        P(None, "col"),
        P("col"),
        P(None, "col"),
        P("col"),
        P("col"),
        P("col"),
        P("col"),
        P("col"),
        P("row", "col"),
    )
    return jax.shard_map(
        per_device, mesh=mesh, in_specs=in_specs, out_specs=out_specs, check_vma=False
    )
```

profile of v0, /device:TPU:0, one launch (start us, length us, event | category | flops | bytes accessed | tf_op | source)
XLA Modules:
  0.0 1768.3 jit_solution(11300912638570919922)
XLA Ops:
  37.9 137.8 %all-gather.6.cloned.1.call-done = bf16[2048,2048]{1,0:T(8,128)(2,1)} async-done(((bf16[2048,512]{1,0:T(8,128)(2,1)}), bf16[2048,2048]{1,0:T(8,128)(2,1)}) %all-gather.6.cloned.1.call-update) | async-done | bytes 8388624 | tf_op jit(solution)/shard_map/all_gather | solution.py:108
  215.4 52.2 %all-gather.8.cloned.1.call-done = bf16[2048,2,1024]{2,1,0:T(2,128)(2,1)} async-done(((bf16[256,2,1024]{2,1,0:T(2,128)(2,1)}), bf16[2048,2,1024]{2,1,0:T(2,128)(2,1)}) %all-gather.8.cloned.1.call-update) | async-done | bytes 8388624 | tf_op jit(solution)/shard_map/all_gather | solution.py:110
  277.8 21.5 %fusion.127 = f32[2048,2048]{1,0:T(8,128)S(1)} fusion(bf16[2048,2048]{1,0:T(8,128)(2,1)} %all-gather.6.cloned.1.call-done, bf16[2048,2048]{1,0:T(8,128)(2,1)} %bitcast.308), kind=kOutput, calls=%fused_computation.236 | convolution fusion | flops 17179869184 | bytes 33554432 | tf_op jit(solution)/shard_map/dot_general | solution.py:116
  316.6 20.2 %multiply_convert_fusion.1 = (bf16[2,1024,1024]{1,2,0:T(8,128)(2,1)}, f32[2,1024,1024]{1,2,0:T(8,128)}) fusion(f32[2,1024]{1,0:T(2,128)S(1)} %get-tuple-element.598, f32[2,1024,1024]{1,2,0:T(8,128)} %copy.323, f32[1024]{0:T(1024)S(1)} %bitcast.334, f32[2,1024]{1,0:T(2,128)S(1)} %get-tuple-element.597, f32[1024]{0:T(1024)S(1)} %bitcast.336, ...), kind=kLoop, calls=%fused_computation.90 | loop fusion | flops 33554432 | bytes 21016576 | tf_op jit(solution)/shard_map/convert_element_type | solution.py:134
  381.8 27.9 %bitcast_add_fusion.3 = f32[2,4,256,16,64]{2,4,3,1,0:T(8,128)} fusion(f32[2,4,256,16,64]{2,4,3,1,0:T(8,128)S(1)} %fusion.65, f32[2,4,256,16]{2,3,1,0:T(8,128)S(1)} %get-tuple-element.584, f32[2,4,256,16]{2,3,1,0:T(8,128)S(1)} %copy-done.45, f32[2,4,256,16]{2,3,1,0:T(8,128)S(1)} %copy-done.35, f32[2,4,256,256]{3,2,1,0:T(8,128)S(1)} %copy-done.18, ...), kind=kOutput, calls=%fused_computation.72 | convolution fusion | flops 6488588288 | bytes 23986176 | tf_op jit(solution)/shard_map/jvp(vmap(ctsh,cshp->cthp))/dot_general | solution.py:48
  463.9 16.7 multiply_reduce_fusion.2
  489.2 21.3 %fusion.36 = (f32[1024]{0:T(1024)}, f32[2048,1024]{1,0:T(8,128)}, bf16[2048,1024]{1,0:T(8,128)(2,1)}) fusion(f32[2,1024,1024]{2,1,0:T(8,128)} %copy.349, f32[2048,2048]{1,0:T(8,128)} %copy-done.2, f32[2048]{0:T(1024)S(1)} %broadcast_multiply_fusion.1, f32[2048,1024]{1,0:T(8,128)} %get-tuple-element.562, f32[2048]{0:T(1024)S(1)} %get-tuple-element.592, ...), kind=kLoop, calls=%fused_computation.71 | loop fusion | flops 46136320 | bytes 54562816 | tf_op jit(solution)/shard_map/transpose(jvp())/reduce_sum | solution.py:147
  530.5 17.7 %fusion.80 = f32[2,4,256,128]{3,2,1,0:T(8,128)S(1)} fusion(f32[4,2,16,64,128]{4,3,2,1,0:T(8,128)} %get-tuple-element.747, f32[2,4,256,16,64]{2,1,0,4,3:T(4,128)} %reshape.395, f32[2,4,256,16]{2,3,1,0:T(8,128)S(1)} %get-tuple-element.584), kind=kOutput, calls=%fused_computation.135 | convolution fusion | flops 3223322624 | bytes 13762560 | tf_op jit(solution)/shard_map/transpose(jvp(vmap(ctn,chpn->cthp)))/dot_general | solution.py:64
  592.8 44.1 %fusion.13 = (f32[2,4,256,16]{2,3,1,0:T(8,128)}, f32[2,4,256,16]{2,3,1,0:T(8,128)}, f32[2,4,256,16]{2,3,1,0:T(8,128)}, f32[2,4,256,256]{3,2,1,0:T(8,128)S(1)}) fusion(f32[2,4,256,16]{2,3,1,0:T(8,128)S(1)} %copy-done.46, f32[2,4,256,16]{2,3,1,0:T(8,128)S(1)} %copy-done.35, f32[2,4,256,256]{3,2,1,0:T(8,128)S(1)} %copy-done.19, ...), kind=kOutput, calls=%fused_computation.29 | convolution fusion | flops 6567657472 | bytes 17956864 | tf_op jit(solution)/shard_map/transpose(jvp(vmap(ctsh,cshp->cthp)))/dot_general | solution.py:48
  641.9 34.6 %bitcast_add_fusion.2 = f32[2,4,256,16,64]{2,4,3,1,0:T(8,128)} fusion(f32[2,4,256,16,64]{2,4,3,1,0:T(8,128)} %fusion.62, f32[2,4,256,16]{2,3,1,0:T(8,128)S(1)} %get-tuple-element.585, f32[2,4,256,16]{2,3,1,0:T(8,128)S(1)} %copy-done.46, f32[2,4,256,16]{2,3,1,0:T(8,128)S(1)} %copy-done.35, f32[2,4,256,256]{3,2,1,0:T(8,128)} %fusion.129, ...), kind=kOutput, calls=%fused_computation.67 | convolution fusion | flops 6488588288 | bytes 28180480 | tf_op jit(solution)/shard_map/transpose(jvp(vmap(ctsh,cshp->cthp)))/dot_general | solution.py:48
  726.5 21.9 %multiply_reduce_fusion.6 = (f32[1024]{0:T(1024)}, f32[1024]{0:T(1024)}, f32[1024]{0:T(1024)}, f32[1024]{0:T(1024)}, f32[1024]{0:T(1024)}, /*index=5*/f32[2,1024,1024]{1,2,0:T(8,128)S(1)}) fusion(f32[2,1024,1024]{1,2,0:T(8,128)} %copy.323, f32[2,1024]{1,0:T(2,128)S(1)} %copy-done.31, f32[2,1024]{1,0:T(2,128)S(1)} %copy-done.29, f32[2,1024]{1,0:T(2,128)S(1)} %copy-done.27, ...), kind=kLoop, calls=%fused_computation.78 | loop fusion | flops 44035072 | bytes 33599488 | tf_op jit(solution)/shard_map/transpose(jvp())/reduce_sum | solution.py:25
  777.6 24.6 %fusion.45 = f32[2048,2048]{0,1:T(8,128)} fusion(bf16[2048,2048]{1,0:T(8,128)(2,1)} %all-gather.6.cloned.1.call-done, bf16[2048,1024]{1,0:T(8,128)(2,1)} %bitcast.317, bf16[2048,1024]{1,0:T(8,128)(2,1)} %get-tuple-element.569), kind=kOutput, calls=%fused_computation.102 | convolution fusion | flops 17196646400 | bytes 33554432 | tf_op jit(solution)/shard_map/dot_general | solution.py:70
  802.2 25.3 %copy.380 = f32[2048,2,1024]{2,1,0:T(2,128)} copy(f32[2048,2,1024]{0,2,1:T(8,128)} %bitcast.299) | data formatting | bytes 33554432 | tf_op jit(solution)/shard_map/reshape | solution.py:188
  828.2 17.2 convolution_bitcast_fusion
  870.1 19.9 %reduce-window.16 = f32[2,4,16,2,128]{4,2,3,1,0:T(8,128)S(1)} reduce-window(f32[2,4,16,2,128]{4,2,3,1,0:T(8,128)S(1)} %copy_bitcast_fusion.1, f32[]{:T(128)} %constant.117.clone.1), window={size=1x1x1x1x128 pad=0_0x0_0x0_0x0_0x0_127}, to_apply=%region_19.20 | reduce-window | flops 4161536 | bytes 262148 | tf_op jit(solution)/shard_map/reduce-window.2
  912.2 28.6 %add_add_fusion = f32[2048,2048]{1,0:T(8,128)} fusion(f32[2048,2048]{1,0:T(8,128)} %fusion.130, f32[2048,2048]{1,0:T(8,128)} %fusion.104, bf16[2048,2048]{1,0:T(8,128)(2,1)} %bitcast.309, bf16[2048,1024]{1,0:T(8,128)(2,1)} %bitcast.318, bf16[2048,1024]{1,0:T(8,128)(2,1)} %get-tuple-element.569), kind=kOutput, calls=%fused_computation.30 | convolution fusion | flops 17205035008 | bytes 67108864 | tf_op jit(solution)/shard_map/dot_general | solution.py:76
  940.9 16.8 fusion.117
  971.1 73.2 %all-reduce.32.cloned.1.call-done = f32[2048,2,1024]{2,1,0:T(2,128)} async-done(((f32[2048,2,1024]{2,1,0:T(2,128)}), f32[2048,2,1024]{2,1,0:T(2,128)}) %all-reduce.32.cloned.1.call-update) | async-done | bytes 16777232
  1048.0 71.1 %reduce-scatter.17.cloned.1.call-done = f32[256,1024]{0,1:T(8,128)} async-done(((f32[2048,1024]{0,1:T(8,128)}), f32[256,1024]{0,1:T(8,128)}) %reduce-scatter.17.cloned.1.call-update) | async-done | bytes 1048592 | tf_op jit(solution)/shard_map/reduce_scatter | solution.py:206
  1121.7 280.3 %reduce-scatter.11.cloned.1.call-done = f32[2048,512]{1,0:T(8,128)} async-done(((f32[2048,2048]{1,0:T(8,128)}), f32[2048,512]{1,0:T(8,128)}) %reduce-scatter.11.cloned.1.call-update) | async-done | bytes 4194320 | tf_op jit(solution)/shard_map/reduce_scatter | solution.py:194
  1416.8 23.1 %all-reduce.29 = (f32[512]{0:T(512)}, f32[4,1024]{1,0:T(4,128)}, f32[1024]{0:T(1024)}, f32[4,64]{1,0:T(4,128)}, f32[64]{0:T(128)}, /*index=5*/f32[16]{0:T(128)}, f32[16]{0:T(128)}, f32[16]{0:T(128)}, f32[1024]{0:T(1024)}) all-reduce(f32[512]{0:T(512)S(1)} %get-tuple-element.507, ...), channel_id=1, replica_groups=mesh['row'=8,'col'=4] {'row'}, use_global_device_ids=true, to_apply=%region_27.28 | all-reduce | flops 7024 | bytes 56192 | tf_op jit(solution)/shard_map/psum | solution.py:208
  1439.9 245.4 %reduce-scatter.9.cloned.1.call-done = f32[2048,512]{1,0:T(8,128)} async-done(((f32[2048,2048]{1,0:T(8,128)}), f32[2048,512]{1,0:T(8,128)}) %reduce-scatter.9.cloned.1.call-update) | async-done | bytes 4194320 | tf_op jit(solution)/shard_map/reduce_scatter | solution.py:166
  1691.4 31.9 %reduce-scatter.13.cloned.1.call-done = f32[256,16]{0,1:T(8,128)} async-done(((f32[2048,16]{0,1:T(8,128)}), f32[256,16]{0,1:T(8,128)}) %reduce-scatter.13.cloned.1.call-update) | async-done | bytes 16400 | tf_op jit(solution)/shard_map/reduce_scatter | solution.py:204
  1723.3 37.6 %reduce-scatter.15.cloned.1.call-done = f32[256,64]{0,1:T(8,128)} async-done(((f32[2048,64]{0,1:T(8,128)}), f32[256,64]{0,1:T(8,128)}) %reduce-scatter.15.cloned.1.call-update) | async-done | bytes 65552 | tf_op jit(solution)/shard_map/reduce_scatter | solution.py:205
  (387 shorter events, 463.3 us)
Async XLA Ops:
  7.2 168.5 %all-gather.6.cloned.1.call-start = ((), (), s32[]{:S(2)}) async-start(), calls=%async_computation.6 | async-start | bytes 10485760 | tf_op jit(solution)/shard_map/all_gather | solution.py:108
  27.7 155.7 %copy-start.89 = (f32[64]{0:T(128)S(1)}, f32[64]{0:T(128)}, u32[]{:S(2)}) copy-start(f32[64]{0:T(128)} %param.29) | copy-start | bytes 772
  27.7 184.0 %all-gather.10.cloned.1.call-start = ((), (), s32[]{:S(2)}) async-start(), calls=%async_computation.8 | async-start | bytes 1310720 | tf_op jit(solution)/shard_map/all_gather | solution.py:136
  37.8 278.7 %copy-start.26 = (f32[2,1024]{1,0:T(2,128)}, f32[2,1024]{1,0:T(2,128)S(1)}, u32[]{:S(2)}) copy-start(f32[2,1024]{1,0:T(2,128)S(1)} %get-tuple-element.596) | copy-start | bytes 24580
  37.8 278.7 %copy-start.28 = (f32[2,1024]{1,0:T(2,128)}, f32[2,1024]{1,0:T(2,128)S(1)}, u32[]{:S(2)}) copy-start(f32[2,1024]{1,0:T(2,128)S(1)} %get-tuple-element.597) | copy-start | bytes 24580
  37.8 278.7 %copy-start.30 = (f32[2,1024]{1,0:T(2,128)}, f32[2,1024]{1,0:T(2,128)S(1)}, u32[]{:S(2)}) copy-start(f32[2,1024]{1,0:T(2,128)S(1)} %get-tuple-element.598) | copy-start | bytes 24580
  37.9 160.2 %copy-start.81 = (f32[16]{0:T(128)S(1)}, f32[16]{0:T(128)}, u32[]{:S(2)}) copy-start(f32[16]{0:T(128)} %param.30) | copy-start | bytes 196
  185.5 82.1 %all-gather.8.cloned.1.call-start = ((), (), s32[]{:S(2)}) async-start(), calls=%async_computation.7 | async-start | bytes 9437184 | tf_op jit(solution)/shard_map/all_gather | solution.py:110
  186.2 277.6 %all-gather.12.cloned.1.call-start = ((), (), s32[]{:S(2)}) async-start(), calls=%async_computation.9 | async-start | bytes 4718592 | tf_op jit(solution)/shard_map/all_gather | solution.py:113
  186.8 277.1 %all-gather.14.cloned.1.call-start = ((), (), s32[]{:S(2)}) async-start(), calls=%async_computation.11 | async-start | bytes 10485760 | tf_op jit(solution)/shard_map/all_gather | solution.py:168
  187.4 711.7 %reduce-scatter.19.cloned.1.call-start = ((), (), s32[]{:S(2)}) async-start(), calls=%async_computation.16 | async-start | bytes 2621440
  198.1 180.5 %copy-start.23 = (pred[2,4,256,256]{3,2,1,0:T(8,128)(4,1)}, pred[2,4,256,256]{3,2,1,0:T(8,128)(4,1)S(1)}, u32[]{:S(2)}) copy-start(pred[2,4,256,256]{3,2,1,0:T(8,128)(4,1)S(1)} %compare_and_fusion) | copy-start | bytes 1572868
  641.9 402.5 %all-reduce.32.cloned.1.call-start = ((), (), s32[]{:S(2)}) async-start(), calls=%async_computation.17 | async-start | bytes 33554432
  827.6 291.6 %reduce-scatter.17.cloned.1.call-start = ((), (), s32[]{:S(2)}) async-start(), calls=%async_computation.15 | async-start | bytes 9437184 | tf_op jit(solution)/shard_map/reduce_scatter | solution.py:206
  845.5 556.4 %reduce-scatter.11.cloned.1.call-start = ((), (), s32[]{:S(2)}) async-start(), calls=%async_computation.12 | async-start | bytes 20971520 | tf_op jit(solution)/shard_map/reduce_scatter | solution.py:194
  940.8 744.5 %reduce-scatter.9.cloned.1.call-start = ((), (), s32[]{:S(2)}) async-start(), calls=%async_computation.10 | async-start | bytes 20971520 | tf_op jit(solution)/shard_map/reduce_scatter | solution.py:166
  957.8 765.6 %reduce-scatter.13.cloned.1.call-start = ((), (), s32[]{:S(2)}) async-start(), calls=%async_computation.13 | async-start | bytes 147456 | tf_op jit(solution)/shard_map/reduce_scatter | solution.py:204
  965.1 795.9 %reduce-scatter.15.cloned.1.call-start = ((), (), s32[]{:S(2)}) async-start(), calls=%async_computation.14 | async-start | bytes 589824 | tf_op jit(solution)/shard_map/reduce_scatter | solution.py:205
  965.2 436.8 %copy-start.6 = (bf16[2048,512]{1,0:T(8,128)(2,1)S(1)}, bf16[2048,512]{1,0:T(8,128)(2,1)}, u32[]{:S(2)}) copy-start(bf16[2048,512]{1,0:T(8,128)(2,1)} %param.20) | copy-start | bytes 6291460
  965.2 436.8 %copy-start.41 = (f32[2048]{0:T(1024)S(1)}, f32[2048]{0:T(1024)}, u32[]{:S(2)}) copy-start(f32[2048]{0:T(1024)} %copy-done.40) | copy-start | bytes 24580
  965.2 436.8 %copy-start.62 = (f32[512]{0:T(512)S(1)}, f32[512]{0:T(512)}, u32[]{:S(2)}) copy-start(f32[512]{0:T(512)} %param.22) | copy-start | bytes 6148
  971.1 445.7 %copy-start.64 = (f32[1024]{0:T(1024)S(1)}, f32[1024]{0:T(1024)}, u32[]{:S(2)}) copy-start(f32[1024]{0:T(1024)} %get-tuple-element.506) | copy-start | bytes 12292
  971.1 445.7 %copy-start.84 = (f32[1024]{0:T(1024)S(1)}, f32[1024]{0:T(1024)}, u32[]{:S(2)}) copy-start(f32[1024]{0:T(1024)} %get-tuple-element.500) | copy-start | bytes 12292
  971.1 714.2 %copy-start.57 = (f32[2048]{0:T(1024)S(1)}, f32[2048]{0:T(1024)}, u32[]{:S(2)}) copy-start(f32[2048]{0:T(1024)} %get-tuple-element.590) | copy-start | bytes 24580
  (82 other events, 2641.1 us)
Sparse Core Ops, SparseCore 0:
  27.9 147.8 all-gather.5
  185.6 26.1 all-gather.9
  213.7 53.8 all-gather.7
  269.3 36.7 all-gather.11
  307.5 149.6 all-gather.13
  642.0 42.6 reduce-scatter.18
  827.7 216.6 all-reduce.31
  1047.8 71.2 reduce-scatter.16
  1121.6 280.2 reduce-scatter.10
  1404.1 281.1 reduce-scatter.8
  1689.2 34.1 reduce-scatter.12
  1726.8 34.0 reduce-scatter.14
where the time goes:
time: 1780 us; the launch traced here: 1770 us
  waiting for transfers between devices  932 us (52%)
  matrix products  338 us (19%)
  other arithmetic  204 us (11%)
  local copies, waits for them, and re-layouts  189 us (11%)
  blocking collectives  87.6 us (5%)
    reduce_scatter x1, waiting for transfers between devices, per_device(): d_here = lax.psum_scatter(d_normed, 'col', scatter_dimension=1, tiled=True)  280 us
    reduce_scatter x1, waiting for transfers between devices, per_device(): lax.psum_scatter(partial_out, 'col', scatter_dimension=1, tiled=True)  245 us
    all_gather x1, waiting for transfers between devices, per_device(): normed = lax.all_gather(normed_here, 'col', axis=1, tiled=True)  138 us
    dot_general x3, matrix products, span_scan(): jnp.einsum('ctsh,cshp->cthp', weights, x_blocks, precision=highest)  107 us
    unnamed x14, waiting for transfers between devices  75.1 us
    reduce_scatter x1, waiting for transfers between devices, per_device(): lax.psum_scatter(grad_out, 'row', scatter_dimension=0, tiled=True)  71.1 us
    dot_general x4, matrix products, contract_cols(): lax.dot_general(left, right, (((1,), (1,)), ((), ())), preferred_element_...  62.2 us
    dot_general x4, matrix products, contract_rows(): lax.dot_general(left, right, (((0,), (0,)), ((), ())), preferred_element_...  52.9 us
  transfers between devices with their start and end apart: 12, of which 9 were waited for; matrix products, arithmetic and copies ran while one was open for 30% of the time, Pallas kernels for 0%

commit v1 on v0

v1 whole, which is shorter than its diff:
```python
import functools

import jax
import jax.numpy as jnp
from jax import lax
from jax.experimental import pallas as pl
from jax.experimental.pallas import tpu as pltpu
from jax.sharding import Mesh, PartitionSpec as P

HEADDIM = 64
STATE = 128
KW = 4
EPS = 1e-05
SPAN = 256
GROUP = 256
PER = GROUP // HEADDIM
F32 = jnp.float32
BF16 = jnp.bfloat16
VMEM_LIMIT = 60 * 1024 * 1024


def dot_nn(a, b):
    return lax.dot_general(a, b, (((1,), (0,)), ((), ())), preferred_element_type=F32)


def dot_nt(a, b):
    return lax.dot_general(a, b, (((1,), (1,)), ((), ())), preferred_element_type=F32)


def dot_tn(a, b):
    return lax.dot_general(a, b, (((0,), (0,)), ((), ())), preferred_element_type=F32)


def dot_exact(a, b):
    return lax.dot_general(
        a, b, (((1,), (0,)), ((), ())), preferred_element_type=F32, precision=lax.Precision.HIGHEST
    )


def twice(v):
    return jnp.concatenate([v, v], axis=1)


def spread(cols):
    rows = cols.shape[0]
    lane = lax.broadcasted_iota(jnp.int32, (rows, 128), 1)
    low = lane < HEADDIM
    first = jnp.where(low, cols[:, 0:1], cols[:, 1:2])
    second = jnp.where(low, cols[:, 2:3], cols[:, 3:4])
    return jnp.concatenate([first, second], axis=1)


def head_mask(h):
    lane = lax.broadcasted_iota(jnp.int32, (1, GROUP), 1)
    return ((lane >= h * HEADDIM) & (lane < (h + 1) * HEADDIM)).astype(F32).astype(BF16)


def prep_kernel(
    small_ref, segc_ref, segr_ref, bcp_ref, hp_ref,
    bc_ref, bct_ref, g_ref, gt_ref, colp_ref, cumt_ref, kexp_ref, lag_ref,
):
    length = small_ref.shape[0]
    blocks = length // SPAN
    groups = colp_ref.shape[0]
    seg = segc_ref[...]
    pos = lax.broadcasted_iota(jnp.int32, (length, 128), 0)
    lag = jnp.zeros((length, 128), F32)
    for j in range(1, KW):
        lag = lag + ((pltpu.roll(seg, j, 0) == seg) & (pos >= j)).astype(F32)
    lag_ref[0:length, :] = lag
    lag_ref[length:, :] = jnp.zeros((8, 128), F32)
    lag2 = twice(lag)
    raw = small_ref[:, 0:256]
    v = bcp_ref[4:5, :] + bcp_ref[3:4, :] * raw
    for j in range(1, KW):
        v = v + bcp_ref[3 - j : 4 - j, :] * jnp.where(lag2 >= j, pltpu.roll(raw, j, 0), 0.0)
    act = v * jax.nn.sigmoid(v)
    bc_ref[...] = act.astype(BF16)
    bct_ref[...] = jnp.transpose(act).astype(BF16)
    z = small_ref[:, 256:384] + hp_ref[0:1, :]
    dt = jnp.maximum(z, 0.0) + jnp.log1p(jnp.exp(-jnp.abs(z)))
    a = -dt * jnp.exp(hp_ref[1:2, :])
    tri_r = lax.broadcasted_iota(jnp.int32, (SPAN, SPAN), 0)
    tri_c = lax.broadcasted_iota(jnp.int32, (SPAN, SPAN), 1)
    lower = (tri_r >= tri_c).astype(F32)
    seg_row = segr_ref[0:1, :]
    for c in range(blocks):
        r0 = c * SPAN
        rows = slice(r0, r0 + SPAN)
        cum = dot_exact(lower, a[rows])
        segb = seg[rows]
        last = seg[r0 + SPAN - 1 : r0 + SPAN]
        tail = (segb == last).astype(F32)
        end = cum[SPAN - 1 : SPAN]
        q = jnp.exp(end - cum) * tail
        if c > 0:
            prev = seg[r0 - 1 : r0]
            p = jnp.exp(cum) * (segb == prev).astype(F32)
            k = jnp.exp(end) * (last == prev).astype(F32)
        else:
            p = jnp.zeros_like(cum)
            k = jnp.zeros_like(end)
        kexp_ref[c : c + 1, :] = k
        cumt = jnp.transpose(cum)
        dtb = dt[rows]
        for g in range(groups):
            hs = slice(PER * g, PER * g + PER)
            colp_ref[g, rows, 0:4] = cum[:, hs]
            colp_ref[g, rows, 4:8] = dtb[:, hs]
            colp_ref[g, rows, 8:12] = p[:, hs]
            colp_ref[g, rows, 12:16] = q[:, hs]
            cumt_ref[g, 0:4, rows] = cumt[hs, :]
        bb = bc_ref[rows, 0:STATE]
        cc = bc_ref[rows, STATE : 2 * STATE]
        same = twice(segb) == seg_row[:, rows]
        g_ref[rows, :] = jnp.where(same & (tri_r >= tri_c), dot_nt(cc, bb), 0.0)
        gt_ref[rows, :] = jnp.where(same & (tri_r <= tri_c), dot_nt(bb, cc), 0.0)
    kexp_ref[blocks:, :] = jnp.zeros((kexp_ref.shape[0] - blocks, 128), F32)


def conv_rows(xr_ref, lag_ref, chan_ref, r0):
    cur = xr_ref[pl.ds(r0, SPAN), :]
    before = xr_ref[pl.ds(pl.multiple_of(jnp.maximum(r0 - 8, 0), 8), 8), :]
    both = jnp.concatenate([before, cur], axis=0)
    lag = twice(lag_ref[pl.ds(r0, SPAN), :])
    v = chan_ref[4:5, :] + chan_ref[3:4, :] * cur
    for j in range(1, KW):
        earlier = pltpu.roll(both, j, 0)[8:]
        v = v + chan_ref[3 - j : 4 - j, :] * jnp.where(lag >= j, earlier, 0.0)
    return cur, v


def scan_kernel(
    gate_ref, xr_ref, chan_ref, lag_ref, bc_ref, bct_ref, g_ref, colp_ref, cumt_ref, kexp_ref,
    y_ref, gated_ref, sq_ref, st_ref, state,
):
    length = gate_ref.shape[0]
    blocks = length // SPAN
    state[...] = jnp.zeros_like(state)

    @pl.when(pl.program_id(0) == 0)
    def _():
        sq_ref[...] = jnp.zeros_like(sq_ref)

    def body(c, carry):
        r0 = pl.multiple_of(c * SPAN, SPAN)
        rows = pl.ds(r0, SPAN)
        _, v = conv_rows(xr_ref, lag_ref, chan_ref, r0)
        xc = (v * jax.nn.sigmoid(v)).astype(BF16).astype(F32)
        cp = colp_ref[0, rows, :]
        xd = (spread(cp[:, 4:8]) * xc).astype(BF16)
        px = spread(cp[:, 8:12])
        qx = spread(cp[:, 12:16])
        gb = g_ref[rows, :]
        lefts, rights = [], []
        for h in range(PER):
            gap = cp[:, h : h + 1] - cumt_ref[0, h : h + 1, rows]
            lefts.append((gb * jnp.exp(jnp.minimum(gap, 0.0))).astype(BF16))
            rights.append(xd * head_mask(h))
        y = dot_nn(jnp.concatenate(lefts, axis=1), jnp.concatenate(rights, axis=0))
        st = state[...]
        stb = st.astype(BF16)
        st_ref[c] = stb
        y = y + px * dot_nn(bc_ref[rows, STATE : 2 * STATE], stb)
        kx = kexp_ref[pl.ds(c, 1), :]
        state[...] = kx * st + dot_nn(bct_ref[0:STATE, rows], (qx * xd.astype(F32)).astype(BF16))
        y = y + chan_ref[5:6, :] * xc
        y_ref[rows, :] = y
        gate = gate_ref[rows, :]
        gated = y * (gate * jax.nn.sigmoid(gate))
        gated_ref[rows, :] = gated.astype(BF16)
        sq = gated * gated
        sq_ref[rows, :] += sq[:, 0:128] + sq[:, 128:256]
        return carry

    lax.fori_loop(0, blocks, body, 0)


def scan_grad_kernel(
    gate_ref, xr_ref, y_ref, dh_ref, chan_ref, lag_ref, ir_ref, cf_ref, bc_ref, bct_ref, gt_ref,
    colp_ref, cumt_ref, kexp_ref, st_ref, segc_ref, segr_ref,
    dgate_ref, dxr_ref, hd_ref, end_ref, chg_ref, dbc_ref, nd_ref,
    dst, head, dgt,
):
    length = gate_ref.shape[0]
    blocks = length // SPAN
    step = pl.program_id(0)
    dst[...] = jnp.zeros_like(dst)
    head[...] = jnp.zeros_like(head)
    end_ref[...] = jnp.zeros_like(end_ref)
    chg_ref[...] = jnp.zeros_like(chg_ref)

    @pl.when(step == 0)
    def _():
        dgt[...] = jnp.zeros_like(dgt)
        dbc_ref[...] = jnp.zeros_like(dbc_ref)
        nd_ref[...] = jnp.zeros_like(nd_ref)

    def total(v):
        return jnp.sum(v, axis=0, keepdims=True)

    def body(back, carry):
        c = blocks - 1 - back
        r0 = pl.multiple_of(c * SPAN, SPAN)
        rows = pl.ds(r0, SPAN)
        cur, v = conv_rows(xr_ref, lag_ref, chan_ref, r0)
        sv = jax.nn.sigmoid(v)
        xc = (v * sv).astype(BF16).astype(F32)
        cp = colp_ref[0, rows, :]
        dtx = spread(cp[:, 4:8])
        px = spread(cp[:, 8:12])
        qx = spread(cp[:, 12:16])
        xd = (dtx * xc).astype(BF16)
        xdf = xd.astype(F32)
        gate = gate_ref[rows, :]
        y = y_ref[rows, :]
        dh = dh_ref[rows, :].astype(F32)
        ir = twice(ir_ref[rows, :])
        cf = twice(cf_ref[rows, :])
        sg = jax.nn.sigmoid(gate)
        sl = gate * sg
        gated = y * sl
        dgd = ir * (dh * chan_ref[6:7, :]) - gated * cf
        dy = dgd * sl
        dgate = dgd * y * (sg * (1.0 + gate * (1.0 - sg)))
        dgate_ref[rows, :] = dgate.astype(BF16)
        dyb = dy.astype(BF16)
        gt = gt_ref[rows, :]
        lefts, rights = [], []
        acc = dgt[rows, :]
        for h in range(PER):
            gap = cumt_ref[0, h : h + 1, rows] - cp[:, h : h + 1]
            et = jnp.exp(jnp.minimum(gap, 0.0))
            lefts.append((gt * et).astype(BF16))
            dym = dyb * head_mask(h)
            rights.append(dym)
            acc = acc + dot_nt(xd, dym) * et
        dgt[rows, :] = acc
        u = dot_nn(jnp.concatenate(lefts, axis=1), jnp.concatenate(rights, axis=0))
        ds = dst[...]
        dsb = ds.astype(BF16)
        bb = bc_ref[rows, 0:STATE]
        cc = bc_ref[rows, STATE : 2 * STATE]
        ui = qx * dot_nn(bb, dsb)
        u = u + ui
        dxc = chan_ref[5:6, :] * dy + dtx * u
        yscan = y - chan_ref[5:6, :] * xc
        terms = jnp.concatenate([dyb.astype(F32) * yscan - xdf * u, xc * u], axis=1)
        hi = terms.astype(BF16)
        lo = (terms - hi.astype(F32)).astype(BF16)
        pick_r = lax.broadcasted_iota(jnp.int32, (2 * GROUP, 128), 0)
        pick_c = lax.broadcasted_iota(jnp.int32, (2 * GROUP, 128), 1)
        pick = (pick_r // HEADDIM == pick_c).astype(F32).astype(BF16)
        sums = dot_nn(hi, pick) + dot_nn(lo, pick)
        hd_ref[0, rows, :] = sums[:, 0:8]
        stb = st_ref[c]
        kx = kexp_ref[pl.ds(c, 1), :]
        end_ref[pl.ds(c, 1), :] = total(xdf * ui) + kx * total(ds * stb.astype(F32))
        pdy = (px * dyb.astype(F32)).astype(BF16)
        dbc_ref[rows, 0:STATE] += dot_nt((qx * xdf).astype(BF16), dsb)
        dbc_ref[rows, STATE : 2 * STATE] += dot_nt(pdy, stb)
        dst[...] = kx * ds + dot_nn(bct_ref[STATE : 2 * STATE, rows], pdy)
        dv = dxc * (sv * (1.0 + v * (1.0 - sv)))
        after = pl.ds(pl.multiple_of(r0 + SPAN, 8), 8)
        wide = jnp.concatenate([dv, head[...]], axis=0)
        lagw = jnp.concatenate([twice(lag_ref[rows, :]), twice(lag_ref[after, :])], axis=0)
        head[...] = dv[0:8]
        dxr = chan_ref[3:4, :] * dv
        chg_ref[3:4, :] += total(cur * dv)
        chg_ref[4:5, :] += total(dv)
        chg_ref[5:6, :] += total(dy * xc)
        chg_ref[6:7, :] += total(dh * gated * ir)
        for j in range(1, KW):
            later = pltpu.roll(jnp.where(lagw >= j, wide, 0.0), SPAN + 8 - j, 0)[0:SPAN]
            dxr = dxr + chan_ref[3 - j : 4 - j, :] * later
            chg_ref[3 - j : 4 - j, :] += total(cur * later)
        dxr_ref[rows, :] = dxr.astype(BF16)
        nd = dgate * gate + dxr * cur
        nd_ref[rows, :] += nd[:, 0:128] + nd[:, 128:256]
        return carry

    lax.fori_loop(0, blocks, body, 0)

    @pl.when(step == pl.num_programs(0) - 1)
    def _():
        tri_r = lax.broadcasted_iota(jnp.int32, (SPAN, SPAN), 0)
        tri_c = lax.broadcasted_iota(jnp.int32, (SPAN, SPAN), 1)
        for c in range(blocks):
            rows = slice(c * SPAN, (c + 1) * SPAN)
            same = twice(segc_ref[rows, :]) == segr_ref[0:1, rows]
            full = jnp.where(same & (tri_r <= tri_c), dgt[rows, :], 0.0)
            dbc_ref[rows, 0:STATE] += dot_nn(full.astype(BF16), bc_ref[rows, STATE : 2 * STATE])
            dbc_ref[rows, STATE : 2 * STATE] += dot_nn(
                jnp.transpose(full).astype(BF16), bc_ref[rows, 0:STATE]
            )


def whole(shape):
    return pl.BlockSpec(shape, lambda g: (0,) * len(shape))


def tile(rows, first=0):
    return pl.BlockSpec((rows, GROUP), lambda g: (0, g + first))


def prep(small, segc, segr, bcp, hp, groups):
    length = small.shape[0]
    return pl.pallas_call(
        prep_kernel,
        out_shape=(
            jax.ShapeDtypeStruct((length, 2 * STATE), BF16),
            jax.ShapeDtypeStruct((2 * STATE, length), BF16),
            jax.ShapeDtypeStruct((length, SPAN), F32),
            jax.ShapeDtypeStruct((length, SPAN), F32),
            jax.ShapeDtypeStruct((groups, length, 16), F32),
            jax.ShapeDtypeStruct((groups, 8, length), F32),
            jax.ShapeDtypeStruct((8, 128), F32),
            jax.ShapeDtypeStruct((length + 8, 128), F32),
        ),
        compiler_params=pltpu.CompilerParams(vmem_limit_bytes=VMEM_LIMIT),
        name="prep",
    )(small, segc, segr, bcp, hp)


def scan(gate, xr, chan, lag, bc, bct, gmat, colp, cumt, kexp, first):
    length, width = gate.shape
    groups = width // GROUP
    blocks = length // SPAN
    return pl.pallas_call(
        scan_kernel,
        grid=(groups,),
        in_specs=[
            tile(length),
            tile(length),
            tile(8),
            whole((length + 8, 128)),
            whole((length, 2 * STATE)),
            whole((2 * STATE, length)),
            whole((length, SPAN)),
            pl.BlockSpec((1, length, 16), lambda g: (g + first, 0, 0)),
            pl.BlockSpec((1, 8, length), lambda g: (g + first, 0, 0)),
            tile(8, first),
        ],
        out_specs=[
            tile(length),
            tile(length),
            whole((length, 128)),
            pl.BlockSpec((blocks, STATE, GROUP), lambda g: (0, 0, g)),
        ],
        out_shape=(
            jax.ShapeDtypeStruct((length, width), F32),
            jax.ShapeDtypeStruct((length, width), BF16),
            jax.ShapeDtypeStruct((length, 128), F32),
            jax.ShapeDtypeStruct((blocks, STATE, width), BF16),
        ),
        scratch_shapes=[pltpu.VMEM((STATE, GROUP), F32)],
        compiler_params=pltpu.CompilerParams(vmem_limit_bytes=VMEM_LIMIT),
        name="scan",
    )(gate, xr, chan, lag, bc, bct, gmat, colp, cumt, kexp)


def scan_grad(
    gate, xr, y, dh, chan, lag, ir, cf, bc, bct, gtmat, colp, cumt, kexp, st, segc, segr, first
):
    length, width = gate.shape
    groups = width // GROUP
    blocks = length // SPAN
    return pl.pallas_call(
        scan_grad_kernel,
        grid=(groups,),
        in_specs=[
            tile(length),
            tile(length),
            tile(length),
            tile(length),
            tile(8),
            whole((length + 8, 128)),
            whole((length, 128)),
            whole((length, 128)),
            whole((length, 2 * STATE)),
            whole((2 * STATE, length)),
            whole((length, SPAN)),
            pl.BlockSpec((1, length, 16), lambda g: (g + first, 0, 0)),
            pl.BlockSpec((1, 8, length), lambda g: (g + first, 0, 0)),
            tile(8, first),
            pl.BlockSpec((blocks, STATE, GROUP), lambda g: (0, 0, g)),
            whole((length, 128)),
            whole((8, length)),
        ],
        out_specs=[
            tile(length),
            tile(length),
            pl.BlockSpec((1, length, 8), lambda g: (g, 0, 0)),
            tile(8),
            tile(8),
            whole((length, 2 * STATE)),
            whole((length, 128)),
        ],
        out_shape=(
            jax.ShapeDtypeStruct((length, width), BF16),
            jax.ShapeDtypeStruct((length, width), BF16),
            jax.ShapeDtypeStruct((groups, length, 8), F32),
            jax.ShapeDtypeStruct((8, width), F32),
            jax.ShapeDtypeStruct((8, width), F32),
            jax.ShapeDtypeStruct((length, 2 * STATE), F32),
            jax.ShapeDtypeStruct((length, 128), F32),
        ),
        scratch_shapes=[
            pltpu.VMEM((STATE, GROUP), F32),
            pltpu.VMEM((8, GROUP), F32),
            pltpu.VMEM((length, SPAN), F32),
        ],
        compiler_params=pltpu.CompilerParams(vmem_limit_bytes=VMEM_LIMIT),
        name="scan_grad",
    )(gate, xr, y, dh, chan, lag, ir, cf, bc, bct, gtmat, colp, cumt, kexp, st, segc, segr)


def shifted_silu(raw, taps, bias, lag):
    v = bias + taps[KW - 1] * raw
    for j in range(1, KW):
        earlier = jnp.pad(raw, ((j, 0), (0, 0)))[: raw.shape[0]]
        v = v + taps[KW - 1 - j] * jnp.where(lag[:, None] >= j, earlier, 0.0)
    return jax.nn.silu(v)


def build(nrow, nl):
    def swap(v):
        return lax.ppermute(v, "zh", [(0, 1), (1, 0)])

    def pair_sum(v):
        if nl == 2:
            return v + lax.ppermute(v, "zl", [(0, 1), (1, 0)])
        return lax.psum(v, "zl")

    def row_gather(v):
        return lax.all_gather(v, "row", axis=0, tiled=True)

    def row_scatter(v):
        return lax.psum_scatter(v, "row", scatter_dimension=0, tiled=True)

    def per_device(
        tokens, segment_ids, norm_gain, in_zx, in_dt, in_bc, conv_x, conv_x_bias, conv_bc,
        conv_bc_bias, dt_bias, a_log, d_skip, inner_gain, out_proj, cotangent,
    ):
        seq_count, length = segment_ids.shape
        assert seq_count == 2
        feat = tokens.shape[1]
        width = feat * 2 * nl
        cb = inner_gain.shape[0]
        hb = dt_bias.shape[0]
        inner = cb * 2 * nl
        blocks = length // SPAN
        gb = cb // GROUP
        mh = lax.axis_index("zh")
        ml = lax.axis_index("zl")
        first_h = mh == 0

        def mine(v, axis=0):
            return lax.dynamic_index_in_dim(v, mh, axis, keepdims=False)

        def other(v, axis=0):
            return lax.dynamic_index_in_dim(v, 1 - mh, axis, keepdims=False)

        def gather_features(v):
            halves = v.reshape(2, length, feat)
            own = mine(halves)
            got = swap(other(halves))
            both = jnp.where(first_h, jnp.stack([own, got]), jnp.stack([got, own]))
            if nl == 2:
                rest = lax.ppermute(both, "zl", [(0, 1), (1, 0)])
                every = jnp.where(ml == 0, jnp.stack([both, rest], 1), jnp.stack([rest, both], 1))
            else:
                every = jnp.moveaxis(lax.all_gather(both, "zl"), 0, 1)
            full = jnp.transpose(every, (2, 0, 1, 3)).reshape(length, width)
            return own, got, full

        def scatter_features(v):
            parts = v.reshape(length, 2, nl, feat)
            if nl == 2:
                keep = lax.dynamic_index_in_dim(parts, ml, 2, keepdims=False)
                send = lax.dynamic_index_in_dim(parts, 1 - ml, 2, keepdims=False)
                got = lax.ppermute(send, "zl", [(0, 1), (1, 0)])
                both = keep.astype(F32) + got.astype(F32)
            else:
                both = lax.psum_scatter(parts, "zl", scatter_dimension=2, tiled=False).astype(F32)
            return mine(both, 1), other(both, 1)

        def to_rows(own, got):
            back = swap(got)
            return jnp.where(
                first_h, jnp.concatenate([own, back], 0), jnp.concatenate([back, own], 0)
            )

        chan = jnp.concatenate(
            [
                conv_x,
                conv_x_bias[None],
                jnp.repeat(d_skip, HEADDIM)[None],
                inner_gain[None],
                jnp.pad(jnp.concatenate([dt_bias, a_log]), (0, cb - 2 * hb))[None],
            ],
            axis=0,
        )
        chans = (chan, swap(chan))
        bcn = conv_bc.shape[1]
        packed = jnp.concatenate([norm_gain, conv_bc.reshape(-1), conv_bc_bias])
        packs = lax.all_gather(packed, ("zh", "zl"))
        gain = packs[:, :feat].reshape(width)
        bc_taps = jnp.moveaxis(packs[:, feat : feat + KW * bcn].reshape(-1, KW, bcn), 0, 1)
        bc_taps = bc_taps.reshape(KW, 2 * STATE)
        bc_shift = packs[:, feat + KW * bcn :].reshape(2 * STATE)
        thin = lax.all_gather(jnp.concatenate([in_bc, in_dt], axis=1), ("row", "zh", "zl"))
        thin = thin.reshape(nrow, 2, nl, -1, bcn + hb)
        w_bc = jnp.transpose(thin[..., :bcn], (0, 3, 1, 2, 4)).reshape(width, 2 * STATE)
        w_dt = lax.dynamic_index_in_dim(thin[..., bcn:], ml, 2, keepdims=False)
        w_dt = [pick(w_dt, 1).reshape(width, hb) for pick in (mine, other)]
        w_small = jnp.concatenate([w_bc] + w_dt, axis=1)
        w_small = jnp.pad(w_small, ((0, 0), (0, 384 - w_small.shape[1])))

        x_own, x_got, x_full = gather_features(tokens)
        zx_pair = (in_zx, swap(in_zx))
        out_pair = (out_proj, swap(out_proj))
        w_gate = [row_gather(w[:, 0]) for w in zx_pair]
        w_x = [row_gather(w[:, 1]) for w in zx_pair]
        w_out = [row_gather(w) for w in out_pair]
        x32 = x_full.astype(F32)
        inv_root = lax.rsqrt(jnp.mean(x32 * x32, axis=1, keepdims=True) + EPS)
        normed = (x32 * inv_root * gain).astype(BF16)

        seg = mine(segment_ids)
        segc = jnp.broadcast_to(seg[:, None], (length, 128))
        segr = jnp.broadcast_to(seg[None, :], (8, length))
        small = dot_nn(normed, w_small)
        hp = jnp.concatenate([c[7, : 2 * hb].reshape(2, hb) for c in chans], axis=1)
        hp = jnp.pad(hp, ((0, 6), (0, 128 - 2 * hb)))
        bcp = jnp.concatenate([bc_taps, bc_shift[None], jnp.zeros((3, 2 * STATE), F32)], axis=0)
        bc, bct, gmat, gtmat, colp, cumt, kexp, lag = prep(small, segc, segr, bcp, hp, 2 * gb)
        kexp = jnp.repeat(kexp[:, : 2 * hb], HEADDIM, axis=1)

        gates, xrs, ys, gateds, sts = [], [], [], [], []
        gate_sq = 0.0
        for b in range(2):
            gates.append(dot_nn(normed, w_gate[b]))
            xrs.append(dot_nn(normed, w_x[b]))
            y, gated, sq, st = scan(
                gates[b], xrs[b], chans[b], lag, bc, bct, gmat, colp, cumt, kexp, b * gb
            )
            ys.append(y)
            gateds.append(gated)
            sts.append(st)
            gate_sq = gate_sq + jnp.sum(sq, axis=1)
        gate_sq = pair_sum(gate_sq)
        inner_root = lax.rsqrt(gate_sq / inner + EPS)[:, None]
        gains = [c[6] for c in chans]
        hidden = [(g.astype(F32) * inner_root * k).astype(BF16) for g, k in zip(gateds, gains)]
        partial_out = sum(dot_nt(h, w) for h, w in zip(hidden, w_out)).astype(BF16)
        o_own, o_got = scatter_features(partial_out)
        output = to_rows((o_own + x_own).astype(BF16), (o_got + x_got).astype(BF16))

        c_own, c_got, c_full = gather_features(cotangent)
        dh = [dot_nn(c_full, w).astype(BF16) for w in w_out]
        gate_dot = sum(
            jnp.sum(d.astype(F32) * g.astype(F32) * k, axis=1) for d, g, k in zip(dh, gateds, gains)
        )
        gate_dot = pair_sum(gate_dot)[:, None]
        coef = inner_root**3 / inner * gate_dot
        ir = jnp.broadcast_to(inner_root, (length, 128))
        cf = jnp.broadcast_to(coef, (length, 128))
        g_out = [row_scatter(dot_tn(c_full, h).astype(BF16)) for h in hidden]
        dgates, dxrs, hds, ends, chgs, dbc, nd = [], [], [], [], [], 0.0, 0.0
        for b in range(2):
            dgate, dxr, hd, end, chg, dbc_b, nd_b = scan_grad(
                gates[b], xrs[b], ys[b], dh[b], chans[b], lag, ir, cf, bc, bct, gtmat, colp, cumt,
                kexp, sts[b], segc, segr, b * gb,
            )
            dgates.append(dgate)
            dxrs.append(dxr)
            hds.append(jnp.moveaxis(hd, 0, 1))
            ends.append(end)
            chgs.append(chg)
            dbc = dbc + dbc_b
            nd = nd + nd_b

        hd = jnp.concatenate(hds, axis=1)
        d_cum = hd[..., :PER].reshape(blocks, SPAN, 2 * hb)
        d_dt = hd[..., PER:].reshape(length, 2 * hb)
        end = jnp.concatenate(ends, axis=1)[:blocks].reshape(blocks, 1, 2 * hb, HEADDIM).sum(-1)
        upper = jnp.triu(jnp.ones((SPAN, SPAN), F32))
        d_a = jnp.einsum("ts,csh->cth", upper, d_cum, precision=lax.Precision.HIGHEST) + end
        d_a = d_a.reshape(length, 2 * hb)
        z = small[:, 256 : 256 + 2 * hb] + hp[0, : 2 * hb]
        rate = jnp.exp(hp[1, : 2 * hb])
        dt = jax.nn.softplus(z)
        ddt_raw = (d_dt - rate * d_a) * jax.nn.sigmoid(z)
        g_dtb = jnp.sum(ddt_raw, axis=0)
        g_alog = -jnp.sum(d_a * dt, axis=0) * rate
        _, bc_pull = jax.vjp(
            lambda r, t, s: shifted_silu(r, t, s, lag[:length, 0]), small[:, :256], bc_taps, bc_shift
        )
        dbc_raw, g_cb, g_cbb = bc_pull(dbc)
        d_small = jnp.concatenate([dbc_raw, ddt_raw], axis=1).astype(BF16)
        d_small = jnp.pad(d_small, ((0, 0), (0, 384 - d_small.shape[1])))

        dn = dot_nt(d_small, w_small)
        for b in range(2):
            dn = dn + dot_nt(dgates[b], w_gate[b]) + dot_nt(dxrs[b], w_x[b])
        nd = jnp.sum(nd, axis=1) + jnp.sum(d_small.astype(F32) * small, axis=1)
        nd = pair_sum(nd)[:, None]
        d_own, d_got = scatter_features(dn.astype(BF16))
        gain4 = lax.dynamic_index_in_dim(gain.reshape(2, nl, feat), ml, 1, keepdims=False)
        k_own, k_got = mine(gain4), other(gain4)
        tail = inv_root * inv_root / width * nd
        t_own = c_own + inv_root * k_own * d_own - x_own * tail
        t_got = c_got + inv_root * k_got * d_got - x_got * tail
        tokens_grad = to_rows(t_own.astype(BF16), t_got.astype(BF16))
        g_gain = [jnp.sum(d * x * inv_root, axis=0) for d, x in ((d_own, x_own), (d_got, x_got))]

        g_gate = [row_scatter(dot_tn(normed, d).astype(BF16)) for d in dgates]
        g_x = [row_scatter(dot_tn(normed, d).astype(BF16)) for d in dxrs]
        g_small = row_scatter(dot_tn(normed, d_small))
        g_bc = g_small[:, : 2 * STATE].reshape(-1, 2, nl, bcn)
        g_bc = lax.psum_scatter(g_bc, "zl", scatter_dimension=2, tiled=False)
        g_dts = g_small[:, 2 * STATE : 2 * STATE + 2 * hb].reshape(-1, 2, hb)
        thin_own = jnp.concatenate([mine(g_bc, 1), g_dts[:, 0]], axis=1)
        thin_got = jnp.concatenate([other(g_bc, 1), g_dts[:, 1]], axis=1)
        thin = thin_own + swap(thin_got)

        def join(pair):
            return pair[0].astype(F32) + swap(pair[1]).astype(F32)

        g_zx = jnp.stack([join(g_gate), join(g_x)], axis=1)
        g_wout = join(g_out)

        def small_pack(b, pick):
            cbg = jnp.concatenate([g_cb, g_cbb[None]], axis=0).reshape(KW + 1, 2, nl, bcn)
            return (
                g_gain[b],
                chgs[b][0:7],
                g_dtb[b * hb : (b + 1) * hb],
                g_alog[b * hb : (b + 1) * hb],
                pick(cbg, 1),
            )

        own = small_pack(0, mine)
        got = small_pack(1, other)
        got = jax.tree.map(swap, got)
        both = jax.tree.map(jnp.add, own, got)
        both = lax.psum(both, "row")
        cbg = lax.psum_scatter(both[4], "zl", scatter_dimension=1, tiled=False)
        chg = both[1]
        return (
            output,
            tokens_grad,
            both[0],
            g_zx,
            thin[:, bcn:],
            thin[:, :bcn],
            chg[0:KW],
            chg[4],
            cbg[0:KW],
            cbg[KW],
            both[2],
            both[3],
            chg[5].reshape(hb, HEADDIM).sum(1),
            chg[6],
            g_wout,
        )

    return per_device


def solution(mesh):
    nrow, ncol = mesh.shape["row"], mesh.shape["col"]
    nl = ncol // 2
    split = Mesh(mesh.devices.reshape(nrow, 2, nl), ("row", "zh", "zl"))
    col = ("zh", "zl")
    in_specs = (
        P("row", col), P("row", None), P(col), P("row", None, col), P("row", col), P("row", col),
        P(None, col), P(col), P(None, col), P(col), P(col), P(col), P(col), P(col),
        P("row", col), P("row", col),
    )
    out_specs = (
        P("row", col), P("row", col), P(col), P("row", None, col), P("row", col), P("row", col),
        P(None, col), P(col), P(None, col), P(col), P(col), P(col), P(col), P(col), P("row", col),
    )
    return jax.shard_map(
        build(nrow, nl), mesh=split, in_specs=in_specs, out_specs=out_specs, check_vma=False
    )
```

time: 1780 us -> 1020 us (0.57)
  waiting for transfers between devices: 932 us -> 298 us
  matrix products: 338 us -> 186 us
  other arithmetic: 204 us -> 69.5 us
  Pallas kernels: 0 us -> 131 us
  local copies, waits for them, and re-layouts: 189 us -> 105 us
  blocking collectives: 87.6 us -> 167 us
  starting transfers between devices: 0.66 us -> 34.7 us
    reduce_scatter x5 -> x7, waiting for transfers between devices: 666 us -> 44.6 us  [row_scatter(): return lax.psum_scatter(v, 'row', scatter_dimension=0, tiled=True)]
    ppermute x0 -> x23, waiting for transfers between devices: none -> 252 us  [the longest x16 222 us: swap(): return lax.ppermute(v, 'zh', [(0, 1), (1, 0)])]
    all_gather x5 -> x7, waiting for transfers between devices: 191 us -> 0.05 us  [the longest x6 0.05 us: row_gather(): return lax.all_gather(v, 'row', axis=0, tiled=True)]
    dot_general x24 -> x22, matrix products: 338 us -> 186 us  [the longest x7 67.9 us: dot_nt(): lax.dot_general(a, b, (((1,), (1,)), ((), ())), preferred_element_type=F32)]
    unnamed x0 -> x2, blocking collectives: none -> 141 us
    pallas_call x0 -> x5, Pallas kernels: none -> 131 us  [the longest x2 80.6 us: scan_grad(): pl.pallas_call(scan_grad_kernel, grid=(groups,), in_specs=[tile(length),...]
    reshape x14 -> x12, local copies, waits for them, and re-layouts: 113 us -> 21.5 us  [the longest x2 15.7 us: scatter_features(): parts = v.reshape(length, 2, nl, feat)]
    unnamed x14 -> x16, waiting for transfers between devices: 75.1 us -> 1.87 us
  transfers between devices with their start and end apart: 12 -> 38, of which waited for: 9 -> 11; matrix products, arithmetic and copies ran while one was open for 30% -> 32% of each run, Pallas kernels for 0% -> 5%
where the time goes in v1:
time: 1020 us; the launch traced here: 1010 us
  waiting for transfers between devices  298 us (29%)
  matrix products  186 us (18%)
  blocking collectives  167 us (16%)
  Pallas kernels  131 us (13%)
  local copies, waits for them, and re-layouts  105 us (10%)
  other arithmetic  69.5 us (7%)
  starting transfers between devices  34.7 us (3%)
  between operations  16.8 us (2%)
    ppermute x16, waiting for transfers between devices, swap(): return lax.ppermute(v, 'zh', [(0, 1), (1, 0)])  222 us
    unnamed x2, blocking collectives  141 us
    pallas_call x2, Pallas kernels, scan_grad(): pl.pallas_call(scan_grad_kernel, grid=(groups,), in_specs=[tile(length),...  80.6 us
    dot_general x7, matrix products, dot_nt(): lax.dot_general(a, b, (((1,), (1,)), ((), ())), preferred_element_type=F32)  67.9 us
    dot_general x7, matrix products, dot_nn(): lax.dot_general(a, b, (((1,), (0,)), ((), ())), preferred_element_type=F32)  65 us
    dot_general x7, matrix products, dot_tn(): lax.dot_general(a, b, (((0,), (0,)), ((), ())), preferred_element_type=F32)  52.6 us
    reduce_scatter x7, waiting for transfers between devices, row_scatter(): return lax.psum_scatter(v, 'row', scatter_dimension=0, tiled=True)  44.6 us
    pallas_call x2, Pallas kernels, scan(): pl.pallas_call(scan_kernel, grid=(groups,), in_specs=[tile(length), tile(...  40.6 us
  transfers between devices with their start and end apart: 38, of which 11 were waited for; matrix products, arithmetic and copies ran while one was open for 32% of the time, Pallas kernels for 5%

profile of v1, /device:TPU:0, one launch (start us, length us, event | category | flops | bytes accessed | tf_op | source)
XLA Modules:
  0.0 1008.1 jit_solution(3066463158950604997)
XLA Ops:
  16.7 47.3 %collective-permute-done.3 = bf16[256,2,1024]{2,0,1:T(8,128)(2,1)S(1)} collective-permute-done((bf16[256,2,1024]{2,0,1:T(8,128)(2,1)S(1)}, bf16[256,2,1024]{2,0,1:T(8,128)(2,1)S(1)}, u32[]{:S(2)}, u32[]{:S(2)}) %collective-permute-start.3) | collective-permute-done | bytes 1048608 | tf_op jit(solution)/shard_map/ppermute | solution.py:428
  78.8 120.0 %all-reduce.14 = f32[3328]{0:T(1024)S(1)} all-reduce(f32[3328]{0:T(1024)S(1)} %maximum_dynamic-update-slice_fusion), channel_id=2, replica_groups=mesh['row'=8,'zh'=2,'zl'=2] {'zh','zl'}, use_global_device_ids=true, to_apply=%add.14 | all-reduce | flops 3328 | bytes 26624
  224.9 24.9 %collective-permute-done.1 = bf16[2,1024,512]{2,1,0:T(8,128)(2,1)} collective-permute-done((bf16[2,1024,512]{2,1,0:T(8,128)(2,1)}, bf16[2,1024,512]{2,1,0:T(8,128)(2,1)}, u32[]{:S(2)}, u32[]{:S(2)}) %collective-permute-start.1) | collective-permute-done | bytes 2097184 | tf_op jit(solution)/shard_map/ppermute | solution.py:470
  300.7 10.1 %fusion.22.xr_ref = f32[1024,1024]{1,0:T(8,128)} fusion(bf16[1024,2048]{0,1:T(8,128)(2,1)} %copy-done.16, bf16[2048,1,1024]{2,0,1:T(8,128)(2,1)} %all-gather.20.cloned.1.call-done), kind=kOutput, calls=%fused_computation.35 | convolution fusion | flops 4294967296 | bytes 12582912 | tf_op jit(solution)/shard_map/dot_general | solution.py:23
  310.8 10.0 fusion.26.gate_ref
  320.8 20.7 %scan.2 = (f32[1024,1024]{1,0:T(8,128)}, bf16[1024,1024]{1,0:T(8,128)(2,1)}, f32[1024,128]{1,0:T(8,128)}, bf16[4,128,1024]{2,1,0:T(8,128)(2,1)}) custom-call(f32[1024,1024]{1,0:T(8,128)} %fusion.26.gate_ref, f32[1024,1024]{1,0:T(8,128)} %fusion.22.xr_ref, f32[8,1024]{1,0:T(8,128)} %copy-done.25, f32[1032,128]{1,0:T(8,128)} %get-tuple-element.45.lag_ref, ...), custom_call_target="tpu_custom_call" | custom-call | tf_op jit(solution)/shard_map/scan/pallas_call | solution.py:329
  342.8 10.7 %fusion.6 = (f32[1024]{0:T(1024)S(1)}, bf16[1024,1024]{1,0:T(8,128)(2,1)}) fusion(bf16[1024,1024]{1,0:T(8,128)(2,1)} %get-tuple-element.52, f32[1024]{0:T(1024)S(1)} %copy-done.50, bf16[1024,2048]{0,1:T(8,128)(2,1)} %bitcast.222, bf16[2048,1024]{1,0:T(8,128)(2,1)} %all-gather.14.cloned.1.call-done), kind=kOutput, calls=%fused_computation.15 | convolution fusion | flops 4301257728 | bytes 12591104 | tf_op jit(solution)/shard_map/dot_general | solution.py:23
  353.5 10.0 fusion.14.xr_ref
  363.5 10.3 %fusion.18.gate_ref = f32[1024,1024]{1,0:T(8,128)} fusion(bf16[1024,2048]{0,1:T(8,128)(2,1)} %copy-done.16, bf16[2048,1,1024]{2,0,1:T(8,128)(2,1)} %all-gather.24.cloned.1.call-done), kind=kOutput, calls=%fused_computation.31 | convolution fusion | flops 4294967296 | bytes 12582912 | tf_op jit(solution)/shard_map/dot_general | solution.py:23
  373.8 19.8 %scan.3 = (f32[1024,1024]{1,0:T(8,128)}, bf16[1024,1024]{1,0:T(8,128)(2,1)}, f32[1024,128]{1,0:T(8,128)}, bf16[4,128,1024]{2,1,0:T(8,128)(2,1)}) custom-call(f32[1024,1024]{1,0:T(8,128)} %fusion.18.gate_ref, f32[1024,1024]{1,0:T(8,128)} %fusion.14.xr_ref, f32[8,1024]{1,0:T(8,128)} %copy-done.26, f32[1032,128]{1,0:T(8,128)} %get-tuple-element.45.lag_ref, ...), custom_call_target="tpu_custom_call" | custom-call | tf_op jit(solution)/shard_map/scan/pallas_call | solution.py:329
  396.8 10.3 %fusion.10 = (f32[1024]{0:T(1024)S(1)}, bf16[1024,1024]{1,0:T(8,128)(2,1)}) fusion(bf16[1024,1024]{1,0:T(8,128)(2,1)} %get-tuple-element.55, f32[1024]{0:T(1024)S(1)} %bitcast.257, bf16[1024,2048]{0,1:T(8,128)(2,1)} %bitcast.223, bf16[2048,1024]{1,0:T(8,128)(2,1)} %all-gather.16.cloned.1.call-done), kind=kOutput, calls=%fused_computation.19 | convolution fusion | flops 4301257728 | bytes 12591104 | tf_op jit(solution)/shard_map/dot_general | solution.py:23
  412.7 40.0 %scan_grad.2 = (bf16[1024,1024]{1,0:T(8,128)(2,1)}, bf16[1024,1024]{1,0:T(8,128)(2,1)}, f32[4,1024,8]{2,1,0:T(8,128)}, f32[8,1024]{1,0:T(8,128)}, f32[8,1024]{1,...) custom-call(f32[1024,1024]{1,0:T(8,128)} %fusion.26.gate_ref, f32[1024,1024]{1,0:T(8,128)} %fusion.22.xr_ref, ...), custom_call_target="tpu_custom_call" | custom-call | tf_op jit(solution)/shard_map/scan_grad/pallas_call | solution.py:368
  452.8 40.6 %scan_grad.3 = (bf16[1024,1024]{1,0:T(8,128)(2,1)}, bf16[1024,1024]{1,0:T(8,128)(2,1)}, f32[4,1024,8]{2,1,0:T(8,128)}, f32[8,1024]{1,0:T(8,128)}, f32[8,1024]{1,...) custom-call(f32[1024,1024]{1,0:T(8,128)} %fusion.18.gate_ref, f32[1024,1024]{1,0:T(8,128)} %fusion.14.xr_ref, ...), custom_call_target="tpu_custom_call" | custom-call | tf_op jit(solution)/shard_map/scan_grad/pallas_call | solution.py:368
  516.6 44.5 %reduce-scatter.20.cloned.1.call-done = f32[256,384]{1,0:T(8,128)} async-done(((f32[2048,384]{1,0:T(8,128)}), f32[256,384]{1,0:T(8,128)}) %reduce-scatter.20.cloned.1.call-update) | async-done | bytes 393232 | tf_op jit(solution)/shard_map/reduce_scatter | solution.py:439
  602.0 11.3 %fusion.63 = f32[1024,2048]{1,0:T(8,128)} fusion(bf16[2048,1024]{1,0:T(8,128)(2,1)} %all-gather.14.cloned.1.call-done, bf16[1024,1024]{1,0:T(8,128)(2,1)} %get-tuple-element.52, f32[1024]{0:T(1024)S(1)} %copy-done.51, f32[1024]{0:T(1024)S(1)} %get-tuple-element.174), kind=kOutput, calls=%fused_computation.124 | convolution fusion | flops 4299161600 | bytes 14688256 | tf_op jit(solution)/shard_map/dot_general | solution.py:27
  642.9 10.9 %fusion.24 = f32[1024,2048]{1,0:T(8,128)} fusion(bf16[1024,1024]{1,0:T(8,128)(2,1)} %get-tuple-element.67, bf16[2048,1,1024]{2,0,1:T(8,128)(2,1)} %all-gather.18.cloned.1.call-done), kind=kOutput, calls=%fused_computation.37 | convolution fusion | flops 4294967296 | bytes 14680064 | tf_op jit(solution)/shard_map/dot_general | solution.py:27
  667.7 16.3 %add_convert_fusion = bf16[1024,2048]{1,0:T(8,128)(2,1)} fusion(f32[1024,2048]{1,0:T(8,128)} %fusion.16, f32[1024,2048]{1,0:T(8,128)} %fusion.20, f32[1024,2048]{1,0:T(8,128)} %fusion.85, f32[1024,2048]{1,0:T(8,128)} %fusion.24, bf16[1024,1024]{1,0:T(8,128)(2,1)S(1)} %copy-done.21, bf16[2048,1,1024]{2,0,1:T(8,128)(2,1)} %all-gather.26.cloned.1.call-done), kind=kOutput, calls=%fused_computation.6 | convolution fusion | flops 4305453056 | bytes 44040192 | tf_op jit(solution)/shard_map/dot_general | solution.py:27
  691.9 20.5 %constant_dynamic-slice_fusion.4 = (bf16[1024,2,1,512]{3,2,1,0:T(2,128)(2,1)}, bf16[1024,2,1,512]{3,2,1,0:T(2,128)(2,1)S(1)}, bf16[1024,2,1,512]{3,2,1,0:T(2,128)(2,1)S(1)}, bf16[1024,2,1,512]{3,2,1,0:T(2,128)(2,1)}) fusion(bf16[1024,2,2,512]{3,2,1,0:T(2,128)(2,1)} %reshape.307, s32[]{:T(128)S(6)} %select_n.141, s32[]{:T(128)S(6)} %select_n.144, ...), kind=kLoop, calls=%fused_computation.166 | loop fusion | bytes 16777224 | tf_op jit(solution)/shard_map/jit(dynamic_index_in_dim)/dynamic_slice | solution.py:480
  733.6 73.4 %collective-permute-done.21 = f32[16]{0:T(128)S(1)} collective-permute-done((f32[16]{0:T(128)S(1)}, f32[16]{0:T(128)S(1)}, u32[]{:S(2)}, u32[]{:S(2)}) %collective-permute-start.21) | collective-permute-done | bytes 96 | tf_op jit(solution)/shard_map/ppermute | solution.py:428
  826.2 20.6 %all-reduce.16 = f32[5,2,64]{2,1,0:T(2,128)S(1)} all-reduce(f32[5,2,64]{2,1,0:T(2,128)S(1)} %fusion.77), channel_id=14, replica_groups=mesh['row'=8,'zh'=2,'zl'=2] {'zl'}, use_global_device_ids=true, to_apply=%region_24.25.clone | all-reduce | flops 640 | bytes 5120
  850.6 43.1 %collective-permute-done.14 = f32[512]{0:T(512)S(1)} collective-permute-done((f32[512]{0:T(512)S(1)}, f32[512]{0:T(512)S(1)}, u32[]{:S(2)}, u32[]{:S(2)}) %collective-permute-start.14) | collective-permute-done | bytes 2080 | tf_op jit(solution)/shard_map/ppermute | solution.py:428
  893.7 26.0 %all-reduce.17 = (f32[512]{0:T(512)}, f32[7,1024]{1,0:T(8,128)S(1)}, f32[5,1,64]{2,1,0:T(1,128)S(1)}, f32[16]{0:T(128)}, f32[16]{0:T(128)}) all-reduce(f32[512]{0:T(512)S(1)} %add.316, f32[7,1024]{1,0:T(8,128)S(1)} %slice_add_fusion.1, ...), channel_id=1, replica_groups=mesh['row'=8,'zh'=2,'zl'=2] {'row'}, use_global_device_ids=true, to_apply=%region_10.11 | all-reduce | flops 8032 | bytes 64256 | tf_op jit(solution)/shard_map/psum | solution.py:648
  933.9 31.4 %collective-permute-done.17 = f32[256,80]{0,1:T(8,128)S(1)} collective-permute-done((f32[256,80]{0,1:T(8,128)S(1)}, f32[256,80]{0,1:T(8,128)S(1)}, u32[]{:S(2)}, u32[]{:S(2)}) %collective-permute-start.17) | collective-permute-done | bytes 81952 | tf_op jit(solution)/shard_map/ppermute | solution.py:428
  967.9 19.9 %collective-permute-done.16 = bf16[256,1024]{1,0:T(8,128)(2,1)S(1)} collective-permute-done((bf16[256,1024]{1,0:T(8,128)(2,1)}, bf16[256,1024]{1,0:T(8,128)(2,1)S(1)}, u32[]{:S(2)}, u32[]{:S(2)}) %collective-permute-start.16) | collective-permute-done | bytes 524320 | tf_op jit(solution)/shard_map/ppermute | solution.py:428
  (394 shorter events, 298.6 us)
Async XLA Ops:
  7.2 211.7 %all-gather.22.cloned.1.call-start = ((), (), s32[]{:S(2)}) async-start(), calls=%async_computation.18 | async-start | bytes 1351680 | tf_op jit(solution)/shard_map/all_gather | solution.py:512
  8.7 292.0 %all-gather.20.cloned.1.call-start = ((), (), s32[]{:S(2)}) async-start(), calls=%async_computation.17 | async-start | bytes 4718592 | tf_op jit(solution)/shard_map/all_gather | solution.py:436
  11.3 299.5 %all-gather.18.cloned.1.call-start = ((), (), s32[]{:S(2)}) async-start(), calls=%async_computation.16 | async-start | bytes 4718592 | tf_op jit(solution)/shard_map/all_gather | solution.py:436
  12.0 330.8 %all-gather.14.cloned.1.call-start = ((), (), s32[]{:S(2)}) async-start(), calls=%async_computation.7 | async-start | bytes 4718592 | tf_op jit(solution)/shard_map/all_gather | solution.py:436
  12.6 340.9 %all-gather.26.cloned.1.call-start = ((), (), s32[]{:S(2)}) async-start(), calls=%async_computation.20 | async-start | bytes 4718592 | tf_op jit(solution)/shard_map/all_gather | solution.py:436
  65.1 298.4 %all-gather.24.cloned.1.call-start = ((), (), s32[]{:S(2)}) async-start(), calls=%async_computation.19 | async-start | bytes 4718592 | tf_op jit(solution)/shard_map/all_gather | solution.py:436
  65.7 331.1 %all-gather.16.cloned.1.call-start = ((), (), s32[]{:S(2)}) async-start(), calls=%async_computation.8 | async-start | bytes 4718592 | tf_op jit(solution)/shard_map/all_gather | solution.py:436
  68.4 130.8 %collective-permute-start = (bf16[1024,512]{1,0:T(8,128)(2,1)}, bf16[1024,512]{1,0:T(8,128)(2,1)S(1)}, u32[]{:S(2)}, u32[]{:S(2)}) collective-permute-start(bf16[1024,512]{1,0:T(8,128)(2,1)} %get-tuple-element.191), channel_id=1, source_target_pairs={{0,2},{2,0},{1,3},{3,1},{4,6},{6,4},{5,7},{7,5},{8,10},{10,8},{9,1... | collective-permute-start | bytes 3145736 | tf_op jit(solution)/shard_map/ppermute | solution.py:428
  68.4 139.8 %collective-permute-start.5 = (bf16[256,1024]{1,0:T(8,128)(2,1)}, bf16[256,1024]{1,0:T(8,128)(2,1)}, u32[]{:S(2)}, u32[]{:S(2)}) collective-permute-start(bf16[256,1024]{1,0:T(8,128)(2,1)} %param.30), channel_id=1, source_target_pairs={{0,2},{2,0},{1,3},{3,1},{4,6},{6,4},{5,7},{7,5},{8,10},{10,8},{9,1... | collective-permute-start | bytes 1572872 | tf_op jit(solution)/shard_map/ppermute | solution.py:428
  71.7 134.7 %collective-permute-start.2 = (f32[8,1024]{1,0:T(8,128)S(1)}, f32[8,1024]{1,0:T(8,128)S(1)}, u32[]{:S(2)}, u32[]{:S(2)}) collective-permute-start(f32[8,1024]{1,0:T(8,128)S(1)} %concatenate.88.chan_ref), channel_id=1, source_target_pairs={{0,2},{2,0},{1,3},{3,1},{4,6},{6,4},{5,7},{7,5},{8,10},{10,8},{9,1... | collective-permute-start | bytes 98312 | tf_op jit(solution)/shard_map/ppermute | solution.py:428
  74.4 133.9 %collective-permute-start.8 = (bf16[1024,512]{1,0:T(8,128)(2,1)}, bf16[1024,512]{1,0:T(8,128)(2,1)}, u32[]{:S(2)}, u32[]{:S(2)}) collective-permute-start(bf16[1024,512]{1,0:T(8,128)(2,1)} %get-tuple-element.189), channel_id=1, source_target_pairs={{0,2},{2,0},{1,3},{3,1},{4,6},{6,4},{5,7},{7,5},{8,10},{10,8},{9,1... | collective-permute-start | bytes 3145736 | tf_op jit(solution)/shard_map/ppermute | solution.py:428
  208.3 352.8 %reduce-scatter.20.cloned.1.call-start = ((), (), s32[]{:S(2)}) async-start(), calls=%async_computation.13 | async-start | bytes 3538944 | tf_op jit(solution)/shard_map/reduce_scatter | solution.py:439
  516.5 409.8 %all-reduce.20.cloned.1.call-start = ((), (), s32[]{:S(2)}) async-start(), calls=%async_computation.21 | async-start | bytes 524288
  562.9 364.4 %reduce-scatter.14.cloned.1.call-start = ((), (), s32[]{:S(2)}) async-start(), calls=%async_computation.10 | async-start | bytes 4718592 | tf_op jit(solution)/shard_map/reduce_scatter | solution.py:439
  571.3 359.0 %reduce-scatter.18.cloned.1.call-start = ((), (), s32[]{:S(2)}) async-start(), calls=%async_computation.12 | async-start | bytes 4718592 | tf_op jit(solution)/shard_map/reduce_scatter | solution.py:439
  581.6 385.0 %reduce-scatter.24.cloned.1.call-start = ((), (), s32[]{:S(2)}) async-start(), calls=%async_computation.15 | async-start | bytes 4718592 | tf_op jit(solution)/shard_map/reduce_scatter | solution.py:439
  591.9 374.7 %reduce-scatter.12.cloned.1.call-start = ((), (), s32[]{:S(2)}) async-start(), calls=%async_computation.9 | async-start | bytes 4718592 | tf_op jit(solution)/shard_map/reduce_scatter | solution.py:439
  601.4 366.5 %reduce-scatter.16.cloned.1.call-start = ((), (), s32[]{:S(2)}) async-start(), calls=%async_computation.11 | async-start | bytes 4718592 | tf_op jit(solution)/shard_map/reduce_scatter | solution.py:439
  642.8 349.4 %reduce-scatter.22.cloned.1.call-start = ((), (), s32[]{:S(2)}) async-start(), calls=%async_computation.14 | async-start | bytes 4718592 | tf_op jit(solution)/shard_map/reduce_scatter | solution.py:439
  714.4 99.5 %collective-permute-start.11 = (bf16[1024,2,512]{2,0,1:T(8,128)(2,1)}, bf16[1024,2,512]{2,0,1:T(8,128)(2,1)}, u32[]{:S(2)}, u32[]{:S(2)}) collective-permute-start(bf16[1024,2,512]{2,0,1:T(8,128)(2,1)} %bitcast.213), channel_id=1, source_target_pairs={{0,1},{1,0},{2,3},{3,2},{4,5},{5,4},{6,7},{7,6},{8,9},{9,8},{10,11... | collective-permute-start | bytes 6291464 | tf_op jit(solution)/shard_map/ppermute | solution.py:482
  718.2 99.9 %collective-permute-start.6 = (bf16[1024,2,512]{2,0,1:T(8,128)(2,1)}, bf16[1024,2,512]{2,0,1:T(8,128)(2,1)}, u32[]{:S(2)}, u32[]{:S(2)}) collective-permute-start(bf16[1024,2,512]{2,0,1:T(8,128)(2,1)} %bitcast.214), channel_id=1, source_target_pairs={{0,1},{1,0},{2,3},{3,2},{4,5},{5,4},{6,7},{7,6},{8,9},{9,8},{10,11... | collective-permute-start | bytes 6291464 | tf_op jit(solution)/shard_map/ppermute | solution.py:482
  729.9 96.3 %collective-permute-start.20 = (f32[16]{0:T(128)S(1)}, f32[16]{0:T(128)S(1)}, u32[]{:S(2)}, u32[]{:S(2)}) collective-permute-start(f32[16]{0:T(128)S(1)} %slice.193), channel_id=1, source_target_pairs={{0,2},{2,0},{1,3},{3,1},{4,6},{6,4},{5,7},{7,5},{8,10},{10,8},{9,1... | collective-permute-start | bytes 200 | tf_op jit(solution)/shard_map/ppermute | solution.py:428
  730.2 96.0 %collective-permute-start.19 = (f32[5,2,64]{2,1,0:T(2,128)S(1)}, f32[5,2,64]{2,1,0:T(2,128)S(1)}, u32[]{:S(2)}, u32[]{:S(2)}) collective-permute-start(f32[5,2,64]{2,1,0:T(2,128)S(1)} %fusion.78), channel_id=1, source_target_pairs={{0,2},{2,0},{1,3},{3,1},{4,6},{6,4},{5,7},{7,5},{8,10},{10,8},{9,1... | collective-permute-start | bytes 7688 | tf_op jit(solution)/shard_map/ppermute | solution.py:428
  825.6 97.1 %collective-permute-start.13 = (bf16[1024,512]{1,0:T(8,128)(2,1)}, bf16[1024,512]{1,0:T(8,128)(2,1)}, u32[]{:S(2)}, u32[]{:S(2)}) collective-permute-start(bf16[1024,512]{1,0:T(8,128)(2,1)} %get-tuple-element.184), channel_id=1, source_target_pairs={{0,2},{2,0},{1,3},{3,1},{4,6},{6,4},{5,7},{7,5},{8,10},{10,8},{9,1... | collective-permute-start | bytes 3145736 | tf_op jit(solution)/shard_map/ppermute | solution.py:428
  (93 other events, 2618.5 us)
Sparse Core Ops, SparseCore 0:
  11.5 129.6 all-gather.21
  143.0 39.3 all-gather.19
  184.3 36.7 all-gather.17
  222.8 36.7 all-gather.13
  261.3 36.7 all-gather.25
  299.8 36.7 all-gather.23
  338.4 36.7 all-gather.15
  516.6 44.3 reduce-scatter.19
  563.5 23.7 all-reduce.19
  590.5 51.3 reduce-scatter.13
  645.6 51.2 reduce-scatter.17
  700.2 51.3 reduce-scatter.23
  755.3 51.2 reduce-scatter.11
  809.8 51.3 reduce-scatter.15
  864.7 51.8 reduce-scatter.21

commit v2 on v1

--- a/solution.py
+++ b/solution.py
@@ -415,6 +415,36 @@
     )(gate, xr, y, dh, chan, lag, ir, cf, bc, bct, gtmat, colp, cumt, kexp, st, segc, segr)
 
 
+def back_kernel(a0, a1, a2, a3, a4, w0, w1, w2, w3, w4, nb_ref, dn_ref, gg_ref):
+    total = dot_nt(a0[...], w0[...])
+    for a, w in ((a1, w1), (a2, w2), (a3, w3), (a4, w4)):
+        total = total + dot_nt(a[...], w[...])
+    dn_ref[...] = total.astype(BF16)
+    gg = jnp.sum(total * nb_ref[...].astype(F32), axis=0, keepdims=True)
+    gg_ref[...] = jnp.broadcast_to(gg, gg_ref.shape)
+
+
+def back(lefts, weights, nb):
+    length, width = nb.shape
+    return pl.pallas_call(
+        back_kernel,
+        grid=(width // 256,),
+        in_specs=[whole(a.shape) for a in lefts]
+        + [pl.BlockSpec((256, w.shape[1]), lambda n: (n, 0)) for w in weights]
+        + [pl.BlockSpec((length, 256), lambda n: (0, n))],
+        out_specs=[
+            pl.BlockSpec((length, 256), lambda n: (0, n)),
+            pl.BlockSpec((8, 256), lambda n: (0, n)),
+        ],
+        out_shape=(
+            jax.ShapeDtypeStruct((length, width), BF16),
+            jax.ShapeDtypeStruct((8, width), F32),
+        ),
+        compiler_params=pltpu.CompilerParams(vmem_limit_bytes=VMEM_LIMIT),
+        name="back",
+    )(*lefts, *weights, nb)
+
+
 def shifted_silu(raw, taps, bias, lag):
     v = bias + taps[KW - 1] * raw
     for j in range(1, KW):
@@ -423,14 +453,429 @@
     return jax.nn.silu(v)
 
 
+MESH_ID = pl.DeviceIdType.MESH
+
+
+class Copies:
+    def __init__(self, send, recv):
+        self.send, self.recv, self.count, self.open = send, recv, 0, []
+
+    def start(self, src, dst, to):
+        copy = pltpu.make_async_remote_copy(
+            src_ref=src, dst_ref=dst, send_sem=self.send.at[self.count],
+            recv_sem=self.recv.at[self.count], device_id=to, device_id_type=MESH_ID,
+        )
+        self.count += 1
+        copy.start()
+        self.open.append(copy)
+        return copy
+
+    def finish(self):
+        for copy in self.open:
+            copy.wait_send()
+
+
+def places():
+    h, l, r = lax.axis_index("zh"), lax.axis_index("zl"), lax.axis_index("row")
+    c, x, y = lax.rem(r, 2), lax.rem(r // 2, 2), r // 4
+    rx, ry = r + 2 - 4 * x, r + 4 - 8 * y
+    rc = r + 1 - 2 * c
+    return h, l, r, c, x, y, rx, ry, rc
+
+
+def meet(peers):
+    barrier = pltpu.get_barrier_semaphore()
+    for to in peers:
+        pl.semaphore_signal(barrier, inc=1, device_id=to, device_id_type=MESH_ID)
+    pl.semaphore_wait(barrier, len(peers))
+
+
+GATHER_COPIES = 64
+PIECES = 4
+
+
+def gather_kernel(
+    x_ref, wg_ref, wx_ref, thin_ref, par_ref,
+    nb_ref, nt_ref, ir_ref, par_out, wg0_ref, wx0_ref, wg1_ref, wx1_ref, thin_out,
+    xv, parv, send, recv, local,
+):
+    h, l, r, c, x, y, rx, ry, rc = places()
+    rd = rx + ry - r
+    me, zhp = h * 2 + l, (1 - h) * 2 + l
+    zh, zl, zd = {"zh": 1 - h}, {"zl": 1 - l}, {"zh": 1 - h, "zl": 1 - l}
+    to_x, to_y, to_c = {"row": rx}, {"row": ry}, {"row": rc}
+    length, feat = x_ref.shape[1], x_ref.shape[2]
+    step = length // PIECES
+    shard = wg_ref.shape[0]
+    meet((zh, zl, zd, to_x, to_y, to_c))
+    copies = Copies(send, recv)
+    start = copies.start
+
+    def cols(block):
+        return pl.ds(pl.multiple_of(block * feat, feat), feat)
+
+    def toks(p):
+        return pl.ds(p * step, step)
+
+    def rows(row):
+        return pl.ds(pl.multiple_of(row * shard, shard), shard)
+
+    src = (wg_ref, wx_ref)
+    first = (wg0_ref, wx0_ref)
+    second = (wg1_ref, wx1_ref)
+    keeps = [
+        pltpu.make_async_copy(par_ref, parv.at[me], local.at[0]),
+        pltpu.make_async_copy(thin_ref, thin_out.at[r, me], local.at[1]),
+        pltpu.make_async_copy(x_ref.at[h], xv.at[:, cols(me)], local.at[2]),
+        pltpu.make_async_copy(wg_ref, wg0_ref.at[rows(r)], local.at[3]),
+        pltpu.make_async_copy(wx_ref, wx0_ref.at[rows(r)], local.at[4]),
+    ]
+    for keep in keeps:
+        keep.start()
+    pars = [start(par_ref, parv.at[me], to) for to in (zh, zl, zd)]
+    thins = [start(thin_ref, thin_out.at[r, me], to) for to in (zh, zl, zd)]
+    x1, x2, x3, wz = [], [], [], []
+    for p in range(PIECES):
+        x1.append(start(x_ref.at[1 - h, toks(p)], xv.at[toks(p), cols(me)], zh))
+        if p % 2 == 1:
+            k = p // 2
+            wz.append(start(src[k], second[k].at[rows(r)], zh))
+    own_x = [start(src[k], first[k].at[rows(r)], to_x) for k in range(2)]
+    own_y = [start(src[k], first[k].at[rows(r)], to_y) for k in range(2)]
+    sib = [start(src[k], first[k].at[rows(r)], to_c) for k in range(2)]
+    for p in range(PIECES):
+        x2.append(start(x_ref.at[h, toks(p)], xv.at[toks(p), cols(me)], zl))
+    keeps[1].wait()
+    for copy in thins:
+        copy.wait_recv()
+    thin_x = start(thin_out.at[r], thin_out.at[r], to_x)
+    thin_y = start(thin_out.at[r], thin_out.at[r], to_y)
+    sib.append(start(thin_out.at[r], thin_out.at[r], to_c))
+
+    def onward(p):
+        x1[p].wait_recv()
+        x3.append(start(xv.at[toks(p), cols(zhp)], xv.at[toks(p), cols(zhp)], zl))
+
+    diag = []
+
+    def around(from_x, from_y, dst):
+        for k in range(2):
+            from_x[k].wait_recv()
+            if k == 0:
+                diag.append((start(dst[k].at[rows(rx)], dst[k].at[rows(rx)], to_y), dst[k]))
+            sib.append(start(dst[k].at[rows(rx)], dst[k].at[rows(rx)], to_c))
+            from_y[k].wait_recv()
+            if k == 1:
+                diag.append((start(dst[k].at[rows(ry)], dst[k].at[rows(ry)], to_x), dst[k]))
+            sib.append(start(dst[k].at[rows(ry)], dst[k].at[rows(ry)], to_c))
+
+    onward(0)
+    thin_x.wait_recv()
+    thin_d = start(thin_out.at[rx], thin_out.at[rx], to_y)
+    sib.append(start(thin_out.at[rx], thin_out.at[rx], to_c))
+    thin_y.wait_recv()
+    sib.append(start(thin_out.at[ry], thin_out.at[ry], to_c))
+    onward(1)
+    around(own_x, own_y, first)
+    got_x, got_y = [], []
+    for k in range(2):
+        wz[k].wait_recv()
+        part = second[k].at[rows(r)]
+        got_x.append(start(part, part, to_x))
+        got_y.append(start(part, part, to_y))
+        sib.append(start(part, part, to_c))
+        onward(2 + k)
+    thin_d.wait_recv()
+    sib.append(start(thin_out.at[rd], thin_out.at[rd], to_c))
+    for copy, dst in diag[0:2]:
+        copy.wait_recv()
+        sib.append(start(dst.at[rows(rd)], dst.at[rows(rd)], to_c))
+
+    keeps[0].wait()
+    keeps[2].wait()
+    for copy in pars:
+        copy.wait_recv()
+    par_out[...] = parv[...]
+
+    def norm(p):
+        x2[p].wait_recv()
+        x3[p].wait_recv()
+        total = jnp.zeros((step, 1), F32)
+        for b in range(4):
+            part = xv[toks(p), b * feat : (b + 1) * feat].astype(F32)
+            total = total + jnp.sum(part * part, axis=1, keepdims=True)
+        root = lax.rsqrt(total / (4 * feat) + EPS)
+        ir_ref[toks(p), :] = jnp.broadcast_to(root, (step, 128))
+        for b in range(4):
+            part = xv[toks(p), b * feat : (b + 1) * feat].astype(F32)
+            part = (part * root * parv[b, 8:9, 0:feat]).astype(BF16)
+            nb_ref[toks(p), b * feat : (b + 1) * feat] = part
+            nt_ref[b * feat : (b + 1) * feat, toks(p)] = jnp.transpose(part.astype(F32)).astype(BF16)
+
+    norm(0)
+    norm(1)
+    around(got_x, got_y, second)
+    norm(2)
+    norm(3)
+    for copy, dst in diag[2:4]:
+        copy.wait_recv()
+        sib.append(start(dst.at[rows(rd)], dst.at[rows(rd)], to_c))
+    for copy in sib:
+        copy.wait_recv()
+    keeps[3].wait()
+    keeps[4].wait()
+    copies.finish()
+
+
+def gather_all(x, wg, wx, thin, par):
+    _, length, feat = x.shape
+    shard, cb = wg.shape
+    anywhere = pl.BlockSpec(memory_space=pl.ANY)
+    inside = pl.BlockSpec(memory_space=pltpu.VMEM)
+    weight = jax.ShapeDtypeStruct((8 * shard, cb), BF16)
+    return pl.pallas_call(
+        gather_kernel,
+        in_specs=[anywhere] * 5,
+        out_specs=[inside] * 4 + [anywhere] * 5,
+        out_shape=(
+            jax.ShapeDtypeStruct((length, 4 * feat), BF16),
+            jax.ShapeDtypeStruct((4 * feat, length), BF16),
+            jax.ShapeDtypeStruct((length, 128), F32),
+            jax.ShapeDtypeStruct((4,) + par.shape, F32),
+            weight, weight, weight, weight,
+            jax.ShapeDtypeStruct((8, 4) + thin.shape, BF16),
+        ),
+        scratch_shapes=[
+            pltpu.VMEM((length, 4 * feat), BF16),
+            pltpu.VMEM((4,) + par.shape, F32),
+            pltpu.SemaphoreType.DMA((GATHER_COPIES,)),
+            pltpu.SemaphoreType.DMA((GATHER_COPIES,)),
+            pltpu.SemaphoreType.DMA((8,)),
+        ],
+        compiler_params=pltpu.CompilerParams(
+            collective_id=0, has_side_effects=True, vmem_limit_bytes=VMEM_LIMIT
+        ),
+        name="gather_all",
+    )(x, wg, wx, thin, par)
+
+
+GRAD_COPIES = 96
+
+
+def grad_kernel(
+    nt_ref, dg0_ref, dx0_ref, dg1_ref, dx1_ref, ds_ref, small_ref,
+    gz_ref, thin_out, small_out,
+    cs, cr, ts, tr, fs, fr, kept, ss, sr, total, zs, zr, tfs, tfr, tkept, tss, tsr, tz, tzr,
+    sbuf, srecv, szr, send, recv,
+):
+    h, l, r, c, x, y, rx, ry, rc = places()
+    me = h * 2 + l
+    zh, zl, zd = {"zh": 1 - h}, {"zl": 1 - l}, {"zh": 1 - h, "zl": 1 - l}
+    to_x, to_y, to_c = {"row": rx}, {"row": ry}, {"row": rc}
+    shard = gz_ref.shape[1]
+    ncol = gz_ref.shape[2]
+    meet((zh, zl, zd, to_x, to_y, to_c))
+    copies = Copies(send, recv)
+    start = copies.start
+
+    def product(row, d_ref, at):
+        left = nt_ref[pl.ds(pl.multiple_of(row * shard, shard), shard), :]
+        return dot_nn(left, d_ref[:, at])
+
+    def tiles(d_ref, body):
+        width = d_ref.shape[1]
+        wide = 256 if width % 256 == 0 else 128
+
+        def one(n, carry):
+            body(pl.ds(pl.multiple_of(n * wide, wide), wide))
+            return carry
+
+        lax.fori_loop(0, width // wide, one, 0)
+
+    sbuf[0] = small_ref[...]
+    small_hops = [to_c, to_x, to_y]
+    small_copy = start(sbuf.at[0], srecv.at[0], to_c)
+
+    quarters = [
+        dict(d=dg0_ref, first=to_x, second=to_y, mine=x, along=y, b=0, k=0, swap=False),
+        dict(d=dg1_ref, first=to_y, second=to_x, mine=y, along=x, b=1, k=0, swap=True),
+        dict(d=dx0_ref, first=to_x, second=to_y, mine=x, along=y, b=0, k=1, swap=False),
+        dict(d=dx1_ref, first=to_y, second=to_x, mine=y, along=x, b=1, k=1, swap=True),
+    ]
+
+    def spot(q, first, second):
+        return 2 * first + second if q["swap"] else 2 * second + first
+
+    def refs(i):
+        if i == 4:
+            return ts, tr, tfs, tfr, tkept, tss, tsr
+        return (cs.at[i], cr.at[i], fs.at[i], fr.at[i], kept.at[i], ss.at[i], sr.at[i])
+
+    thin_q = dict(d=ds_ref, first=to_x, second=to_y, mine=x, along=y, swap=False)
+
+    def to_core(i, q):
+        out, back = refs(i)[0:2]
+
+        def each(j, carry):
+            row = 2 * j + 1 - c
+
+            def body(at):
+                out[j, :, at] = product(row, q["d"], at).astype(BF16)
+
+            tiles(q["d"], body)
+            return carry
+
+        lax.fori_loop(0, 4, each, 0)
+        q["core"] = start(out, back, to_c)
+
+    def to_first(i, q):
+        _, back, fsend, frecv, keep, _, _ = refs(i)
+        q["core"].wait_recv()
+
+        def fill(dst, at_first):
+            def each(s, carry):
+                j = spot(q, at_first, s)
+                row = 2 * j + c
+
+                def body(at):
+                    dst[s, :, at] = (product(row, q["d"], at) + back[j, :, at].astype(F32)).astype(BF16)
+
+                tiles(q["d"], body)
+                return carry
+
+            lax.fori_loop(0, 2, each, 0)
+
+        fill(fsend, 1 - q["mine"])
+        q["f"] = start(fsend, frecv, q["first"])
+        fill(keep, q["mine"])
+
+    def to_second(i, q):
+        _, _, _, frecv, keep, ssend, srcv = refs(i)
+        q["f"].wait_recv()
+        far = 1 - q["along"]
+        ssend[...] = (keep[far].astype(F32) + frecv[far].astype(F32)).astype(BF16)
+        q["s"] = start(ssend, srcv, q["second"])
+
+    def settle(i, q):
+        _, _, _, frecv, keep, _, srcv = refs(i)
+        q["s"].wait_recv()
+        near = q["along"]
+        return keep[near].astype(F32) + frecv[near].astype(F32) + srcv[...].astype(F32)
+
+    to_core(4, thin_q)
+    to_core(0, quarters[0])
+    to_core(1, quarters[1])
+    to_first(4, thin_q)
+    to_first(0, quarters[0])
+    small_copy.wait_recv()
+    sbuf[1] = sbuf[0] + srecv[0]
+    small_copy = start(sbuf.at[1], srecv.at[1], to_x)
+    to_core(2, quarters[2])
+    to_first(1, quarters[1])
+    to_core(3, quarters[3])
+    to_first(2, quarters[2])
+    to_second(4, thin_q)
+    small_copy.wait_recv()
+    sbuf[2] = sbuf[1] + srecv[1]
+    small_copy = start(sbuf.at[2], srecv.at[2], to_y)
+    to_first(3, quarters[3])
+    tz[...] = settle(4, thin_q)
+    thin_z = [start(tz, tzr.at[n], to) for n, to in enumerate((zh, zl, zd))]
+    small_copy.wait_recv()
+    sbuf[3] = sbuf[2] + srecv[2]
+    small_z = [start(sbuf.at[3], szr.at[n], to) for n, to in enumerate((zh, zl, zd))]
+    to_second(0, quarters[0])
+    to_second(1, quarters[1])
+    z_copy = [None, None]
+
+    def send_z(i, k):
+        zs[k] = settle(i, quarters[i]).astype(BF16)
+        z_copy[k] = start(zs.at[k], zr.at[k], zh)
+
+    total[0] = settle(0, quarters[0])
+    send_z(1, 0)
+    to_second(2, quarters[2])
+    to_second(3, quarters[3])
+    total[1] = settle(2, quarters[2])
+    send_z(3, 1)
+    for copy in thin_z:
+        copy.wait_recv()
+    for copy in small_z:
+        copy.wait_recv()
+    thin_out[0] = tz[...]
+    small_out[0] = sbuf[3]
+    for n in range(3):
+        thin_out[n + 1] = tzr[n]
+        small_out[n + 1] = szr[n]
+    for k in range(2):
+        z_copy[k].wait_recv()
+        gz_ref[k] = total[k] + zr[k].astype(F32)
+    copies.finish()
+
+
+def grad_all(nt, dg0, dx0, dg1, dx1, d_small, small):
+    width, length = nt.shape
+    shard, cb = width // 8, dg0.shape[1]
+    ns = d_small.shape[1]
+    inside = pl.BlockSpec(memory_space=pltpu.VMEM)
+    V = pltpu.VMEM
+    return pl.pallas_call(
+        grad_kernel,
+        in_specs=[inside] * 7,
+        out_specs=[inside] * 3,
+        out_shape=(
+            jax.ShapeDtypeStruct((2, shard, cb), F32),
+            jax.ShapeDtypeStruct((4, shard, ns), F32),
+            jax.ShapeDtypeStruct((4,) + small.shape, F32),
+        ),
+        scratch_shapes=[
+            V((4, 4, shard, cb), BF16),
+            V((4, 4, shard, cb), BF16),
+            V((4, shard, ns), BF16),
+            V((4, shard, ns), BF16),
+            V((4, 2, shard, cb), BF16),
+            V((4, 2, shard, cb), BF16),
+            V((4, 2, shard, cb), BF16),
+            V((4, shard, cb), BF16),
+            V((4, shard, cb), BF16),
+            V((2, shard, cb), F32),
+            V((2, shard, cb), BF16),
+            V((2, shard, cb), BF16),
+            V((2, shard, ns), BF16),
+            V((2, shard, ns), BF16),
+            V((2, shard, ns), BF16),
+            V((shard, ns), BF16),
+            V((shard, ns), BF16),
+            V((shard, ns), F32),
+            V((3, shard, ns), F32),
+            V((4,) + small.shape, F32),
+            V((3,) + small.shape, F32),
+            V((3,) + small.shape, F32),
+            pltpu.SemaphoreType.DMA((GRAD_COPIES,)),
+            pltpu.SemaphoreType.DMA((GRAD_COPIES,)),
+        ],
+        compiler_params=pltpu.CompilerParams(
+            collective_id=1, has_side_effects=True, vmem_limit_bytes=VMEM_LIMIT
+        ),
+        name="grad_all",
+    )(nt, dg0, dx0, dg1, dx1, d_small, small)
+
+
 def build(nrow, nl):
+    direct = nrow == 8 and nl == 2
+    col = ("zh", "zl")
+
     def swap(v):
         return lax.ppermute(v, "zh", [(0, 1), (1, 0)])
 
+    def swap_zl(v):
+        return lax.ppermute(v, col, [(0, 1), (1, 0), (2, 3), (3, 2)])
+
+    def swap_both(v):
+        return lax.ppermute(v, col, [(0, 3), (3, 0), (1, 2), (2, 1)])
+
     def pair_sum(v):
-        if nl == 2:
-            return v + lax.ppermute(v, "zl", [(0, 1), (1, 0)])
-        return lax.psum(v, "zl")
+        return v + swap_zl(v) if nl == 2 else lax.psum(v, "zl")
 
     def row_gather(v):
         return lax.all_gather(v, "row", axis=0, tiled=True)
@@ -454,6 +899,8 @@
         mh = lax.axis_index("zh")
         ml = lax.axis_index("zl")
         first_h = mh == 0
+        here = mh * nl + ml
+        bcn = conv_bc.shape[1]
 
         def mine(v, axis=0):
             return lax.dynamic_index_in_dim(v, mh, axis, keepdims=False)
@@ -461,35 +908,40 @@
         def other(v, axis=0):
             return lax.dynamic_index_in_dim(v, 1 - mh, axis, keepdims=False)
 
+        def seqs(v):
+            return v.reshape(2, length, feat)
+
+        def by_seq(own, away):
+            return jnp.where(first_h, jnp.stack([own, away]), jnp.stack([away, own]))
+
         def gather_features(v):
-            halves = v.reshape(2, length, feat)
-            own = mine(halves)
-            got = swap(other(halves))
-            both = jnp.where(first_h, jnp.stack([own, got]), jnp.stack([got, own]))
-            if nl == 2:
-                rest = lax.ppermute(both, "zl", [(0, 1), (1, 0)])
-                every = jnp.where(ml == 0, jnp.stack([both, rest], 1), jnp.stack([rest, both], 1))
-            else:
-                every = jnp.moveaxis(lax.all_gather(both, "zl"), 0, 1)
-            full = jnp.transpose(every, (2, 0, 1, 3)).reshape(length, width)
-            return own, got, full
+            own, away = mine(seqs(v)), other(seqs(v))
+            if direct:
+                full = jnp.zeros((length, width), v.dtype)
+                for part, at in (
+                    (own, here),
+                    (swap(away), (1 - mh) * nl + ml),
+                    (swap_zl(own), mh * nl + 1 - ml),
+                    (swap_both(away), (1 - mh) * nl + 1 - ml),
+                ):
+                    full = lax.dynamic_update_slice(full, part, (0, at * feat))
+                return full
+            both = by_seq(own, swap(away))
+            every = jnp.moveaxis(lax.all_gather(both, "zl"), 0, 1)
+            return jnp.transpose(every, (2, 0, 1, 3)).reshape(length, width)
 
         def scatter_features(v):
+            def part(a, b):
+                return lax.dynamic_slice(v, (0, (a * nl + b) * feat), (length, feat))
+
+            if direct:
+                own = part(mh, ml).astype(F32) + swap_zl(part(mh, 1 - ml)).astype(F32)
+                away = swap(part(1 - mh, ml)).astype(F32)
+                away = away + swap_both(part(1 - mh, 1 - ml)).astype(F32)
+                return by_seq(own, away)
             parts = v.reshape(length, 2, nl, feat)
-            if nl == 2:
-                keep = lax.dynamic_index_in_dim(parts, ml, 2, keepdims=False)
-                send = lax.dynamic_index_in_dim(parts, 1 - ml, 2, keepdims=False)
-                got = lax.ppermute(send, "zl", [(0, 1), (1, 0)])
-                both = keep.astype(F32) + got.astype(F32)
-            else:
-                both = lax.psum_scatter(parts, "zl", scatter_dimension=2, tiled=False).astype(F32)
-            return mine(both, 1), other(both, 1)
-
-        def to_rows(own, got):
-            back = swap(got)
-            return jnp.where(
-                first_h, jnp.concatenate([own, back], 0), jnp.concatenate([back, own], 0)
-            )
+            both = lax.psum_scatter(parts, "zl", scatter_dimension=2, tiled=False)
+            return by_seq(mine(both, 1), swap(other(both, 1))).astype(F32)
 
         chan = jnp.concatenate(
             [
@@ -501,31 +953,44 @@
             ],
             axis=0,
         )
-        chans = (chan, swap(chan))
-        bcn = conv_bc.shape[1]
         packed = jnp.concatenate([norm_gain, conv_bc.reshape(-1), conv_bc_bias])
-        packs = lax.all_gather(packed, ("zh", "zl"))
+        thin = jnp.concatenate([in_bc, in_dt], axis=1)
+        if direct:
+            packed = jnp.pad(packed, (0, cb - packed.shape[0]))[None]
+            par = jnp.concatenate([chan, packed, jnp.zeros((7, cb), F32)], axis=0)
+            thin = jnp.pad(thin, ((0, 0), (0, 128 - thin.shape[1])))
+            normed, normed_t, inv_root, par, wg0, wx0, wg1, wx1, thin = gather_all(
+                seqs(tokens), in_zx[:, 0], in_zx[:, 1], thin, par
+            )
+            inv_root = inv_root[:, 0:1]
+            w_gate, w_x = (wg0, wg1), (wx0, wx1)
+            packs = par[:, 8]
+            chans = (chan, lax.dynamic_index_in_dim(par, (1 - mh) * nl + ml, 0, keepdims=False)[0:8])
+            thin = jnp.moveaxis(thin, 1, 0).reshape(2, nl, width, 128)
+            thin = jnp.moveaxis(thin, 2, 0)
+            late_out, late_cot, _ = lax.optimization_barrier((out_proj, cotangent, normed))
+        else:
+            chans = (chan, swap(chan))
+            packs = lax.all_gather(packed, col)
+            thin = lax.all_gather(thin, ("row", "zh", "zl")).reshape(nrow, 2, nl, -1, bcn + hb)
+            thin = jnp.moveaxis(thin, 3, 1).reshape(width, 2, nl, bcn + hb)
+            w_gate = [row_gather(w) for w in (in_zx[:, 0], swap(in_zx[:, 0]))]
+            w_x = [row_gather(w) for w in (in_zx[:, 1], swap(in_zx[:, 1]))]
+            late_out, late_cot = out_proj, cotangent
         gain = packs[:, :feat].reshape(width)
         bc_taps = jnp.moveaxis(packs[:, feat : feat + KW * bcn].reshape(-1, KW, bcn), 0, 1)
         bc_taps = bc_taps.reshape(KW, 2 * STATE)
-        bc_shift = packs[:, feat + KW * bcn :].reshape(2 * STATE)
-        thin = lax.all_gather(jnp.concatenate([in_bc, in_dt], axis=1), ("row", "zh", "zl"))
-        thin = thin.reshape(nrow, 2, nl, -1, bcn + hb)
-        w_bc = jnp.transpose(thin[..., :bcn], (0, 3, 1, 2, 4)).reshape(width, 2 * STATE)
-        w_dt = lax.dynamic_index_in_dim(thin[..., bcn:], ml, 2, keepdims=False)
-        w_dt = [pick(w_dt, 1).reshape(width, hb) for pick in (mine, other)]
-        w_small = jnp.concatenate([w_bc] + w_dt, axis=1)
+        bc_shift = packs[:, feat + KW * bcn : feat + (KW + 1) * bcn].reshape(2 * STATE)
+        w_bc = thin[..., :bcn].reshape(width, 2 * STATE)
+        w_dt = lax.dynamic_index_in_dim(thin[..., bcn : bcn + hb], ml, 2, keepdims=False)
+        w_small = jnp.concatenate([w_bc, mine(w_dt, 1), other(w_dt, 1)], axis=1)
         w_small = jnp.pad(w_small, ((0, 0), (0, 384 - w_small.shape[1])))
-
-        x_own, x_got, x_full = gather_features(tokens)
-        zx_pair = (in_zx, swap(in_zx))
-        out_pair = (out_proj, swap(out_proj))
-        w_gate = [row_gather(w[:, 0]) for w in zx_pair]
-        w_x = [row_gather(w[:, 1]) for w in zx_pair]
-        w_out = [row_gather(w) for w in out_pair]
-        x32 = x_full.astype(F32)
-        inv_root = lax.rsqrt(jnp.mean(x32 * x32, axis=1, keepdims=True) + EPS)
-        normed = (x32 * inv_root * gain).astype(BF16)
+        if not direct:
+            x32 = gather_features(tokens).astype(F32)
+            inv_root = lax.rsqrt(jnp.mean(x32 * x32, axis=1, keepdims=True) + EPS)
+            normed = (x32 * inv_root * gain).astype(BF16)
+        w_out = [row_gather(w) for w in (late_out, swap(late_out))]
+        c_full = gather_features(late_cot)
 
         seg = mine(segment_ids)
         segc = jnp.broadcast_to(seg[:, None], (length, 128))
@@ -554,10 +1019,8 @@
         gains = [c[6] for c in chans]
         hidden = [(g.astype(F32) * inner_root * k).astype(BF16) for g, k in zip(gateds, gains)]
         partial_out = sum(dot_nt(h, w) for h, w in zip(hidden, w_out)).astype(BF16)
-        o_own, o_got = scatter_features(partial_out)
-        output = to_rows((o_own + x_own).astype(BF16), (o_got + x_got).astype(BF16))
-
-        c_own, c_got, c_full = gather_features(cotangent)
+        output = (scatter_features(partial_out) + seqs(tokens)).astype(BF16).reshape(tokens.shape)
+
         dh = [dot_nn(c_full, w).astype(BF16) for w in w_out]
         gate_dot = sum(
             jnp.sum(d.astype(F32) * g.astype(F32) * k, axis=1) for d, g, k in zip(dh, gateds, gains)
@@ -567,6 +1030,7 @@
         ir = jnp.broadcast_to(inner_root, (length, 128))
         cf = jnp.broadcast_to(coef, (length, 128))
         g_out = [row_scatter(dot_tn(c_full, h).astype(BF16)) for h in hidden]
+        g_wout = g_out[0].astype(F32) + swap(g_out[1]).astype(F32)
         dgates, dxrs, hds, ends, chgs, dbc, nd = [], [], [], [], [], 0.0, 0.0
         for b in range(2):
             dgate, dxr, hd, end, chg, dbc_b, nd_b = scan_grad(
@@ -601,66 +1065,76 @@
         d_small = jnp.concatenate([dbc_raw, ddt_raw], axis=1).astype(BF16)
         d_small = jnp.pad(d_small, ((0, 0), (0, 384 - d_small.shape[1])))
 
-        dn = dot_nt(d_small, w_small)
-        for b in range(2):
-            dn = dn + dot_nt(dgates[b], w_gate[b]) + dot_nt(dxrs[b], w_x[b])
+        lefts = (dgates[0], dxrs[0], dgates[1], dxrs[1], d_small)
+        dn, gg = back(lefts, (w_gate[0], w_x[0], w_gate[1], w_x[1], w_small), normed)
         nd = jnp.sum(nd, axis=1) + jnp.sum(d_small.astype(F32) * small, axis=1)
         nd = pair_sum(nd)[:, None]
-        d_own, d_got = scatter_features(dn.astype(BF16))
-        gain4 = lax.dynamic_index_in_dim(gain.reshape(2, nl, feat), ml, 1, keepdims=False)
-        k_own, k_got = mine(gain4), other(gain4)
-        tail = inv_root * inv_root / width * nd
-        t_own = c_own + inv_root * k_own * d_own - x_own * tail
-        t_got = c_got + inv_root * k_got * d_got - x_got * tail
-        tokens_grad = to_rows(t_own.astype(BF16), t_got.astype(BF16))
-        g_gain = [jnp.sum(d * x * inv_root, axis=0) for d, x in ((d_own, x_own), (d_got, x_got))]
-
-        g_gate = [row_scatter(dot_tn(normed, d).astype(BF16)) for d in dgates]
-        g_x = [row_scatter(dot_tn(normed, d).astype(BF16)) for d in dxrs]
-        g_small = row_scatter(dot_tn(normed, d_small))
-        g_bc = g_small[:, : 2 * STATE].reshape(-1, 2, nl, bcn)
-        g_bc = lax.psum_scatter(g_bc, "zl", scatter_dimension=2, tiled=False)
-        g_dts = g_small[:, 2 * STATE : 2 * STATE + 2 * hb].reshape(-1, 2, hb)
-        thin_own = jnp.concatenate([mine(g_bc, 1), g_dts[:, 0]], axis=1)
-        thin_got = jnp.concatenate([other(g_bc, 1), g_dts[:, 1]], axis=1)
-        thin = thin_own + swap(thin_got)
-
-        def join(pair):
-            return pair[0].astype(F32) + swap(pair[1]).astype(F32)
-
-        g_zx = jnp.stack([join(g_gate), join(g_x)], axis=1)
-        g_wout = join(g_out)
-
-        def small_pack(b, pick):
-            cbg = jnp.concatenate([g_cb, g_cbb[None]], axis=0).reshape(KW + 1, 2, nl, bcn)
-            return (
-                g_gain[b],
-                chgs[b][0:7],
-                g_dtb[b * hb : (b + 1) * hb],
-                g_alog[b * hb : (b + 1) * hb],
-                pick(cbg, 1),
+        tail = jnp.concatenate([inv_root, inv_root * inv_root / width * nd], axis=1)
+        tail = by_seq(tail, swap(tail))
+        d_here = scatter_features(dn)
+        x32 = seqs(tokens).astype(F32)
+        tokens_grad = seqs(cotangent) + tail[..., 0:1] * norm_gain * d_here - x32 * tail[..., 1:2]
+        tokens_grad = tokens_grad.astype(BF16).reshape(tokens.shape)
+        g_gain = gg[0] / gain
+        g_bcs = jnp.concatenate([g_cb, g_cbb[None]], axis=0)
+
+        if direct:
+            rows = []
+            for b in range(2):
+                hs = slice(b * hb, (b + 1) * hb)
+                heads = jnp.concatenate([g_dtb[hs], g_alog[hs]])
+                rows += [chgs[b][0:7], jnp.pad(heads, (0, cb - 2 * hb))[None]]
+            last = jnp.concatenate([g_gain, g_bcs.reshape(-1)])
+            last = jnp.pad(last, (0, 8 * cb - last.shape[0])).reshape(8, cb)
+            gz, thins, smalls = grad_all(
+                normed_t, dgates[0], dxrs[0], dgates[1], dxrs[1], d_small,
+                jnp.concatenate(rows + [last], axis=0),
             )
-
-        own = small_pack(0, mine)
-        got = small_pack(1, other)
-        got = jax.tree.map(swap, got)
-        both = jax.tree.map(jnp.add, own, got)
-        both = lax.psum(both, "row")
-        cbg = lax.psum_scatter(both[4], "zl", scatter_dimension=1, tiled=False)
-        chg = both[1]
+            g_zx = jnp.transpose(gz, (1, 0, 2))
+            g_bc = lax.dynamic_slice(thins.sum(0), (0, here * bcn), (thins.shape[1], bcn))
+            g_dt = thins[0, :, 2 * STATE : 2 * STATE + hb]
+            g_dt = g_dt + thins[1, :, 2 * STATE + hb : 2 * STATE + 2 * hb]
+            chg = smalls[0, 0:8] + smalls[1, 8:16]
+            last = smalls[:, 16:].sum(0).reshape(-1)
+            g_gain = lax.dynamic_slice(last, (here * feat,), (feat,))
+            g_bcs = last[width : width + (KW + 1) * 2 * STATE].reshape(KW + 1, 2 * nl, bcn)
+            g_bcs = lax.dynamic_index_in_dim(g_bcs, here, 1, keepdims=False)
+            g_dtb, g_alog = chg[7, :hb], chg[7, hb : 2 * hb]
+        else:
+
+            def join(own, away):
+                return own.astype(F32) + swap(away).astype(F32)
+
+            g_gate = [row_scatter(dot_tn(normed, d).astype(BF16)) for d in dgates]
+            g_x = [row_scatter(dot_tn(normed, d).astype(BF16)) for d in dxrs]
+            g_zx = jnp.stack([join(*g_gate), join(*g_x)], axis=1)
+            thins = row_scatter(dot_tn(normed, d_small))
+            g_bc = lax.psum(thins[:, : 2 * STATE], col).reshape(-1, 2 * nl, bcn)
+            g_bc = lax.dynamic_index_in_dim(g_bc, here, 1, keepdims=False)
+            g_dts = thins[:, 2 * STATE : 2 * STATE + 2 * hb].reshape(-1, 2, hb)
+            g_dt = g_dts[:, 0] + swap(g_dts[:, 1])
+            every = ("row", "zh", "zl")
+            g_gain, g_bcs = lax.psum((g_gain, g_bcs), every)
+            g_gain = lax.dynamic_slice(g_gain, (here * feat,), (feat,))
+            g_bcs = g_bcs.reshape(KW + 1, 2 * nl, bcn)
+            g_bcs = lax.dynamic_index_in_dim(g_bcs, here, 1, keepdims=False)
+            chg = chgs[0] + swap(chgs[1])
+            g_dtb = g_dtb[:hb] + swap(g_dtb[hb:])
+            g_alog = g_alog[:hb] + swap(g_alog[hb:])
+            chg, g_dtb, g_alog = lax.psum((chg, g_dtb, g_alog), "row")
         return (
             output,
             tokens_grad,
-            both[0],
+            g_gain,
             g_zx,
-            thin[:, bcn:],
-            thin[:, :bcn],
+            g_dt,
+            g_bc,
             chg[0:KW],
             chg[4],
-            cbg[0:KW],
-            cbg[KW],
-            both[2],
-            both[3],
+            g_bcs[0:KW],
+            g_bcs[KW],
+            g_dtb,
+            g_alog,
             chg[5].reshape(hb, HEADDIM).sum(1),
             chg[6],
             g_wout,

time: 1020 us -> 915 us (0.90)
  Pallas kernels: 131 us -> 460 us
  blocking collectives: 167 us -> 0 us
  waiting for transfers between devices: 298 us -> 200 us
  matrix products: 186 us -> 93.4 us
  local copies, waits for them, and re-layouts: 105 us -> 63 us
  other arithmetic: 69.5 us -> 40 us
    pallas_call x0 -> x3, Pallas kernels: none -> 328 us  [the longest x1 160 us: grad_all(): pl.pallas_call(grad_kernel, in_specs=[inside] * 7, out_specs=[inside] * 3...]
    unnamed x2 -> x0, blocking collectives: 141 us -> none
    ppermute x16 -> x6, waiting for transfers between devices: 222 us -> 134 us  [swap(): return lax.ppermute(v, 'zh', [(0, 1), (1, 0)])]
    dot_general x7 -> x2, matrix products: 67.9 us -> 20.1 us  [dot_nt(): lax.dot_general(a, b, (((1,), (1,)), ((), ())), preferred_element_type=F32)]
    reduce_scatter x7 -> x2, waiting for transfers between devices: 44.6 us -> 0.01 us  [row_scatter(): return lax.psum_scatter(v, 'row', scatter_dimension=0, tiled=True)]
    ppermute x7 -> x9, waiting for transfers between devices: 30 us -> 66.5 us  [the longest x6 66.5 us: swap_zl(): return lax.ppermute(v, col, [(0, 1), (1, 0), (2, 3), (3, 2)])]
    dot_general x7 -> x2, matrix products: 52.6 us -> 16.2 us  [dot_tn(): lax.dot_general(a, b, (((0,), (0,)), ((), ())), preferred_element_type=F32)]
    psum x1 -> x0, blocking collectives: 26 us -> none  [per_device(): both = lax.psum(both, 'row')]
  transfers between devices with their start and end apart: 38 -> 19, of which waited for: 11 -> 7; matrix products, arithmetic and copies ran while one was open for 32% -> 19% of each run, Pallas kernels for 5% -> 35%
where the time goes in v2:
time: 915 us; the launch traced here: 908 us
  Pallas kernels  460 us (50%)
  waiting for transfers between devices  200 us (22%)
  matrix products  93.4 us (10%)
  local copies, waits for them, and re-layouts  63 us (7%)
  other arithmetic  40 us (4%)
  starting transfers between devices  35.9 us (4%)
  between operations  15.1 us (2%)
    pallas_call x1, Pallas kernels, grad_all(): pl.pallas_call(grad_kernel, in_specs=[inside] * 7, out_specs=[inside] * 3...  160 us
    pallas_call x1, Pallas kernels, gather_all(): pl.pallas_call(gather_kernel, in_specs=[anywhere] * 5, out_specs=[inside]...  141 us
    ppermute x6, waiting for transfers between devices, swap(): return lax.ppermute(v, 'zh', [(0, 1), (1, 0)])  134 us
    pallas_call x2, Pallas kernels, scan_grad(): pl.pallas_call(scan_grad_kernel, grid=(groups,), in_specs=[tile(length),...  82.5 us
    ppermute x6, waiting for transfers between devices, swap_zl(): return lax.ppermute(v, col, [(0, 1), (1, 0), (2, 3), (3, 2)])  66.5 us
    dot_general x7, matrix products, dot_nn(): lax.dot_general(a, b, (((1,), (0,)), ((), ())), preferred_element_type=F32)  56.7 us
    pallas_call x2, Pallas kernels, scan(): pl.pallas_call(scan_kernel, grid=(groups,), in_specs=[tile(length), tile(...  39.7 us
    pallas_call x1, Pallas kernels, back(): pl.pallas_call(back_kernel, grid=(width // 256,), in_specs=[whole(a.shape...  27.3 us
  transfers between devices with their start and end apart: 19, of which 7 were waited for; matrix products, arithmetic and copies ran while one was open for 19% of the time, Pallas kernels for 35%

profile of v2, /device:TPU:0, one launch (start us, length us, event | category | flops | bytes accessed | tf_op | source)
XLA Modules:
  0.0 907.5 jit_solution(14395892220827506964)
XLA Ops:
  16.7 140.6 %gather_all.1 = (bf16[1024,2048]{1,0:T(8,128)(2,1)}, bf16[2048,1024]{1,0:T(8,128)(2,1)}, f32[1024,128]{1,0:T(8,128)}, f32[4,16,1024]{2,1,0:T(8,128)}, bf16[2048,...) custom-call(bf16[2,1024,512]{2,1,0:T(8,128)(2,1)} %bitcast.138, ...), custom_call_target="tpu_custom_call" | custom-call | tf_op jit(solution)/shard_map/gather_all/pallas_call | solution.py:636
  175.5 52.8 %collective-permute-done.1 = bf16[256,1024]{1,0:T(8,128)(2,1)} collective-permute-done((bf16[256,1024]{1,0:T(8,128)(2,1)}, bf16[256,1024]{1,0:T(8,128)(2,1)}, u32[]{:S(2)}, u32[]{:S(2)}) %collective-permute-start.1) | collective-permute-done | bytes 524320 | tf_op jit(solution)/shard_map/ppermute | solution.py:869
  236.4 10.1 %prep.1 = (bf16[1024,256]{1,0:T(8,128)(2,1)}, bf16[256,1024]{1,0:T(8,128)(2,1)}, f32[1024,256]{1,0:T(8,128)}, f32[1024,256]{1,0:T(8,128)}, f32[8,1024,16]{2,1,0:...) custom-call(f32[1024,384]{1,0:T(8,128)} %fusion.67.small_ref, ...), custom_call_target="tpu_custom_call" | custom-call | tf_op jit(solution)/shard_map/prep/pallas_call | solution.py:308
  248.0 10.8 %fusion.68.gate_ref = f32[1024,1024]{1,0:T(8,128)} fusion(bf16[1024,2048]{1,0:T(8,128)(2,1)} %get-tuple-element.61.nb_ref, bf16[2048,1024]{1,0:T(8,128)(2,1)} %get-tuple-element.75.w2), kind=kOutput, calls=%fused_computation.169 | convolution fusion | flops 4294967296 | bytes 12582912 | tf_op jit(solution)/shard_map/dot_general | solution.py:23
  258.8 6.3 fusion.69.xr_ref
  265.0 19.7 %scan.3 = (f32[1024,1024]{1,0:T(8,128)}, bf16[1024,1024]{1,0:T(8,128)(2,1)}, f32[1024,128]{1,0:T(8,128)}, bf16[4,128,1024]{2,1,0:T(8,128)(2,1)}) custom-call(f32[1024,1024]{1,0:T(8,128)} %fusion.68.gate_ref, f32[1024,1024]{1,0:T(8,128)} %fusion.69.xr_ref, f32[8,1024]{1,0:T(8,128)} %copy-done.24, f32[1032,128]{1,0:T(8,128)} %get-tuple-element.66.lag_ref, ...), custom_call_target="tpu_custom_call" | custom-call | tf_op jit(solution)/shard_map/scan/pallas_call | solution.py:329
  286.0 10.0 %fusion.66.xr_ref = f32[1024,1024]{1,0:T(8,128)} fusion(bf16[1024,2048]{1,0:T(8,128)(2,1)} %get-tuple-element.61.nb_ref, bf16[2048,1024]{1,0:T(8,128)(2,1)} %get-tuple-element.63.w1), kind=kOutput, calls=%fused_computation.167 | convolution fusion | flops 4294967296 | bytes 12582912 | tf_op jit(solution)/shard_map/dot_general | solution.py:23
  302.1 20.0 %scan.2 = (f32[1024,1024]{1,0:T(8,128)}, bf16[1024,1024]{1,0:T(8,128)(2,1)}, f32[1024,128]{1,0:T(8,128)}, bf16[4,128,1024]{2,1,0:T(8,128)(2,1)}) custom-call(f32[1024,1024]{1,0:T(8,128)} %fusion.65.gate_ref, f32[1024,1024]{1,0:T(8,128)} %fusion.66.xr_ref, f32[8,1024]{1,0:T(8,128)} %concatenate.57.chan_ref, f32[1032,128]{1,0:T(8,128)} %get-tuple-element.66.lag_ref, ...), custom_call_target="tpu_custom_call" | custom-call | tf_op jit(solution)/shard_map/scan/pallas_call | solution.py:329
  331.3 9.9 %fusion.3 = (f32[1024]{0:T(1024)S(1)}, bf16[1024,1024]{1,0:T(8,128)(2,1)}) fusion(bf16[1024,1024]{1,0:T(8,128)(2,1)} %get-tuple-element.73, f32[1024]{0:T(1024)S(1)} %copy-done.34, bf16[1024,2048]{1,0:T(8,128)(2,1)} %constant_dynamic-update-slice_fusion, bf16[2048,1024]{1,0:T(8,128)(2,1)} %all-gather.3.cloned.1.call-done), kind=kOutput, calls=%fused_computation.10 | convolution fusion | flops 4301257728 | bytes 12591104 | tf_op jit(solution)/shard_map/dot_general | solution.py:23
  341.2 10.1 %fusion.7 = (f32[1024]{0:T(1024)S(1)}, bf16[1024,1024]{1,0:T(8,128)(2,1)}) fusion(bf16[1024,1024]{1,0:T(8,128)(2,1)} %get-tuple-element.79, f32[1024]{0:T(1024)S(1)} %bitcast.181, bf16[1024,2048]{1,0:T(8,128)(2,1)} %constant_dynamic-update-slice_fusion, bf16[2048,1024]{1,0:T(8,128)(2,1)} %all-gather.5.cloned.1.call-done), kind=kOutput, calls=%fused_computation.14 | convolution fusion | flops 4301257728 | bytes 12591104 | tf_op jit(solution)/shard_map/dot_general | solution.py:23
  355.0 6.5 convolution_convert_fusion
  365.0 41.8 %scan_grad.3 = (bf16[1024,1024]{1,0:T(8,128)(2,1)}, bf16[1024,1024]{1,0:T(8,128)(2,1)}, f32[4,1024,8]{2,1,0:T(8,128)}, f32[8,1024]{1,0:T(8,128)}, f32[8,1024]{1,...) custom-call(f32[1024,1024]{1,0:T(8,128)} %fusion.68.gate_ref, f32[1024,1024]{1,0:T(8,128)} %fusion.69.xr_ref, ...), custom_call_target="tpu_custom_call" | custom-call | tf_op jit(solution)/shard_map/scan_grad/pallas_call | solution.py:368
  406.9 40.7 %scan_grad.2 = (bf16[1024,1024]{1,0:T(8,128)(2,1)}, bf16[1024,1024]{1,0:T(8,128)(2,1)}, f32[4,1024,8]{2,1,0:T(8,128)}, f32[8,1024]{1,0:T(8,128)}, f32[8,1024]{1,...) custom-call(f32[1024,1024]{1,0:T(8,128)} %fusion.65.gate_ref, f32[1024,1024]{1,0:T(8,128)} %fusion.66.xr_ref, ...), custom_call_target="tpu_custom_call" | custom-call | tf_op jit(solution)/shard_map/scan_grad/pallas_call | solution.py:368
  462.0 27.3 %back.1 = (bf16[1024,2048]{1,0:T(8,128)(2,1)}, f32[8,2048]{1,0:T(8,128)}) custom-call(bf16[1024,1024]{1,0:T(8,128)(2,1)} %get-tuple-element.95.a0.dg0_ref, bf16[1024,1024]{1,0:T(8,128)(2,1)} %get-tuple-element.96.a1.dx0_ref, bf16[1024,1024]{1,0:T(8,128)(2,1)} %get-tuple-element.97.a2.dg1_ref, bf16[1024,1024]{1,0:T(8,128)(2,1)} %get-tuple-element.98.a3.dx1_ref, ...), custom_call_target="tpu_custom_call" | custom-call | tf_op jit(solution)/shard_map/back/pallas_call | solution.py:429
  490.3 9.7 %convolution_convert_fusion.1 = bf16[2048,1024]{1,0:T(8,128)(2,1)} fusion(bf16[1024,2048]{1,0:T(8,128)(2,1)} %constant_dynamic-update-slice_fusion, bf16[1024,1024]{1,0:T(8,128)(2,1)} %get-tuple-element.73, f32[1024]{0:T(1024)S(1)} %copy-done.34, f32[1024]{0:T(1024)S(1)} %get-tuple-element.179), kind=kOutput, calls=%fused_computation.23 | convolution fusion | flops 4301258752 | bytes 10493952 | tf_op jit(solution)/shard_map/dot_general | solution.py:31
  500.0 11.3 %fusion.33 = f32[1024,2048]{1,0:T(8,128)} fusion(bf16[2048,1024]{1,0:T(8,128)(2,1)} %all-gather.3.cloned.1.call-done, bf16[1024,1024]{1,0:T(8,128)(2,1)} %get-tuple-element.73, f32[1024]{0:T(1024)S(1)} %copy-done.34, f32[1024]{0:T(1024)S(1)} %get-tuple-element.179), kind=kOutput, calls=%fused_computation.70 | convolution fusion | flops 4299161600 | bytes 14688256 | tf_op jit(solution)/shard_map/dot_general | solution.py:27
  511.3 8.8 add_convert_fusion
  522.2 159.9 %grad_all.1 = (f32[2,256,1024]{2,1,0:T(8,128)}, f32[4,256,384]{2,1,0:T(8,128)}, f32[4,24,1024]{2,1,0:T(8,128)}) custom-call(bf16[2048,1024]{1,0:T(8,128)(2,1)} %get-tuple-element.100.nt_ref, bf16[1024,1024]{1,0:T(8,128)(2,1)} %get-tuple-element.95.a0.dg0_ref, bf16[1024,1024]{1,0:T(8,128)(2,1)} %get-tuple-element.96.a1.dx0_ref, ...), custom_call_target="tpu_custom_call" | custom-call | tf_op jit(solution)/shard_map/grad_all/pallas_call | solution.py:822
  701.9 54.5 %collective-permute-done.9 = f32[1024]{0:T(1024)S(1)} collective-permute-done((f32[1024]{0:T(1024)S(1)}, f32[1024]{0:T(1024)S(1)}, u32[]{:S(2)}, u32[]{:S(2)}) %collective-permute-start.9) | collective-permute-done | bytes 4128 | tf_op jit(solution)/shard_map/ppermute | solution.py:872
  768.7 13.6 %collective-permute-done.10 = f32[1024,2]{0,1:T(2,128)S(1)} collective-permute-done((f32[1024,2]{0,1:T(2,128)S(1)}, f32[1024,2]{0,1:T(2,128)S(1)}, u32[]{:S(2)}, u32[]{:S(2)}) %collective-permute-start.10) | collective-permute-done | bytes 8224 | tf_op jit(solution)/shard_map/ppermute | solution.py:869
  790.1 10.4 %collective-permute-done.11 = bf16[1024,512]{1,0:T(8,128)(2,1)S(1)} collective-permute-done((bf16[1024,512]{1,0:T(8,128)(2,1)}, bf16[1024,512]{1,0:T(8,128)(2,1)S(1)}, u32[]{:S(2)}, u32[]{:S(2)}) %collective-permute-start.11) | collective-permute-done | bytes 1048608 | tf_op jit(solution)/shard_map/ppermute | solution.py:872
  802.0 52.4 %collective-permute-done.12 = bf16[1024,512]{1,0:T(8,128)(2,1)S(1)} collective-permute-done((bf16[1024,512]{1,0:T(8,128)(2,1)}, bf16[1024,512]{1,0:T(8,128)(2,1)S(1)}, u32[]{:S(2)}, u32[]{:S(2)}) %collective-permute-start.12) | collective-permute-done | bytes 1048608 | tf_op jit(solution)/shard_map/ppermute | solution.py:869
  857.2 20.3 %collective-permute-start.14 = (bf16[256,1024]{1,0:T(8,128)(2,1)}, bf16[256,1024]{1,0:T(8,128)(2,1)S(1)}, u32[]{:S(2)}, u32[]{:S(2)}) collective-permute-start(bf16[256,1024]{1,0:T(8,128)(2,1)} %reduce-scatter.5.cloned.1.call-done), channel_id=1, source_target_pairs={{0,2},{2,0},{1,3},{3,1},{4,6},{6,4},{5,7},{7,5},{8,10},{10,8},{9,1... | collective-permute-start | bytes 1572872 | tf_op jit(solution)/shard_map/ppermute | solution.py:869
  883.6 14.7 %collective-permute-done.14 = bf16[256,1024]{1,0:T(8,128)(2,1)S(1)} collective-permute-done((bf16[256,1024]{1,0:T(8,128)(2,1)}, bf16[256,1024]{1,0:T(8,128)(2,1)S(1)}, u32[]{:S(2)}, u32[]{:S(2)}) %collective-permute-start.14) | collective-permute-done | bytes 524320 | tf_op jit(solution)/shard_map/ppermute | solution.py:869
  (264 shorter events, 130.4 us)
Async XLA Ops:
  7.2 221.3 %copy-start = (s32[2,1024]{1,0:T(2,128)S(1)}, s32[2,1024]{1,0:T(2,128)}, u32[]{:S(2)}) copy-start(s32[2,1024]{1,0:T(2,128)} %param.17) | copy-start | bytes 24580
  7.3 324.0 %all-gather.3.cloned.1.call-start = ((), (), s32[]{:S(2)}) async-start(), calls=%async_computation.2 | async-start | bytes 4718592 | tf_op jit(solution)/shard_map/all_gather | solution.py:881
  12.4 145.1 %copy-start.6 = (bf16[2048,512]{1,0:T(8,128)(2,1)S(1)}, bf16[2048,512]{1,0:T(8,128)(2,1)}, u32[]{:S(2)}) copy-start(bf16[2048,512]{1,0:T(8,128)(2,1)} %param.31) | copy-start | bytes 6291460
  157.3 183.9 %all-gather.5.cloned.1.call-start = ((), (), s32[]{:S(2)}) async-start(), calls=%async_computation.3 | async-start | bytes 4718592 | tf_op jit(solution)/shard_map/all_gather | solution.py:881
  157.3 70.9 %collective-permute-start.1 = (bf16[256,1024]{1,0:T(8,128)(2,1)}, bf16[256,1024]{1,0:T(8,128)(2,1)}, u32[]{:S(2)}, u32[]{:S(2)}) collective-permute-start(bf16[256,1024]{1,0:T(8,128)(2,1)} %param.30), channel_id=1, source_target_pairs={{0,2},{2,0},{1,3},{3,1},{4,6},{6,4},{5,7},{7,5},{8,10},{10,8},{9,1... | collective-permute-start | bytes 1572872 | tf_op jit(solution)/shard_map/ppermute | solution.py:869
  158.5 165.8 %collective-permute-start.5 = (bf16[1024,512]{1,0:T(8,128)(2,1)}, bf16[1024,512]{1,0:T(8,128)(2,1)}, u32[]{:S(2)}, u32[]{:S(2)}) collective-permute-start(bf16[1024,512]{1,0:T(8,128)(2,1)} %dynamic-slice_bitcast_fusion), channel_id=1, source_target_pairs={{0,2},{2,0},{1,3},{3,1},{4,6},{6,4},{5,7},{7,5},{8,10},{10,8},{9,1... | collective-permute-start | bytes 3145736 | tf_op jit(solution)/shard_map/ppermute | solution.py:869
  161.4 167.6 %collective-permute-start.7 = (bf16[1024,512]{1,0:T(8,128)(2,1)}, bf16[1024,512]{1,0:T(8,128)(2,1)}, u32[]{:S(2)}, u32[]{:S(2)}) collective-permute-start(bf16[1024,512]{1,0:T(8,128)(2,1)} %dynamic-slice_bitcast_fusion), channel_id=1, source_target_pairs={{0,3},{3,0},{1,2},{2,1},{4,7},{7,4},{5,6},{6,5},{8,11},{11,8},{9,1... | collective-permute-start | bytes 3145736 | tf_op jit(solution)/shard_map/ppermute | solution.py:875
  166.9 159.8 %collective-permute-start.6 = (bf16[1024,512]{1,0:T(8,128)(2,1)}, bf16[1024,512]{1,0:T(8,128)(2,1)}, u32[]{:S(2)}, u32[]{:S(2)}) collective-permute-start(bf16[1024,512]{1,0:T(8,128)(2,1)} %get-tuple-element.181), channel_id=1, source_target_pairs={{0,1},{1,0},{2,3},{3,2},{4,5},{5,4},{6,7},{7,6},{8,9},{9,8},{10,11... | collective-permute-start | bytes 3145736 | tf_op jit(solution)/shard_map/ppermute | solution.py:872
  228.3 629.0 %reduce-scatter.5.cloned.1.call-start = ((), (), s32[]{:S(2)}) async-start(), calls=%async_computation.5 | async-start | bytes 4718592 | tf_op jit(solution)/shard_map/reduce_scatter | solution.py:884
  323.4 29.9 %collective-permute-start = (f32[1024]{0:T(1024)S(1)}, f32[1024]{0:T(1024)S(1)}, u32[]{:S(2)}, u32[]{:S(2)}) collective-permute-start(f32[1024]{0:T(1024)S(1)} %add.263), channel_id=1, source_target_pairs={{0,1},{1,0},{2,3},{3,2},{4,5},{5,4},{6,7},{7,6},{8,9},{9,8},{10,11... | collective-permute-start | bytes 12296 | tf_op jit(solution)/shard_map/ppermute | solution.py:872
  351.3 3.6 collective-permute-start.8
  361.5 522.1 %reduce-scatter.3.cloned.1.call-start = ((), (), s32[]{:S(2)}) async-start(), calls=%async_computation.4 | async-start | bytes 4718592 | tf_op jit(solution)/shard_map/reduce_scatter | solution.py:884
  688.7 93.6 %collective-permute-start.2 = (bf16[1024,512]{1,0:T(8,128)(2,1)}, bf16[1024,512]{1,0:T(8,128)(2,1)}, u32[]{:S(2)}, u32[]{:S(2)}) collective-permute-start(bf16[1024,512]{1,0:T(8,128)(2,1)} %get-tuple-element.185), channel_id=1, source_target_pairs={{0,1},{1,0},{2,3},{3,2},{4,5},{5,4},{6,7},{7,6},{8,9},{9,8},{10,11... | collective-permute-start | bytes 3145736 | tf_op jit(solution)/shard_map/ppermute | solution.py:872
  688.7 97.0 %collective-permute-start.3 = (bf16[1024,512]{1,0:T(8,128)(2,1)}, bf16[1024,512]{1,0:T(8,128)(2,1)}, u32[]{:S(2)}, u32[]{:S(2)}) collective-permute-start(bf16[1024,512]{1,0:T(8,128)(2,1)} %get-tuple-element.187), channel_id=1, source_target_pairs={{0,2},{2,0},{1,3},{3,1},{4,6},{6,4},{5,7},{7,5},{8,10},{10,8},{9,1... | collective-permute-start | bytes 3145736 | tf_op jit(solution)/shard_map/ppermute | solution.py:869
  690.1 95.6 %collective-permute-start.4 = (bf16[1024,512]{1,0:T(8,128)(2,1)}, bf16[1024,512]{1,0:T(8,128)(2,1)}, u32[]{:S(2)}, u32[]{:S(2)}) collective-permute-start(bf16[1024,512]{1,0:T(8,128)(2,1)} %get-tuple-element.186), channel_id=1, source_target_pairs={{0,3},{3,0},{1,2},{2,1},{4,7},{7,4},{5,6},{6,5},{8,11},{11,8},{9,1... | collective-permute-start | bytes 3145736 | tf_op jit(solution)/shard_map/ppermute | solution.py:875
  693.6 62.8 %collective-permute-start.9 = (f32[1024]{0:T(1024)S(1)}, f32[1024]{0:T(1024)S(1)}, u32[]{:S(2)}, u32[]{:S(2)}) collective-permute-start(f32[1024]{0:T(1024)S(1)} %add.302), channel_id=1, source_target_pairs={{0,1},{1,0},{2,3},{3,2},{4,5},{5,4},{6,7},{7,6},{8,9},{9,8},{10,11... | collective-permute-start | bytes 12296 | tf_op jit(solution)/shard_map/ppermute | solution.py:872
  693.7 69.3 %copy-start.16 = (f32[2,256,1024]{2,1,0:T(8,128)S(1)}, f32[2,256,1024]{2,1,0:T(8,128)}, u32[]{:S(2)}) copy-start(f32[2,256,1024]{2,1,0:T(8,128)} %get-tuple-element.105) | copy-start | bytes 6291460
  701.3 65.3 %copy-start.20 = (f32[256,16]{1,0:T(8,128)S(1)}, f32[256,16]{1,0:T(8,128)}, u32[]{:S(2)}) copy-start(f32[256,16]{1,0:T(8,128)} %add_bitcast_fusion.4) | copy-start | bytes 49156
  701.3 66.0 %copy-start.26 = (f32[8,1024]{1,0:T(8,128)S(1)}, f32[8,1024]{1,0:T(8,128)}, u32[]{:S(2)}) copy-start(f32[8,1024]{1,0:T(8,128)} %copy-done.25) | copy-start | bytes 98308
  760.0 22.3 %collective-permute-start.10 = (f32[1024,2]{0,1:T(2,128)S(1)}, f32[1024,2]{0,1:T(2,128)S(1)}, u32[]{:S(2)}, u32[]{:S(2)}) collective-permute-start(f32[1024,2]{0,1:T(2,128)S(1)} %get-tuple-element.210), channel_id=1, source_target_pairs={{0,2},{2,0},{1,3},{3,1},{4,6},{6,4},{5,7},{7,5},{8,10},{10,8},{9,1... | collective-permute-start | bytes 24584 | tf_op jit(solution)/shard_map/ppermute | solution.py:869
  768.0 32.5 %collective-permute-start.11 = (bf16[1024,512]{1,0:T(8,128)(2,1)}, bf16[1024,512]{1,0:T(8,128)(2,1)S(1)}, u32[]{:S(2)}, u32[]{:S(2)}) collective-permute-start(bf16[1024,512]{1,0:T(8,128)(2,1)} %get-tuple-element.182), channel_id=1, source_target_pairs={{0,1},{1,0},{2,3},{3,2},{4,5},{5,4},{6,7},{7,6},{8,9},{9,8},{10,11... | collective-permute-start | bytes 3145736 | tf_op jit(solution)/shard_map/ppermute | solution.py:872
  782.3 72.1 %collective-permute-start.12 = (bf16[1024,512]{1,0:T(8,128)(2,1)}, bf16[1024,512]{1,0:T(8,128)(2,1)S(1)}, u32[]{:S(2)}, u32[]{:S(2)}) collective-permute-start(bf16[1024,512]{1,0:T(8,128)(2,1)} %get-tuple-element.184), channel_id=1, source_target_pairs={{0,2},{2,0},{1,3},{3,1},{4,6},{6,4},{5,7},{7,5},{8,10},{10,8},{9,1... | collective-permute-start | bytes 3145736 | tf_op jit(solution)/shard_map/ppermute | solution.py:869
  782.3 72.1 %collective-permute-start.13 = (bf16[1024,512]{1,0:T(8,128)(2,1)S(1)}, bf16[1024,512]{1,0:T(8,128)(2,1)S(1)}, u32[]{:S(2)}, u32[]{:S(2)}) collective-permute-start(bf16[1024,512]{1,0:T(8,128)(2,1)S(1)} %copy-done.19), channel_id=1, source_target_pairs={{0,3},{3,0},{1,2},{2,1},{4,7},{7,4},{5,6},{6,5},{8,11},{11,8},{9,1... | collective-permute-start | bytes 3145736 | tf_op jit(solution)/shard_map/ppermute | solution.py:875
  857.2 41.1 %collective-permute-start.14 = (bf16[256,1024]{1,0:T(8,128)(2,1)}, bf16[256,1024]{1,0:T(8,128)(2,1)S(1)}, u32[]{:S(2)}, u32[]{:S(2)}) collective-permute-start(bf16[256,1024]{1,0:T(8,128)(2,1)} %reduce-scatter.5.cloned.1.call-done), channel_id=1, source_target_pairs={{0,2},{2,0},{1,3},{3,1},{4,6},{6,4},{5,7},{7,5},{8,10},{10,8},{9,1... | collective-permute-start | bytes 1572872 | tf_op jit(solution)/shard_map/ppermute | solution.py:869
  (40 other events, 541.6 us)
Sparse Core Ops, SparseCore 0:
  157.4 35.2 all-gather.2
  228.4 35.6 all-gather.4
  361.6 50.8 reduce-scatter.4
  500.1 54.1 reduce-scatter.2

commit v3 on v2

v3 whole, which is shorter than its diff:
```python
import functools

import jax
import jax.numpy as jnp
from jax import lax
from jax.experimental import pallas as pl
from jax.experimental.pallas import tpu as pltpu
from jax.sharding import Mesh, PartitionSpec as P

HEADDIM = 64
STATE = 128
KW = 4
EPS = 1e-05
SPAN = 256
GROUP = 256
PER = GROUP // HEADDIM
F32 = jnp.float32
BF16 = jnp.bfloat16
VMEM_LIMIT = 60 * 1024 * 1024


def dot_nn(a, b):
    return lax.dot_general(a, b, (((1,), (0,)), ((), ())), preferred_element_type=F32)


def dot_nt(a, b):
    return lax.dot_general(a, b, (((1,), (1,)), ((), ())), preferred_element_type=F32)


def dot_tn(a, b):
    return lax.dot_general(a, b, (((0,), (0,)), ((), ())), preferred_element_type=F32)


def dot_exact(a, b):
    return lax.dot_general(
        a, b, (((1,), (0,)), ((), ())), preferred_element_type=F32, precision=lax.Precision.HIGHEST
    )


def twice(v):
    return jnp.concatenate([v, v], axis=1)


def across(v):
    return v if SPAN == 128 else twice(v)


def turned(v):
    n = v.shape[1]
    row = lax.broadcasted_iota(jnp.int32, (n, n), 0)
    col = lax.broadcasted_iota(jnp.int32, (n, n), 1)
    return dot_nt((row == col).astype(F32).astype(BF16), v).astype(BF16)


def spread(cols):
    rows = cols.shape[0]
    lane = lax.broadcasted_iota(jnp.int32, (rows, 128), 1)
    low = lane < HEADDIM
    first = jnp.where(low, cols[:, 0:1], cols[:, 1:2])
    second = jnp.where(low, cols[:, 2:3], cols[:, 3:4])
    return jnp.concatenate([first, second], axis=1)


def head_mask(h):
    lane = lax.broadcasted_iota(jnp.int32, (1, GROUP), 1)
    return ((lane >= h * HEADDIM) & (lane < (h + 1) * HEADDIM)).astype(F32).astype(BF16)


def prep_kernel(
    small_ref, segc_ref, segr_ref, bcp_ref, hp_ref,
    bc_ref, bct_ref, g_ref, gt_ref, colp_ref, cumt_ref, kexp_ref, lag_ref,
):
    length = small_ref.shape[0]
    blocks = length // SPAN
    groups = colp_ref.shape[0]
    seg = segc_ref[...]
    pos = lax.broadcasted_iota(jnp.int32, (length, 128), 0)
    lag = jnp.zeros((length, 128), F32)
    for j in range(1, KW):
        lag = lag + ((pltpu.roll(seg, j, 0) == seg) & (pos >= j)).astype(F32)
    lag_ref[0:length, :] = lag
    lag_ref[length:, :] = jnp.zeros((8, 128), F32)
    lag2 = twice(lag)
    raw = small_ref[:, 0:256]
    v = bcp_ref[4:5, :] + bcp_ref[3:4, :] * raw
    for j in range(1, KW):
        v = v + bcp_ref[3 - j : 4 - j, :] * jnp.where(lag2 >= j, pltpu.roll(raw, j, 0), 0.0)
    act = v * jax.nn.sigmoid(v)
    bc_ref[...] = act.astype(BF16)
    bct_ref[...] = turned(act.astype(BF16))
    z = small_ref[:, 256:384] + hp_ref[0:1, :]
    dt = jnp.maximum(z, 0.0) + jnp.log1p(jnp.exp(-jnp.abs(z)))
    a = -dt * jnp.exp(hp_ref[1:2, :])
    tri_r = lax.broadcasted_iota(jnp.int32, (SPAN, SPAN), 0)
    tri_c = lax.broadcasted_iota(jnp.int32, (SPAN, SPAN), 1)
    lower = (tri_r >= tri_c).astype(F32)
    seg_row = segr_ref[0:1, :]
    for c in range(blocks):
        r0 = c * SPAN
        rows = slice(r0, r0 + SPAN)
        cum = dot_exact(lower, a[rows])
        segb = seg[rows]
        last = seg[r0 + SPAN - 1 : r0 + SPAN]
        tail = (segb == last).astype(F32)
        end = cum[SPAN - 1 : SPAN]
        q = jnp.exp(end - cum) * tail
        if c > 0:
            prev = seg[r0 - 1 : r0]
            p = jnp.exp(cum) * (segb == prev).astype(F32)
            k = jnp.exp(end) * (last == prev).astype(F32)
        else:
            p = jnp.zeros_like(cum)
            k = jnp.zeros_like(end)
        kexp_ref[c : c + 1, :] = k
        cumt = jnp.transpose(cum)
        dtb = dt[rows]
        for g in range(groups):
            hs = slice(PER * g, PER * g + PER)
            colp_ref[g, rows, 0:4] = cum[:, hs]
            colp_ref[g, rows, 4:8] = dtb[:, hs]
            colp_ref[g, rows, 8:12] = p[:, hs]
            colp_ref[g, rows, 12:16] = q[:, hs]
            cumt_ref[g, 0:4, rows] = cumt[hs, :]
        bb = bc_ref[rows, 0:STATE]
        cc = bc_ref[rows, STATE : 2 * STATE]
        same = across(segb) == seg_row[:, rows]
        g_ref[rows, :] = jnp.where(same & (tri_r >= tri_c), dot_nt(cc, bb), 0.0)
        gt_ref[rows, :] = jnp.where(same & (tri_r <= tri_c), dot_nt(bb, cc), 0.0)
    if blocks < kexp_ref.shape[0]:
        kexp_ref[blocks:, :] = jnp.zeros((kexp_ref.shape[0] - blocks, 128), F32)


def conv_rows(xr_ref, lag_ref, chan_ref, r0):
    cur = xr_ref[pl.ds(r0, SPAN), :]
    before = xr_ref[pl.ds(pl.multiple_of(jnp.maximum(r0 - 8, 0), 8), 8), :]
    both = jnp.concatenate([before, cur], axis=0)
    lag = twice(lag_ref[pl.ds(r0, SPAN), :])
    v = chan_ref[4:5, :] + chan_ref[3:4, :] * cur
    for j in range(1, KW):
        earlier = pltpu.roll(both, j, 0)[8:]
        v = v + chan_ref[3 - j : 4 - j, :] * jnp.where(lag >= j, earlier, 0.0)
    return cur, v


def scan_kernel(
    nb_ref, wg_ref, wx_ref, chan_ref, lag_ref, bc_ref, bct_ref, g_ref, colp_ref, cumt_ref, kexp_ref,
    gate_ref, xr_ref, y_ref, gated_ref, sq_ref, st_ref, state,
):
    length = gate_ref.shape[0]
    blocks = length // SPAN
    state[...] = jnp.zeros_like(state)

    @pl.when(pl.program_id(0) == 0)
    def _():
        sq_ref[...] = jnp.zeros_like(sq_ref)

    def project(c, carry):
        rows = pl.ds(pl.multiple_of(c * 512, 512), 512)
        gate_ref[rows, :] = dot_nn(nb_ref[rows, :], wg_ref[...])
        xr_ref[rows, :] = dot_nn(nb_ref[rows, :], wx_ref[...])
        return carry

    lax.fori_loop(0, length // 512, project, 0)

    def body(c, carry):
        r0 = pl.multiple_of(c * SPAN, SPAN)
        rows = pl.ds(r0, SPAN)
        _, v = conv_rows(xr_ref, lag_ref, chan_ref, r0)
        xc = (v * jax.nn.sigmoid(v)).astype(BF16).astype(F32)
        cp = colp_ref[0, rows, :]
        xd = (spread(cp[:, 4:8]) * xc).astype(BF16)
        px = spread(cp[:, 8:12])
        qx = spread(cp[:, 12:16])
        gb = g_ref[rows, :]
        lefts, rights = [], []
        for h in range(PER):
            gap = cp[:, h : h + 1] - cumt_ref[0, h : h + 1, rows]
            lefts.append((gb * jnp.exp(jnp.minimum(gap, 0.0))).astype(BF16))
            rights.append(xd * head_mask(h))
        y = dot_nn(jnp.concatenate(lefts, axis=1), jnp.concatenate(rights, axis=0))
        st = state[...]
        stb = st.astype(BF16)
        st_ref[c] = stb
        y = y + px * dot_nn(bc_ref[rows, STATE : 2 * STATE], stb)
        kx = kexp_ref[pl.ds(c, 1), :]
        state[...] = kx * st + dot_nn(bct_ref[0:STATE, rows], (qx * xd.astype(F32)).astype(BF16))
        y = y + chan_ref[5:6, :] * xc
        y_ref[rows, :] = y
        gate = gate_ref[rows, :]
        gated = y * (gate * jax.nn.sigmoid(gate))
        gated_ref[rows, :] = gated.astype(BF16)
        sq = gated * gated
        sq_ref[rows, :] += sq[:, 0:128] + sq[:, 128:256]
        return carry

    lax.fori_loop(0, blocks, body, 0)


def scan_grad_kernel(
    place, gate_ref, xr_ref, y_ref, dh_ref, chan_ref, lag_ref, ir_ref, cf_ref, bc_ref, bct_ref, gt_ref,
    colp_ref, cumt_ref, kexp_ref, st_ref, segc_ref, segr_ref,
    small_ref, hp_ref, bcp_ref,
    dgate_ref, dxr_ref, chg_ref, nd_ref, ds_ref, pg_ref,
    dst, head, dgt, dbc_ref, end_ref, acc_a, acc_d, acc_e,
):
    length = gate_ref.shape[0]
    blocks = length // SPAN
    step = pl.program_id(0)
    dst[...] = jnp.zeros_like(dst)
    head[...] = jnp.zeros_like(head)
    end_ref[...] = jnp.zeros_like(end_ref)
    chg_ref[...] = jnp.zeros_like(chg_ref)

    @pl.when(step == 0)
    def _():
        dgt[...] = jnp.zeros_like(dgt)
        dbc_ref[...] = jnp.zeros_like(dbc_ref)
        nd_ref[...] = jnp.zeros_like(nd_ref)
        acc_a[...] = jnp.zeros_like(acc_a)
        acc_d[...] = jnp.zeros_like(acc_d)
        acc_e[...] = jnp.zeros_like(acc_e)

    pick_r = lax.broadcasted_iota(jnp.int32, (GROUP, 128), 0)
    pick_c = lax.broadcasted_iota(jnp.int32, (GROUP, 128), 1)
    pick32 = (pick_r // HEADDIM + PER * place == pick_c).astype(F32)
    pick = pick32.astype(BF16)

    def per_head(v):
        hi = v.astype(BF16)
        lo = (v - hi.astype(F32)).astype(BF16)
        return dot_nn(hi, pick) + dot_nn(lo, pick)

    def total(v):
        return jnp.sum(v, axis=0, keepdims=True)

    def body(back, carry):
        c = blocks - 1 - back
        r0 = pl.multiple_of(c * SPAN, SPAN)
        rows = pl.ds(r0, SPAN)
        cur, v = conv_rows(xr_ref, lag_ref, chan_ref, r0)
        sv = jax.nn.sigmoid(v)
        xc = (v * sv).astype(BF16).astype(F32)
        cp = colp_ref[0, rows, :]
        dtx = spread(cp[:, 4:8])
        px = spread(cp[:, 8:12])
        qx = spread(cp[:, 12:16])
        xd = (dtx * xc).astype(BF16)
        xdf = xd.astype(F32)
        gate = gate_ref[rows, :]
        y = y_ref[rows, :]
        dh = dh_ref[rows, :].astype(F32)
        ir = twice(ir_ref[rows, :])
        cf = twice(cf_ref[rows, :])
        sg = jax.nn.sigmoid(gate)
        sl = gate * sg
        gated = y * sl
        dgd = ir * (dh * chan_ref[6:7, :]) - gated * cf
        dy = dgd * sl
        dgate = dgd * y * (sg * (1.0 + gate * (1.0 - sg)))
        dgate_ref[rows, :] = dgate.astype(BF16)
        dyb = dy.astype(BF16)
        gt = gt_ref[rows, :]
        lefts, rights = [], []
        acc = dgt[rows, :]
        for h in range(PER):
            gap = cumt_ref[0, h : h + 1, rows] - cp[:, h : h + 1]
            et = jnp.exp(jnp.minimum(gap, 0.0))
            lefts.append((gt * et).astype(BF16))
            dym = dyb * head_mask(h)
            rights.append(dym)
            acc = acc + dot_nt(xd, dym) * et
        dgt[rows, :] = acc
        u = dot_nn(jnp.concatenate(lefts, axis=1), jnp.concatenate(rights, axis=0))
        ds = dst[...]
        dsb = ds.astype(BF16)
        bb = bc_ref[rows, 0:STATE]
        cc = bc_ref[rows, STATE : 2 * STATE]
        ui = qx * dot_nn(bb, dsb)
        u = u + ui
        dxc = chan_ref[5:6, :] * dy + dtx * u
        yscan = y - chan_ref[5:6, :] * xc
        acc_a[rows, :] += per_head(dyb.astype(F32) * yscan - xdf * u)
        acc_d[rows, :] += per_head(xc * u)
        stb = st_ref[c]
        kx = kexp_ref[pl.ds(c, 1), :]
        end_ref[pl.ds(c, 1), :] = total(xdf * ui) + kx * total(ds * stb.astype(F32))
        pdy = (px * dyb.astype(F32)).astype(BF16)
        dbc_ref[rows, 0:STATE] += dot_nt((qx * xdf).astype(BF16), dsb)
        dbc_ref[rows, STATE : 2 * STATE] += dot_nt(pdy, stb)
        dst[...] = kx * ds + dot_nn(bct_ref[STATE : 2 * STATE, rows], pdy)
        dv = dxc * (sv * (1.0 + v * (1.0 - sv)))
        after = pl.ds(pl.multiple_of(r0 + SPAN, 8), 8)
        wide = jnp.concatenate([dv, head[...]], axis=0)
        lagw = jnp.concatenate([twice(lag_ref[rows, :]), twice(lag_ref[after, :])], axis=0)
        head[...] = dv[0:8]
        dxr = chan_ref[3:4, :] * dv
        chg_ref[3:4, :] += total(cur * dv)
        chg_ref[4:5, :] += total(dv)
        chg_ref[5:6, :] += total(dy * xc)
        chg_ref[6:7, :] += total(dh * gated * ir)
        for j in range(1, KW):
            later = pltpu.roll(jnp.where(lagw >= j, wide, 0.0), SPAN + 8 - j, 0)[0:SPAN]
            dxr = dxr + chan_ref[3 - j : 4 - j, :] * later
            chg_ref[3 - j : 4 - j, :] += total(cur * later)
        dxr_ref[rows, :] = dxr.astype(BF16)
        nd = dgate * gate + dxr * cur
        nd_ref[rows, :] += nd[:, 0:128] + nd[:, 128:256]
        return carry

    lax.fori_loop(0, blocks, body, 0)

    acc_e[...] += dot_exact(end_ref[...], pick32)

    @pl.when(step == pl.num_programs(0) - 1)
    def _():
        tri_r = lax.broadcasted_iota(jnp.int32, (SPAN, SPAN), 0)
        tri_c = lax.broadcasted_iota(jnp.int32, (SPAN, SPAN), 1)
        upper = (tri_r <= tri_c).astype(F32)
        rate = jnp.exp(hp_ref[1:2, :])
        pg_ref[...] = jnp.zeros_like(pg_ref)
        for c in range(blocks):
            rows = slice(c * SPAN, (c + 1) * SPAN)
            same = across(segc_ref[rows, :]) == segr_ref[0:1, rows]
            full = jnp.where(same & (tri_r <= tri_c), dgt[rows, :], 0.0)
            dbc_ref[rows, 0:STATE] += dot_nn(full.astype(BF16), bc_ref[rows, STATE : 2 * STATE])
            dbc_ref[rows, STATE : 2 * STATE] += dot_nn(
                jnp.transpose(full).astype(BF16), bc_ref[rows, 0:STATE]
            )
            da = dot_exact(upper, acc_a[rows, :]) + acc_e[c : c + 1, :]
            raw = small_ref[rows, 2 * STATE :]
            z = raw + hp_ref[0:1, :]
            dt = jnp.maximum(z, 0.0) + jnp.log1p(jnp.exp(-jnp.abs(z)))
            ddt = (acc_d[rows, :] - rate * da) * jax.nn.sigmoid(z)
            pg_ref[5:6, 0:128] += total(ddt)
            pg_ref[6:7, 0:128] += -rate * total(da * dt)
            ds_ref[rows, 2 * STATE :] = ddt.astype(BF16)
            nd_ref[rows, :] += ddt * raw
        raw = small_ref[:, 0 : 2 * STATE]
        lag = twice(lag_ref[0:length, :])
        v = bcp_ref[4:5, :] + bcp_ref[3:4, :] * raw
        for j in range(1, KW):
            v = v + bcp_ref[3 - j : 4 - j, :] * jnp.where(lag >= j, pltpu.roll(raw, j, 0), 0.0)
        sv = jax.nn.sigmoid(v)
        dv = dbc_ref[...] * (sv * (1.0 + v * (1.0 - sv)))
        dr = bcp_ref[3:4, :] * dv
        pg_ref[3:4, :] = total(raw * dv)
        pg_ref[4:5, :] = total(dv)
        for j in range(1, KW):
            later = pltpu.roll(jnp.where(lag >= j, dv, 0.0), length - j, 0)
            dr = dr + bcp_ref[3 - j : 4 - j, :] * later
            pg_ref[3 - j : 4 - j, :] = total(raw * later)
        ds_ref[:, 0 : 2 * STATE] = dr.astype(BF16)
        nd = dr * raw
        nd_ref[...] += nd[:, 0:128] + nd[:, 128:256]


def whole(shape):
    return pl.BlockSpec(shape, lambda g: (0,) * len(shape))


def once(shape):
    return pl.BlockSpec(shape, lambda g: (0,) * len(shape), pipeline_mode=pl.Buffered(1))


def tile(rows):
    return pl.BlockSpec((rows, GROUP), lambda g: (0, g))


def prep_shapes(length, groups):
    return (
        jax.ShapeDtypeStruct((length, 2 * STATE), BF16),
        jax.ShapeDtypeStruct((2 * STATE, length), BF16),
        jax.ShapeDtypeStruct((length, SPAN), F32),
        jax.ShapeDtypeStruct((length, SPAN), F32),
        jax.ShapeDtypeStruct((groups, length, 16), F32),
        jax.ShapeDtypeStruct((groups, 8, length), F32),
        jax.ShapeDtypeStruct((8, 128), F32),
        jax.ShapeDtypeStruct((length + 8, 128), F32),
    )


def prep(small, segc, segr, bcp, hp, groups):
    return pl.pallas_call(
        prep_kernel,
        out_shape=prep_shapes(small.shape[0], groups),
        compiler_params=pltpu.CompilerParams(vmem_limit_bytes=VMEM_LIMIT),
        name="prep",
    )(small, segc, segr, bcp, hp)


def scan_specs(length, width, gb):
    last = 2 * gb - 1

    def at(g):
        return jnp.minimum(g, last)

    def strip(rows):
        return pl.BlockSpec((rows, GROUP), lambda g: (0, at(g)))

    weight = pl.BlockSpec((None, width, GROUP), lambda g: (at(g) // gb, 0, at(g) % gb))
    return [
        once((length, width)),
        weight,
        weight,
        strip(8),
        once((length + 8, 128)),
        once((length, 2 * STATE)),
        once((2 * STATE, length)),
        once((length, SPAN)),
        pl.BlockSpec((1, length, 16), lambda g: (at(g), 0, 0)),
        pl.BlockSpec((1, 8, length), lambda g: (at(g), 0, 0)),
        strip(8),
    ], [
        strip(length),
        strip(length),
        strip(length),
        strip(length),
        whole((length, 128)),
        pl.BlockSpec((length // SPAN, STATE, GROUP), lambda g: (0, 0, at(g))),
    ]


def scan_shapes(length, channels):
    return (
        jax.ShapeDtypeStruct((length, channels), F32),
        jax.ShapeDtypeStruct((length, channels), F32),
        jax.ShapeDtypeStruct((length, channels), F32),
        jax.ShapeDtypeStruct((length, channels), BF16),
        jax.ShapeDtypeStruct((length, 128), F32),
        jax.ShapeDtypeStruct((length // SPAN, STATE, channels), BF16),
    )


def scan(nb, wg, wx, chan, *rest):
    length, width = nb.shape
    channels = chan.shape[1]
    in_specs, out_specs = scan_specs(length, width, channels // GROUP // 2)
    return pl.pallas_call(
        scan_kernel,
        grid=(channels // GROUP,),
        in_specs=in_specs,
        out_specs=out_specs,
        out_shape=scan_shapes(length, channels),
        scratch_shapes=[pltpu.VMEM((STATE, GROUP), F32)],
        compiler_params=pltpu.CompilerParams(vmem_limit_bytes=VMEM_LIMIT),
        name="scan",
    )(nb, wg, wx, chan, *rest)


def scan_grad_specs(length, channels, shift=0):
    blocks = length // SPAN
    groups = channels // GROUP

    def at(g):
        return lax.rem(g + shift, groups)

    def tile(rows):
        return pl.BlockSpec((rows, GROUP), lambda g: (0, at(g)))

    ins = [
        tile(length),
        tile(length),
        tile(length),
        tile(length),
        tile(8),
        once((length + 8, 128)),
        once((length, 128)),
        once((length, 128)),
        once((length, 2 * STATE)),
        once((2 * STATE, length)),
        once((length, SPAN)),
        pl.BlockSpec((1, length, 16), lambda g: (at(g), 0, 0)),
        pl.BlockSpec((1, 8, length), lambda g: (at(g), 0, 0)),
        tile(8),
        pl.BlockSpec((blocks, STATE, GROUP), lambda g: (0, 0, at(g))),
        once((length, 128)),
        once((8, length)),
        once((length, 2 * STATE + 128)),
        once((8, 128)),
        once((8, 2 * STATE)),
    ]
    outs = [
        tile(length),
        tile(length),
        tile(8),
        once((length, 128)),
        once((length, 2 * STATE + 128)),
        once((8, 2 * STATE)),
    ]
    shapes = (
        jax.ShapeDtypeStruct((length, channels), BF16),
        jax.ShapeDtypeStruct((length, channels), BF16),
        jax.ShapeDtypeStruct((8, channels), F32),
        jax.ShapeDtypeStruct((length, 128), F32),
        jax.ShapeDtypeStruct((length, 2 * STATE + 128), BF16),
        jax.ShapeDtypeStruct((8, 2 * STATE), F32),
    )
    scratch = [
        pltpu.VMEM((STATE, GROUP), F32),
        pltpu.VMEM((8, GROUP), F32),
        pltpu.VMEM((length, SPAN), F32),
        pltpu.VMEM((length, 2 * STATE), F32),
        pltpu.VMEM((8, GROUP), F32),
        pltpu.VMEM((length, 128), F32),
        pltpu.VMEM((length, 128), F32),
        pltpu.VMEM((8, 128), F32),
    ]
    return ins, outs, shapes, scratch


def scan_grad(*args):
    length, channels = args[0].shape
    ins, outs, shapes, scratch = scan_grad_specs(length, channels)
    return pl.pallas_call(
        lambda *refs: scan_grad_kernel(pl.program_id(0), *refs),
        grid=(channels // GROUP,),
        in_specs=ins,
        out_specs=outs,
        out_shape=shapes,
        scratch_shapes=scratch,
        compiler_params=pltpu.CompilerParams(vmem_limit_bytes=VMEM_LIMIT),
        name="scan_grad",
    )(*args)


def back_kernel(a0, a1, a2, w0, w1, w2, nb_ref, dn_ref, gg_ref):
    cb = w0.shape[2]
    total = dot_nt(a2[...], w2[...])
    for a, w in ((a0, w0), (a1, w1)):
        for b in range(2):
            total = total + dot_nt(a[:, b * cb : (b + 1) * cb], w[b])
    dn_ref[0] = total.astype(BF16)
    gg = jnp.sum(total * nb_ref[...].astype(F32), axis=0, keepdims=True)
    gg_ref[...] = jnp.broadcast_to(gg, gg_ref.shape)


def back(dgate, dxr, d_small, wg, wx, w_small, nb):
    length, width = nb.shape
    cb = wg.shape[2]
    feat = max(width // 4, 256)
    per = feat // 256
    wide = pl.BlockSpec((2, 256, cb), lambda n: (0, n, 0))
    return pl.pallas_call(
        back_kernel,
        grid=(width // 256,),
        in_specs=[once(a.shape) for a in (dgate, dxr, d_small)]
        + [wide, wide]
        + [pl.BlockSpec((256, d_small.shape[1]), lambda n: (n, 0))]
        + [pl.BlockSpec((length, 256), lambda n: (0, n))],
        out_specs=[
            pl.BlockSpec((1, length, 256), lambda n: (n // per, 0, n % per)),
            pl.BlockSpec((8, 256), lambda n: (0, n)),
        ],
        out_shape=(
            jax.ShapeDtypeStruct((width // feat, length, feat), BF16),
            jax.ShapeDtypeStruct((8, width), F32),
        ),
        compiler_params=pltpu.CompilerParams(vmem_limit_bytes=VMEM_LIMIT),
        name="back",
    )(dgate, dxr, d_small, wg, wx, w_small, nb)


MESH_ID = pl.DeviceIdType.MESH


class Copies:
    def __init__(self, send, recv):
        self.send, self.recv, self.count, self.open = send, recv, 0, []

    def start(self, src, dst, to):
        copy = pltpu.make_async_remote_copy(
            src_ref=src, dst_ref=dst, send_sem=self.send.at[self.count],
            recv_sem=self.recv.at[self.count], device_id=to, device_id_type=MESH_ID,
        )
        self.count += 1
        copy.start()
        self.open.append(copy)
        return copy

    def finish(self):
        for copy in self.open:
            copy.wait_send()


def places():
    h, l, r = lax.axis_index("zh"), lax.axis_index("zl"), lax.axis_index("row")
    c, x, y = lax.rem(r, 2), lax.rem(r // 2, 2), r // 4
    rx, ry = r + 2 - 4 * x, r + 4 - 8 * y
    rc = r + 1 - 2 * c
    return h, l, r, c, x, y, rx, ry, rc


def meet(peers):
    barrier = pltpu.get_barrier_semaphore()
    for to in peers:
        pl.semaphore_signal(barrier, inc=1, device_id=to, device_id_type=MESH_ID)
    pl.semaphore_wait(barrier, len(peers))


GATHER_COPIES = 96
PIECES = 4
FINE = 8


def gather_kernel(
    x_ref, wg_ref, wx_ref, thin_ref, par_ref, segc_ref, segr_ref,
    nb_ref, nt_ref, ir_ref, par_out, ws_ref, small_ref, hp_ref, bcp_ref,
    bc_ref, bct_ref, g_ref, gt_ref, colp_ref, cumt_ref, kexp_ref, lag_ref, wg_out, wx_out,
    xv, parv, thin_v, stage, send, recv, local,
):
    h, l, r, c, x, y, rx, ry, rc = places()
    rd = rx + ry - r
    me, zhp = h * 2 + l, (1 - h) * 2 + l
    zh, zl, zd = {"zh": 1 - h}, {"zl": 1 - l}, {"zh": 1 - h, "zl": 1 - l}
    to_x, to_y, to_c = {"row": rx}, {"row": ry}, {"row": rc}
    length, feat = x_ref.shape[1], x_ref.shape[2]
    step = length // FINE
    shard = wg_ref.shape[0]
    meet((zh, zl, zd, to_x, to_y, to_c))
    copies = Copies(send, recv)
    start = copies.start

    def cols(block):
        return pl.ds(pl.multiple_of(block * feat, feat), feat)

    def toks(p):
        return pl.ds(p * step, step)

    def rows(row):
        return pl.ds(pl.multiple_of(row * shard, shard), shard)

    src = (wg_ref, wx_ref)
    dst = ((wg_out.at[0], wx_out.at[0]), (wg_out.at[1], wx_out.at[1]))
    keeps = [
        pltpu.make_async_copy(par_ref, parv.at[me], local.at[0]),
        pltpu.make_async_copy(thin_ref, thin_v.at[r, me], local.at[1]),
        pltpu.make_async_copy(x_ref.at[h], xv.at[:, cols(me)], local.at[2]),
        pltpu.make_async_copy(wg_ref, stage.at[0], local.at[3]),
        pltpu.make_async_copy(wx_ref, stage.at[1], local.at[4]),
    ]
    for keep in keeps:
        keep.start()
    laid = [pltpu.make_async_copy(stage.at[k], dst[0][k].at[rows(r)], local.at[5 + k]) for k in range(2)]
    pars = [start(par_ref, parv.at[me], to) for to in (zh, zl, zd)]
    thins = [start(thin_ref, thin_v.at[r, me], to) for to in (zh, zl, zd)]
    sib, sib_thin, x1, x3, wz, got, far = [], [], [], [], [], {}, {}
    bcn, hb = 2 * STATE // 4, colp_ref.shape[0] * PER // 2
    part = shard // 2

    def chunk(b, q, row):
        if b == 0:
            return dst[0][q].at[rows(row)]
        return dst[1][q // 2].at[pl.ds(pl.multiple_of(row * shard + q % 2 * part, part), part)]

    def send_w(q):
        wz.append(start(src[q // 2].at[pl.ds(q % 2 * part, part)], chunk(1, q, r), zh))

    def deal(b, q):
        if b == 0:
            got[b, q] = [start(src[q], chunk(b, q, r), to) for to in (to_x, to_y, to_c)]
        else:
            wz[q].wait_recv()
            got[b, q] = [start(chunk(b, q, r), chunk(b, q, r), to) for to in (to_x, to_y, to_c)]
        sib.append(got[b, q][2])

    def pass_on(b, q, n):
        piece = chunk(b, q, (rx, ry)[n])
        got[b, q][n].wait_recv()
        if n == q % 2:
            far[b, q] = start(piece, piece, (to_y, to_x)[n])
        sib.append(start(piece, piece, to_c))

    def corner(b, q):
        far[b, q].wait_recv()
        sib.append(start(chunk(b, q, rd), chunk(b, q, rd), to_c))

    def send_x():
        if len(x1) < FINE:
            p = len(x1)
            x1.append(start(x_ref.at[1 - h, toks(p)], xv.at[toks(p), cols(me)], zh))

    def pass_x(p):
        x1[p].wait_recv()
        x3.append(start(xv.at[toks(p), cols(zhp)], xv.at[toks(p), cols(zhp)], zl))
        send_x()

    for q in range(3):
        send_w(q)
    x2 = start(x_ref.at[h], xv.at[:, cols(me)], zl)
    for q in range(2):
        deal(0, q)
    for k in range(2):
        keeps[3 + k].wait()
        laid[k].start()
    keeps[1].wait()
    for copy in thins:
        copy.wait_recv()
    thin_go = [start(thin_v.at[r], thin_v.at[r], to) for to in (to_x, to_y, to_c)]
    sib_thin.append(thin_go[2])
    for q in range(2):
        for n in range(2):
            pass_on(0, q, n)
    thin_go[0].wait_recv()
    thin_d = start(thin_v.at[rx], thin_v.at[rx], to_y)
    sib_thin.append(start(thin_v.at[rx], thin_v.at[rx], to_c))
    thin_go[1].wait_recv()
    sib_thin.append(start(thin_v.at[ry], thin_v.at[ry], to_c))

    for copy in pars:
        copy.wait_recv()
    keeps[0].wait()
    keeps[2].wait()
    par_out[...] = parv[...]
    bcp_ref[...] = jnp.zeros_like(bcp_ref)
    bcp_ref[0:5, :] = sum(parv[b, 9:14, 0 : 2 * STATE] for b in range(4))
    hp_ref[...] = jnp.zeros_like(hp_ref)
    hp_ref[0:2, :] = parv[me, 14:16, 0:128] + pltpu.roll(parv[zhp, 14:16, 0:128], hb, 1)

    def norm(p):
        if p == 0:
            x2.wait_recv()
        x3[p].wait_recv()
        total = jnp.zeros((step, 1), F32)
        for b in range(4):
            value = xv[toks(p), b * feat : (b + 1) * feat].astype(F32)
            total = total + jnp.sum(value * value, axis=1, keepdims=True)
        root = lax.rsqrt(total / (4 * feat) + EPS)
        ir_ref[toks(p), :] = jnp.broadcast_to(root, (step, 128))
        for b in range(8):
            value = xv[toks(p), b * shard : (b + 1) * shard].astype(F32)
            gain = parv[b // 2, 8:9, b % 2 * shard : (b % 2 + 1) * shard]
            value = (value * root * gain).astype(BF16)
            nb_ref[toks(p), b * shard : (b + 1) * shard] = value
            nt_ref[b % 2, b // 2 * shard : (b // 2 + 1) * shard, toks(p)] = turned(value)

    def narrow(p):
        some = slice(p * (length // 2), (p + 1) * (length // 2))
        small_ref[some, :] = dot_nn(nb_ref[some, :], ws_ref[...])

    corner(0, 1)
    deal(1, 0)
    send_w(3)
    deal(1, 1)
    send_x()
    deal(1, 2)
    send_x()
    thin_d.wait_recv()
    sib_thin.append(start(thin_v.at[rd], thin_v.at[rd], to_c))
    for copy in sib_thin:
        copy.wait_recv()
    ws_ref[...] = jnp.zeros_like(ws_ref)
    for row in range(8):
        at = slice(row * shard, (row + 1) * shard)
        for b in range(4):
            ws_ref[at, b * bcn : (b + 1) * bcn] = thin_v[row, b, :, 0:bcn]
        ws_ref[at, 2 * STATE : 2 * STATE + hb] = thin_v[row, me, :, bcn : bcn + hb]
        ws_ref[at, 2 * STATE + hb : 2 * STATE + 2 * hb] = thin_v[row, zhp, :, bcn : bcn + hb]
    corner(0, 0)
    for q in range(3):
        pass_on(1, q, 0)
    pass_x(0)
    pass_x(1)
    for q in range(3):
        pass_on(1, q, 1)
    corner(1, 1)
    deal(1, 3)
    send_x()
    norm(0)
    norm(1)
    corner(1, 0)
    corner(1, 2)
    pass_x(2)
    pass_x(3)
    pass_on(1, 3, 0)
    pass_on(1, 3, 1)
    norm(2)
    pass_x(4)
    pass_x(5)
    norm(3)
    corner(1, 3)
    narrow(0)
    norm(4)
    pass_x(6)
    pass_x(7)
    norm(5)
    norm(6)
    norm(7)
    narrow(1)
    prep_kernel(
        small_ref, segc_ref, segr_ref, bcp_ref, hp_ref,
        bc_ref, bct_ref, g_ref, gt_ref, colp_ref, cumt_ref, kexp_ref, lag_ref,
    )
    for copy in sib:
        copy.wait_recv()
    for move in laid:
        move.wait()
    copies.finish()


def gather_all(x, wg, wx, thin, par, segc, segr, groups):
    _, length, feat = x.shape
    shard, cb = wg.shape
    anywhere = pl.BlockSpec(memory_space=pl.ANY)
    inside = pl.BlockSpec(memory_space=pltpu.VMEM)
    weight = jax.ShapeDtypeStruct((2, 8 * shard, cb), BF16)
    return pl.pallas_call(
        gather_kernel,
        in_specs=[anywhere] * 5 + [inside] * 2,
        out_specs=[inside] * 16 + [anywhere] * 2,
        out_shape=(
            jax.ShapeDtypeStruct((length, 4 * feat), BF16),
            jax.ShapeDtypeStruct((2, 4 * shard, length), BF16),
            jax.ShapeDtypeStruct((length, 128), F32),
            jax.ShapeDtypeStruct((4,) + par.shape, F32),
            jax.ShapeDtypeStruct((8 * shard, 2 * STATE + 128), BF16),
            jax.ShapeDtypeStruct((length, 2 * STATE + 128), F32),
            jax.ShapeDtypeStruct((8, 128), F32),
            jax.ShapeDtypeStruct((8, 2 * STATE), F32),
        )
        + prep_shapes(length, groups)
        + (weight, weight),
        scratch_shapes=[
            pltpu.VMEM((length, 4 * feat), BF16),
            pltpu.VMEM((4,) + par.shape, F32),
            pltpu.VMEM((8, 4) + thin.shape, BF16),
            pltpu.VMEM((2, shard, cb), BF16),
            pltpu.SemaphoreType.DMA((GATHER_COPIES,)),
            pltpu.SemaphoreType.DMA((GATHER_COPIES,)),
            pltpu.SemaphoreType.DMA((8,)),
        ],
        compiler_params=pltpu.CompilerParams(
            collective_id=0, has_side_effects=True, vmem_limit_bytes=VMEM_LIMIT
        ),
        name="gather_all",
    )(x, wg, wx, thin, par, segc, segr)


GRAD_COPIES = 96


def grad_kernel(
    dn_ref, raw_ref, nt_ref, dx_ref, ds_ref, small_ref, nd_ref, ir_ref, gate_ref,
    gz_ref, thin_out, small_out, own_out, away_out, row_out,
    raw_v, pa, pr, ps, rowv, rowr, local, cs, cr, ts, tr, fs, fr, ss, sr, zs, zr, tfs, tfr, tss, tsr, tz, tzr,
    sbuf, srecv, szr, send, recv,
):
    h, l, r, c, x, y, rx, ry, rc = places()
    me = h * 2 + l
    zh, zl, zd = {"zh": 1 - h}, {"zl": 1 - l}, {"zh": 1 - h, "zl": 1 - l}
    to_x, to_y, to_c = {"row": rx}, {"row": ry}, {"row": rc}
    shard = gz_ref.shape[1]
    ncol = gz_ref.shape[2]
    meet((zh, zl, zd, to_x, to_y, to_c))
    copies = Copies(send, recv)
    start = copies.start

    def product(side, d_ref, at):
        return dot_nn(nt_ref[side], d_ref[:, at])

    def tiles(d_ref, body):
        width = d_ref.shape[1]
        wide = 256 if width % 256 == 0 else 128

        def one(n, carry):
            body(pl.ds(pl.multiple_of(n * wide, wide), wide))
            return carry

        lax.fori_loop(0, width // wide, one, 0)

    length, feat = ps.shape
    piece = length // FINE

    def toks(p):
        return pl.ds(p * piece, piece)

    raw_copy = pltpu.make_async_copy(raw_ref.at[1], raw_v, local.at[2])
    raw_copy.start()
    near = [pltpu.make_async_copy(dn_ref.at[2 * k + l], pa.at[k], local.at[k]) for k in range(2)]
    for move in near:
        move.start()
    pair, far = [], []

    def give():
        p = len(pair)
        if p < FINE:
            pair.append(
                [start(dn_ref.at[2 * k + 1 - l, toks(p)], pr.at[k, toks(p)], zl) for k in range(2)]
            )

    def pair_done(p):
        if p == 0:
            for move in near:
                move.wait()
        for move in pair[p]:
            move.wait_recv()
        give()
        part = pa[1 - h, toks(p)].astype(F32) + pr[1 - h, toks(p)].astype(F32)
        ps[toks(p)] = part.astype(BF16)
        far.append(start(ps.at[toks(p)], away_out.at[toks(p)], zh))
        own_out[toks(p)] = pa[h, toks(p)].astype(F32) + pr[h, toks(p)].astype(F32)

    z_copy = [start(gate_ref, zr.at[0], zh), None]
    for _ in range(3):
        give()
    rowv[...] = jnp.zeros_like(rowv)
    rowv[0:1, :] = jnp.sum(jnp.transpose(nd_ref[...]), axis=0, keepdims=True)
    rowv[1:2, :] = jnp.transpose(ir_ref[...])[0:1, :]
    row_copies = [start(rowv, rowr.at[n], to) for n, to in enumerate((zh, zl, zd))]

    sbuf[0] = small_ref[...]
    small_hops = [to_c, to_x, to_y]
    small_copy = start(sbuf.at[0], srecv.at[0], to_c)

    dx0, dx1 = dx_ref.at[:, 0:ncol], dx_ref.at[:, ncol : 2 * ncol]
    quarters = [
        dict(d=dx1, first=to_x, second=to_y, mine=x, along=y, swap=False),
        dict(d=dx0, first=to_x, second=to_y, mine=x, along=y, swap=False),
        dict(first=to_y, second=to_x, mine=y, along=x, swap=True),
    ]

    def spot(q, first, second):
        return 2 * first + second if q["swap"] else 2 * second + first

    def refs(i):
        if i == 4:
            return ts, tr, tfs, tfr, tss, tsr
        return cs.at[i % 2], cr.at[i], fs.at[i], fr.at[i], ss.at[i], sr.at[i]

    thin_q = dict(d=ds_ref, first=to_y, second=to_x, mine=y, along=x, swap=True)

    def to_core(i, q):
        out, back = refs(i)[0:2]
        if i == 2:
            q["core"] = start(raw_ref.at[0], back, to_c)
            return

        def body(at):
            value = product(1 - c, q["d"], at).astype(BF16)
            for j in range(4):
                out[j, :, at] = value[j * shard : (j + 1) * shard]

        tiles(q["d"], body)
        q["core"] = start(out, back, to_c)

    def to_first(i, q, after=None):
        _, back, fsend, frecv, _, _ = refs(i)
        q["core"].wait_recv()
        if i == 2:
            raw_copy.wait()
            for j in range(4):
                back[j] = (raw_v[j].astype(F32) + back[j].astype(F32)).astype(BF16)
        else:

            def body(at):
                value = product(c, q["d"], at)
                for j in range(4):
                    part = value[j * shard : (j + 1) * shard] + back[j, :, at].astype(F32)
                    back[j, :, at] = part.astype(BF16)

            tiles(q["d"], body)
        for n in range(2):
            fsend[n] = back[spot(q, 1 - q["mine"], n)]
        if after is not None:
            after["f"].wait_recv()
        q["f"] = start(fsend, frecv, q["first"])

    def to_second(i, q):
        _, back, _, frecv, ssend, srcv = refs(i)
        if i != 0:
            q["f"].wait_recv()
        far = 1 - q["along"]
        kept = back[spot(q, q["mine"], far)].astype(F32)
        ssend[...] = (kept + frecv[far].astype(F32)).astype(BF16)
        q["s"] = start(ssend, srcv, q["second"])

    def settle(i, q):
        _, back, _, frecv, _, srcv = refs(i)
        q["s"].wait_recv()
        near = q["along"]
        kept = back[spot(q, q["mine"], near)].astype(F32)
        return kept + frecv[near].astype(F32) + srcv[...].astype(F32)

    to_core(2, quarters[2])
    to_core(0, quarters[0])
    to_first(2, quarters[2])
    to_first(0, quarters[0])
    pair_done(0)
    to_core(1, quarters[1])
    pair_done(1)
    to_core(4, thin_q)
    pair_done(2)
    small_copy.wait_recv()
    sbuf[1] = sbuf[0] + srecv[0]
    small_copy = start(sbuf.at[1], srecv.at[1], to_x)
    pair_done(3)
    to_second(2, quarters[2])
    to_first(1, quarters[1], quarters[0])
    to_second(0, quarters[0])
    to_first(4, thin_q)
    pair_done(4)
    small_copy.wait_recv()
    sbuf[2] = sbuf[1] + srecv[1]
    small_copy = start(sbuf.at[2], srecv.at[2], to_y)
    pair_done(5)
    gz_ref[0] = settle(2, quarters[2])
    zs[...] = settle(0, quarters[0]).astype(BF16)
    z_copy[1] = start(zs, zr.at[1], zh)
    pair_done(6)
    to_second(4, thin_q)
    small_copy.wait_recv()
    sbuf[3] = sbuf[2] + srecv[2]
    small_z = [
        start(sbuf.at[3, lo:], szr.at[n, lo:], to) for n, (to, lo) in enumerate(((zh, 8), (zl, 16), (zd, 16)))
    ]
    pair_done(7)
    to_second(1, quarters[1])
    tz[...] = settle(4, thin_q).astype(BF16)
    thin_z = []
    for n, (to, block) in enumerate(((zh, 2 * (1 - h) + l), (zl, 2 * h + 1 - l), (zd, 2 * (1 - h) + 1 - l))):
        lanes = pl.ds(pl.multiple_of(block // 2 * 128, 128), 128)
        thin_z.append(start(tz.at[:, lanes], tzr.at[n], to))
    thin_z.append(start(tz.at[:, 2 * STATE :], tzr.at[3], zh))
    gz_ref[1] = settle(1, quarters[1])
    row_out[0] = rowv[...]
    for n in range(3):
        row_copies[n].wait_recv()
        row_out[n + 1] = rowr[n]
    for copy in thin_z:
        copy.wait_recv()
    for copy in small_z:
        copy.wait_recv()
    total = tz[:, pl.ds(pl.multiple_of(h * 128, 128), 128)].astype(F32)
    for n in range(3):
        total = total + tzr[n].astype(F32)
    thin_out[:, 0:128] = total
    thin_out[:, 128:256] = tz[:, 2 * STATE :].astype(F32)
    thin_out[:, 256:384] = tzr[3].astype(F32)
    small_out[...] = jnp.zeros_like(small_out)
    small_out[0] = sbuf[3]
    for n, lo in enumerate((8, 16, 16)):
        small_out[n + 1, lo:] = szr[n, lo:]
    for move in far:
        move.wait_recv()
    for k in range(2):
        z_copy[k].wait_recv()
        gz_ref[k] += zr[k].astype(F32)
    copies.finish()


def grad_all(dn, raw, nt, dxr, d_small, small, nd, ir, gate_got):
    _, half, length = nt.shape
    feat = dn.shape[2]
    shard, cb = half // 4, dxr.shape[1] // 2
    ns = d_small.shape[1]
    inside = pl.BlockSpec(memory_space=pltpu.VMEM)
    anywhere = pl.BlockSpec(memory_space=pl.ANY)
    V = pltpu.VMEM
    return pl.pallas_call(
        grad_kernel,
        in_specs=[anywhere] * 2 + [inside] * 6 + [anywhere],
        out_specs=[inside] * 4 + [anywhere, inside],
        out_shape=(
            jax.ShapeDtypeStruct((2, shard, cb), F32),
            jax.ShapeDtypeStruct((shard, 384), F32),
            jax.ShapeDtypeStruct((4,) + small.shape, F32),
            jax.ShapeDtypeStruct((length, feat), F32),
            jax.ShapeDtypeStruct((length, feat), BF16),
            jax.ShapeDtypeStruct((4, 8, length), F32),
        ),
        scratch_shapes=[
            V((4, shard, cb), BF16),
            V((2, length, feat), BF16),
            V((2, length, feat), BF16),
            V((length, feat), BF16),
            V((8, length), F32),
            V((3, 8, length), F32),
            pltpu.SemaphoreType.DMA((3,)),
            V((2, 4, shard, cb), BF16),
            V((3, 4, shard, cb), BF16),
            V((4, shard, ns), BF16),
            V((4, shard, ns), BF16),
            V((3, 2, shard, cb), BF16),
            V((3, 2, shard, cb), BF16),
            V((3, shard, cb), BF16),
            V((3, shard, cb), BF16),
            V((shard, cb), BF16),
            V((2, shard, cb), BF16),
            V((2, shard, ns), BF16),
            V((2, shard, ns), BF16),
            V((shard, ns), BF16),
            V((shard, ns), BF16),
            V((shard, ns), BF16),
            V((4, shard, 128), BF16),
            V((4,) + small.shape, F32),
            V((3,) + small.shape, F32),
            V((3,) + small.shape, F32),
            pltpu.SemaphoreType.DMA((GRAD_COPIES,)),
            pltpu.SemaphoreType.DMA((GRAD_COPIES,)),
        ],
        compiler_params=pltpu.CompilerParams(
            collective_id=1, has_side_effects=True, vmem_limit_bytes=VMEM_LIMIT
        ),
        name="grad_all",
    )(dn, raw, nt, dxr, d_small, small, nd, ir, gate_got)


def table(send, recv):
    def copy(n, src, dst, to):
        return pltpu.make_async_remote_copy(
            src_ref=src, dst_ref=dst, send_sem=send.at[n], recv_sem=recv.at[n],
            device_id=to, device_id_type=MESH_ID,
        )

    return copy


SCAN_COPIES = 32


def scan_all_kernel(*refs):
    (cot_ref, out_ref, gains_ref), refs = refs[0:3], refs[3:]
    ins, refs = refs[0:11], refs[11:]
    gate_ref, xr_ref, y_ref, hid_ref, sq_ref, st_ref, po_ref, ir_ref, cf_ref, wo_ref = refs[0:10]
    state, cot_v, out_v, rows_v, sums, other, send, recv, local, row_sem = refs[10:]
    h, l, r, c, x, y, rx, ry, rc = places()
    rd = rx + ry - r
    me, zhp = h * 2 + l, (1 - h) * 2 + l
    zh, zl = {"zh": 1 - h}, {"zl": 1 - l}
    to_x, to_y, to_c = {"row": rx}, {"row": ry}, {"row": rc}
    length, feat = cot_ref.shape[1], cot_ref.shape[2]
    piece = length // PIECES
    shard = out_ref.shape[0]
    copy = table(send, recv)
    step = pl.program_id(0)
    channels = hid_ref.shape[1]
    groups = channels // GROUP

    def toks(p):
        return pl.ds(p * piece, piece)

    def cols(block):
        return pl.ds(pl.multiple_of(block * feat, feat), feat)

    def rows(row, half=None):
        if half is None:
            return pl.ds(pl.multiple_of(row * shard, shard), shard)
        return pl.ds(pl.multiple_of(row * shard + half * (shard // 2), shard // 2), shard // 2)

    def g1(p):
        return copy(p, cot_ref.at[1 - h, toks(p)], cf_ref.at[toks(p), cols(me)], zh)

    def g2(p):
        return copy(4 + p, cot_ref.at[h, toks(p)], cf_ref.at[toks(p), cols(me)], zl)

    def g3(p):
        part = cf_ref.at[toks(p), cols(zhp)]
        return copy(8 + p, part, part, zl)

    def wz():
        return copy(12, out_ref, wo_ref.at[1, rows(r)], zh)

    def own(n):
        return copy(13 + n, out_ref, wo_ref.at[0, rows(r)], (to_x, to_y, to_c)[n])

    def got(n):
        part = wo_ref.at[1, rows(r)]
        return copy(16 + n, part, part, (to_x, to_y, to_c)[n])

    def diag(b, n):
        part = wo_ref.at[b, rows((rx, ry)[n], n)]
        return copy(19 + 5 * b + n, part, part, (to_y, to_x)[n])

    def sib(b, n):
        part = wo_ref.at[b, rows((rx, ry, rd)[n])]
        return copy(21 + 5 * b + n, part, part, to_c)

    def load(n):
        return pltpu.make_async_copy((cot_ref.at[h], out_ref)[n], (cot_v, out_v)[n], local.at[n])

    def keep(n):
        to = (cf_ref.at[:, cols(me)], wo_ref.at[0, rows(r)])[n]
        return pltpu.make_async_copy((cot_v, out_v)[n], to, local.at[2 + n])

    def load_rows(n, slot):
        part = pl.ds(pl.multiple_of(n * 256, 256), 256)
        return pltpu.make_async_copy(wo_ref.at[:, part], rows_v.at[slot], row_sem.at[slot])

    def onward(p):
        g1(p).wait_recv()
        g3(p).start()

    def step0():
        meet((zh, zl, to_x, to_y, to_c))
        wz().start()
        for n in range(2):
            load(n).start()
        for n in range(3):
            own(n).start()
        for p in range(PIECES):
            g2(p).start()

    def step1():
        g1(0).start()
        for n in range(2):
            load(n).wait()
            keep(n).start()
        for n in range(2):
            own(n).wait_recv()
        for n in range(2):
            diag(0, n).start()
            sib(0, n).start()

    def step2():
        g1(1).start()
        for n in range(2):
            diag(0, n).wait_recv()
        sib(0, 2).start()

    def step3():
        g1(2).start()
        wz().wait_recv()
        for n in range(3):
            got(n).start()

    def step4():
        g1(3).start()

    def step5():
        for n in range(2):
            got(n).wait_recv()
        for n in range(2):
            diag(1, n).start()
            sib(1, n).start()

    def step6():
        for n in range(2):
            diag(1, n).wait_recv()
        sib(1, 2).start()
        onward(0)

    def step8():
        onward(1)

    def step10():
        onward(2)

    def step12():
        onward(3)

    acts = {
        0: step0, 1: step1, 2: step2, 3: step3, 4: step4, 5: step5, 6: step6, 8: step8, 10: step10, 12: step12,
    }
    for at, act in acts.items():
        pl.when(step == at)(act)

    @pl.when(step < groups)
    def _():
        part = hid_ref.at[:, pl.ds(pl.multiple_of(step * GROUP, GROUP), GROUP)]
        scan_kernel(*ins, gate_ref, xr_ref, y_ref, part, sq_ref, st_ref, state)

    def swap_sums():
        return copy(29, sums, other, zl)

    @pl.when(step == groups)
    def _():
        sums[...] = jnp.zeros_like(sums)
        sums[0:1, :] = jnp.sum(jnp.transpose(sq_ref[...]), axis=0, keepdims=True)
        swap_sums().start()
        keep(1).wait()
        for move in [own(2), got(2)] + [sib(b, n) for b in range(2) for n in range(3)]:
            move.wait_recv()
        load_rows(0, 0).start()
        swap_sums().wait()
        root = lax.rsqrt((sums[0:1, :] + other[0:1, :]) / (2 * channels) + EPS)
        ir_ref[...] = jnp.transpose(jnp.broadcast_to(root, (128, length)))
        for n in range(groups):
            part = slice(n * GROUP, (n + 1) * GROUP)
            value = hid_ref[:, part].astype(F32) * twice(ir_ref[...]) * gains_ref[6:7, part]
            hid_ref[:, part] = value.astype(BF16)

    @pl.when(step >= groups)
    def _():
        n = step - groups
        slot = lax.rem(n, 2)
        load_rows(n, slot).wait()

        @pl.when(step < 2 * groups - 1)
        def _():
            load_rows(n + 1, 1 - slot).start()

        half = channels // 2
        out = dot_nt(hid_ref[:, 0:half], rows_v[slot, 0]) + dot_nt(hid_ref[:, half:], rows_v[slot, 1])
        po_ref[0] = out.astype(BF16)

    @pl.when(step == 2 * groups - 1)
    def _():
        late = [g2(p) for p in range(PIECES)] + [g3(p) for p in range(PIECES)]
        for move in late:
            move.wait_recv()
        keep(0).wait()
        sent = [g1(p) for p in range(PIECES)] + late + [wz()]
        sent += [own(n) for n in range(3)] + [got(n) for n in range(3)]
        sent += [diag(b, n) for b in range(2) for n in range(2)]
        sent += [sib(b, n) for b in range(2) for n in range(3)]
        for move in sent:
            move.wait_send()


def scan_all(cot, out_proj, nb, wg, wx, chan, *rest):
    length, width = nb.shape
    channels = chan.shape[1]
    cb = channels // 2
    feat, shard = width // 4, out_proj.shape[0]
    groups = channels // GROUP
    per = feat // 256
    assert groups == 8 and width // 256 == groups
    in_specs, out_specs = scan_specs(length, width, cb // GROUP)
    out_specs[3] = once((length, channels))
    anywhere = pl.BlockSpec(memory_space=pl.ANY)
    shapes = scan_shapes(length, channels)

    def strip(g):
        n = jnp.maximum(g - groups, 0)
        return n // per, 0, n % per

    return pl.pallas_call(
        scan_all_kernel,
        grid=(2 * groups,),
        in_specs=[anywhere] * 2 + [once((8, channels))] + in_specs,
        out_specs=out_specs
        + [pl.BlockSpec((1, length, 256), strip), once((length, 128)), anywhere, anywhere],
        out_shape=shapes
        + (
            jax.ShapeDtypeStruct((4, length, feat), BF16),
            jax.ShapeDtypeStruct((length, 128), F32),
            jax.ShapeDtypeStruct((length, width), BF16),
            jax.ShapeDtypeStruct((2, width, cb), BF16),
        ),
        scratch_shapes=[
            pltpu.VMEM((STATE, GROUP), F32),
            pltpu.VMEM((length, feat), BF16),
            pltpu.VMEM((shard, cb), BF16),
            pltpu.VMEM((2, 2, 256, cb), BF16),
            pltpu.VMEM((8, length), F32),
            pltpu.VMEM((8, length), F32),
            pltpu.SemaphoreType.DMA((SCAN_COPIES,)),
            pltpu.SemaphoreType.DMA((SCAN_COPIES,)),
            pltpu.SemaphoreType.DMA((4,)),
            pltpu.SemaphoreType.DMA((2,)),
        ],
        compiler_params=pltpu.CompilerParams(
            collective_id=2, has_side_effects=True, vmem_limit_bytes=VMEM_LIMIT
        ),
        name="scan_all",
    )(cot, out_proj, chan, nb, wg, wx, chan, *rest)


EARLY = 640


def mid_kernel(
    cf_ref, wc_ref, hid_ref, ir_ref, po_ref,
    dh_ref, go_ref, coef_ref, sum_out,
    ct, dots, sums, other, send, recv,
):
    phase, g = pl.program_id(0), pl.program_id(1)
    last = pl.num_programs(1) - 1
    length, channels = hid_ref.shape
    shard = go_ref.shape[1]
    h, l = lax.axis_index("zh"), lax.axis_index("zl")
    to, zd = {"zl": 1 - l}, {"zh": 1 - h, "zl": 1 - l}
    copy = table(send, recv)
    at = pl.ds(pl.multiple_of(g * GROUP, GROUP), GROUP)

    def part():
        return copy(1, po_ref.at[2 * (1 - h) + 1 - l, pl.ds(0, EARLY)], sum_out, zd)

    @pl.when((phase == 0) & (g == 0))
    def _():
        meet((to, zd))
        part().start()
        dots[...] = jnp.zeros_like(dots)

    @pl.when(phase == 0)
    def _():
        dh = dot_nn(cf_ref[...], wc_ref[...])
        dh_ref[...] = dh.astype(BF16)
        term = dh * hid_ref[:, at].astype(F32)
        dots[...] += term[:, 0:128] + term[:, 128:256]
        ct[at, :] = turned(cf_ref[:, at])

    @pl.when((phase == 0) & (g == last))
    def _():
        sums[...] = jnp.zeros_like(sums)
        sums[0:1, :] = jnp.sum(jnp.transpose(dots[...]), axis=0, keepdims=True)
        move = copy(0, sums, other, to)
        move.start()
        move.wait()
        both = jnp.broadcast_to(sums[0:1, :] + other[0:1, :], (128, length))
        coef_ref[...] = jnp.transpose(both) * ir_ref[...] * ir_ref[...] / (2 * channels)

    @pl.when(phase == 1)
    def _():
        right = hid_ref[:, at]
        for n in range(go_ref.shape[0] // 4):
            value = dot_nn(ct[4 * n * shard : 4 * (n + 1) * shard, :], right).astype(BF16)
            for m in range(4):
                go_ref[4 * n + m] = value[m * shard : (m + 1) * shard]

    @pl.when((phase == 1) & (g == last))
    def _():
        part().wait()


def middle(cf, wo, hid, ir, po):
    length, width = cf.shape
    channels = hid.shape[1]
    gb = channels // 2 // GROUP
    n = channels // GROUP
    shard = width // 8
    assert n == width // 256

    def const(shape):
        return pl.BlockSpec(shape, lambda p, g: (0,) * len(shape), pipeline_mode=pl.Buffered(1))

    def first(p, g):
        return jnp.where(p == 0, g, n - 1)

    return pl.pallas_call(
        mid_kernel,
        grid=(2, n),
        in_specs=[
            const((length, width)),
            pl.BlockSpec((None, width, GROUP), lambda p, g: (first(p, g) // gb, 0, first(p, g) % gb)),
            const((length, channels)),
            const((length, 128)),
            pl.BlockSpec(memory_space=pl.ANY),
        ],
        out_specs=[
            pl.BlockSpec((length, GROUP), lambda p, g: (0, first(p, g))),
            pl.BlockSpec((8, shard, GROUP), lambda p, g: (0, 0, g * p)),
            const((length, 128)),
            pl.BlockSpec(memory_space=pl.ANY),
        ],
        out_shape=(
            jax.ShapeDtypeStruct((length, channels), BF16),
            jax.ShapeDtypeStruct((8, shard, channels), BF16),
            jax.ShapeDtypeStruct((length, 128), F32),
            jax.ShapeDtypeStruct((EARLY, po.shape[2]), BF16),
        ),
        scratch_shapes=[
            pltpu.VMEM((width, length), BF16),
            pltpu.VMEM((length, 128), F32),
            pltpu.VMEM((8, length), F32),
            pltpu.VMEM((8, length), F32),
            pltpu.SemaphoreType.DMA((2,)),
            pltpu.SemaphoreType.DMA((2,)),
        ],
        compiler_params=pltpu.CompilerParams(
            collective_id=3, has_side_effects=True, vmem_limit_bytes=VMEM_LIMIT
        ),
        name="middle",
    )(cf, wo, hid, ir, po)


SHIP_COPIES = 24


def scan_grad_all_kernel(*refs):
    (go_ref, po_ref, nt_ref), refs = refs[0:3], refs[3:]
    ins, refs = refs[0:20], refs[20:]
    outs, refs = refs[0:6], refs[6:]
    own_out, got_out, raw_out, gate_out, sum0, sum1, sum2 = refs[0:7]
    scratch, refs = refs[7:15], refs[15:]
    gm, gr, gf, gfr, gs, gsr, tm, ts, tr, tf, tfr, tg, tgr, send, recv, local = refs
    h, l, _, c, x, y, rx, ry, rc = places()
    zh, zl, zd = {"zh": 1 - h}, {"zl": 1 - l}, {"zh": 1 - h, "zl": 1 - l}
    to_x, to_y, to_c = {"row": rx}, {"row": ry}, {"row": rc}
    shard, cb = own_out.shape
    copy = table(send, recv)
    step = pl.program_id(0)
    groups = pl.num_programs(0)
    first, second = (to_x, to_y), (to_y, to_x)
    mine, along = (x, y), (y, x)
    dgate_ref = outs[0]

    def near(b, j):
        lanes = slice(b * cb, (b + 1) * cb)
        return pltpu.make_async_copy(go_ref.at[2 * j + c, :, lanes], gm.at[b, j], local.at[4 * b + j])

    def core(b, j):
        lanes = slice(b * cb, (b + 1) * cb)
        return copy(4 * b + j, go_ref.at[2 * j + 1 - c, :, lanes], gr.at[b, j], to_c)

    def hop1(b):
        return copy(8 + b, gf.at[b], gfr.at[b], first[b])

    def hop2(b):
        return copy(10 + b, gs.at[b], gsr.at[b], second[b])

    def out_sums():
        late = pl.ds(EARLY, po_ref.shape[1] - EARLY)
        return [
            copy(12, po_ref.at[2 * h + 1 - l], sum0, zl),
            copy(13, po_ref.at[2 * (1 - h) + l], sum1, zh),
            copy(14, po_ref.at[2 * (1 - h) + 1 - l, late], sum2, zd),
        ]

    def gate_core():
        return copy(15, ts, tr, to_c)

    def gate_hop1():
        return copy(16, tf, tfr, to_y)

    def gate_hop2():
        return copy(17, tg, tgr, to_x)

    def spot(b, at_first, at_second):
        return 2 * at_first + at_second if b else 2 * at_second + at_first

    def add(a, b):
        return a.astype(F32) + b.astype(F32)

    @pl.when(step == 0)
    def _():
        meet((zh, zl, zd, to_x, to_y, to_c))
        for b in range(2):
            for j in range(4):
                core(b, j).start()
                near(b, j).start()
        for move in out_sums():
            move.start()

    @pl.when(step == 2)
    def _():
        for b in range(2):
            for j in range(4):
                near(b, j).wait()
                core(b, j).wait_recv()
            for s in range(2):
                j = spot(b, 1 - mine[b], s)
                gf[b, s] = add(gm[b, j], gr[b, j]).astype(BF16)
            hop1(b).start()
            for s in range(2):
                j = spot(b, mine[b], s)
                gm[b, j] = add(gm[b, j], gr[b, j]).astype(BF16)

    @pl.when(step == 5)
    def _():
        for b in range(2):
            hop1(b).wait_recv()
            far = 1 - along[b]
            gs[b] = add(gm[b, spot(b, mine[b], far)], gfr[b, far]).astype(BF16)
            hop2(b).start()
        gate_core().wait_recv()
        for n in range(2):
            tf[n] = add(tm[spot(1, 1 - y, n)], tr[spot(1, 1 - y, n)]).astype(BF16)
        gate_hop1().start()
        for n in range(2):
            tm[spot(1, y, n)] = add(tm[spot(1, y, n)], tr[spot(1, y, n)]).astype(BF16)

    @pl.when(step == groups - 1)
    def _():
        gate_hop1().wait_recv()
        tg[...] = add(tm[spot(1, y, 1 - x)], tfr[1 - x]).astype(BF16)
        gate_hop2().start()

    scan_grad_kernel(lax.rem(step + groups // 2, groups), *ins, *outs, *scratch)

    def products(other, own):
        for side, ref in ((1 - c, other), (c, own)):
            value = dot_nn(nt_ref[side], dgate_ref[...]).astype(BF16)
            for j in range(4):
                ref[j] = value[j * shard : (j + 1) * shard]

    @pl.when(step < groups // 2)
    def _():
        lanes = pl.ds(pl.multiple_of(step * GROUP, GROUP), GROUP)
        products(ts.at[:, :, lanes], tm.at[:, :, lanes])

    @pl.when(step == groups // 2 - 1)
    def _():
        gate_core().start()

    @pl.when(step >= groups // 2)
    def _():
        products(raw_out.at[0], raw_out.at[1])

    @pl.when(step == groups - 1)
    def _():
        for b, out in enumerate((own_out, got_out)):
            hop2(b).wait_recv()
            own = along[b]
            total = add(gm[b, spot(b, mine[b], own)], gfr[b, own]) + gsr[b].astype(F32)
            out[...] = total.astype(out.dtype)
        gate_hop2().wait_recv()
        total = add(tm[spot(1, y, x)], tfr[x]) + tgr[...].astype(F32)
        gate_out[...] = total.astype(BF16)
        for b in range(2):
            for j in range(4):
                core(b, j).wait_send()
            hop1(b).wait_send()
            hop2(b).wait_send()
        for move in (gate_core(), gate_hop1(), gate_hop2()):
            move.wait_send()
        for move in out_sums():
            move.wait()


def scan_grad_all(go, po, nt, *args):
    length, channels = args[0].shape
    groups = channels // GROUP
    ins, outs, shapes, scratch = scan_grad_specs(length, channels, groups // 2)
    _, shard, _ = go.shape
    feat = po.shape[2]
    cb = channels // 2
    anywhere = pl.BlockSpec(memory_space=pl.ANY)
    V = pltpu.VMEM
    return pl.pallas_call(
        scan_grad_all_kernel,
        grid=(groups,),
        in_specs=[anywhere, anywhere, once(nt.shape)] + ins,
        out_specs=outs
        + [
            once((shard, cb)),
            once((shard, cb)),
            pl.BlockSpec((2, 4, shard, GROUP), lambda g: (0, 0, 0, jnp.maximum(g - groups // 2, 0))),
            once((shard, cb)),
            anywhere,
            anywhere,
            anywhere,
        ],
        out_shape=shapes
        + (
            jax.ShapeDtypeStruct((shard, cb), F32),
            jax.ShapeDtypeStruct((shard, cb), BF16),
            jax.ShapeDtypeStruct((2, 4, shard, cb), BF16),
            jax.ShapeDtypeStruct((shard, cb), BF16),
            jax.ShapeDtypeStruct((length, feat), BF16),
            jax.ShapeDtypeStruct((length, feat), BF16),
            jax.ShapeDtypeStruct((length - EARLY, feat), BF16),
        ),
        scratch_shapes=scratch
        + [
            V((2, 4, shard, cb), BF16),
            V((2, 4, shard, cb), BF16),
            V((2, 2, shard, cb), BF16),
            V((2, 2, shard, cb), BF16),
            V((2, shard, cb), BF16),
            V((2, shard, cb), BF16),
            V((4, shard, cb), BF16),
            V((4, shard, cb), BF16),
            V((4, shard, cb), BF16),
            V((2, shard, cb), BF16),
            V((2, shard, cb), BF16),
            V((shard, cb), BF16),
            V((shard, cb), BF16),
            pltpu.SemaphoreType.DMA((SHIP_COPIES,)),
            pltpu.SemaphoreType.DMA((SHIP_COPIES,)),
            pltpu.SemaphoreType.DMA((8,)),
        ],
        compiler_params=pltpu.CompilerParams(
            collective_id=4, has_side_effects=True, vmem_limit_bytes=VMEM_LIMIT
        ),
        name="scan_grad_all",
    )(go, po, nt, *args)


def build(nrow, nl):
    direct = nrow == 8 and nl == 2
    col = ("zh", "zl")

    def swap(v):
        return lax.ppermute(v, "zh", [(0, 1), (1, 0)])

    def pair_sum(v):
        return lax.psum(v, "zl")

    def row_gather(v):
        return lax.all_gather(v, "row", axis=0, tiled=True)

    def row_scatter(v):
        return lax.psum_scatter(v, "row", scatter_dimension=0, tiled=True)

    def per_device(
        tokens, segment_ids, norm_gain, in_zx, in_dt, in_bc, conv_x, conv_x_bias, conv_bc,
        conv_bc_bias, dt_bias, a_log, d_skip, inner_gain, out_proj, cotangent,
    ):
        seq_count, length = segment_ids.shape
        assert seq_count == 2
        feat = tokens.shape[1]
        width = feat * 2 * nl
        cb = inner_gain.shape[0]
        hb = dt_bias.shape[0]
        inner = cb * 2 * nl
        blocks = length // SPAN
        gb = cb // GROUP
        mh = lax.axis_index("zh")
        ml = lax.axis_index("zl")
        first_h = mh == 0
        here = mh * nl + ml
        bcn = conv_bc.shape[1]

        def mine(v, axis=0):
            return lax.dynamic_index_in_dim(v, mh, axis, keepdims=False)

        def other(v, axis=0):
            return lax.dynamic_index_in_dim(v, 1 - mh, axis, keepdims=False)

        def seqs(v):
            return v.reshape(2, length, feat)

        def by_seq(own, away):
            return jnp.where(first_h, jnp.stack([own, away]), jnp.stack([away, own]))

        def gather_features(v):
            own, away = mine(seqs(v)), other(seqs(v))
            both = by_seq(own, swap(away))
            every = jnp.moveaxis(lax.all_gather(both, "zl"), 0, 1)
            return jnp.transpose(every, (2, 0, 1, 3)).reshape(length, width)

        def scatter_features(v):
            parts = v.reshape(length, 2, nl, feat)
            both = lax.psum_scatter(parts, "zl", scatter_dimension=2, tiled=False)
            return by_seq(mine(both, 1), swap(other(both, 1))).astype(F32)

        chan = jnp.concatenate(
            [
                conv_x,
                conv_x_bias[None],
                jnp.repeat(d_skip, HEADDIM)[None],
                inner_gain[None],
                jnp.pad(jnp.concatenate([dt_bias, a_log]), (0, cb - 2 * hb))[None],
            ],
            axis=0,
        )
        thin = jnp.concatenate([in_bc, in_dt], axis=1)
        bc_rows = jnp.concatenate([conv_bc, conv_bc_bias[None]], axis=0)
        seg = mine(segment_ids)
        segc = jnp.broadcast_to(seg[:, None], (length, 128))
        segr = jnp.broadcast_to(seg[None, :], (8, length))
        if direct:
            extra = jnp.zeros((8, cb), F32)
            extra = lax.dynamic_update_slice(extra, norm_gain[None], (0, 0))
            extra = lax.dynamic_update_slice(extra, bc_rows, (1, here * bcn))
            extra = lax.dynamic_update_slice(extra, jnp.stack([dt_bias, a_log]), (6, 0))
            thin = jnp.pad(thin, ((0, 0), (0, 128 - thin.shape[1])))
            (
                normed, normed_t, inv_root, par, w_small, small, hp, bcp,
                bc, bct, gmat, gtmat, colp, cumt, kexp, lag, w_gate, w_x,
            ) = gather_all(
                seqs(tokens), in_zx[:, 0], in_zx[:, 1], thin, jnp.concatenate([chan, extra], axis=0),
                segc, segr, 2 * gb,
            )
            chan_got = lax.dynamic_index_in_dim(par, (1 - mh) * nl + ml, 0, keepdims=False)[0:8]
            gain = par[:, 8, :feat].reshape(width)
        else:
            chan_got = swap(chan)
            packed = jnp.concatenate([norm_gain, bc_rows.reshape(-1)])
            packs = lax.all_gather(packed, col)
            gain = packs[:, :feat].reshape(width)
            bc_all = jnp.moveaxis(packs[:, feat:].reshape(-1, KW + 1, bcn), 0, 1)
            bcp = jnp.pad(bc_all.reshape(KW + 1, 2 * STATE), ((0, 7 - KW), (0, 0)))
            hp = jnp.concatenate([c[7, : 2 * hb].reshape(2, hb) for c in (chan, chan_got)], axis=1)
            hp = jnp.pad(hp, ((0, 6), (0, 128 - 2 * hb)))
            thin = lax.all_gather(thin, ("row", "zh", "zl")).reshape(nrow, 2, nl, -1, bcn + hb)
            thin = jnp.moveaxis(thin, 3, 1).reshape(width, 2, nl, bcn + hb)
            w_gate = jnp.stack([row_gather(w) for w in (in_zx[:, 0], swap(in_zx[:, 0]))])
            w_x = jnp.stack([row_gather(w) for w in (in_zx[:, 1], swap(in_zx[:, 1]))])
            w_bc = thin[..., :bcn].reshape(width, 2 * STATE)
            w_dt = lax.dynamic_index_in_dim(thin[..., bcn:], ml, 2, keepdims=False)
            w_small = jnp.concatenate([w_bc, mine(w_dt, 1), other(w_dt, 1)], axis=1)
            w_small = jnp.pad(w_small, ((0, 0), (0, 384 - w_small.shape[1])))
            x32 = gather_features(tokens).astype(F32)
            inv_root = lax.rsqrt(jnp.mean(x32 * x32, axis=1, keepdims=True) + EPS)
            normed = (x32 * inv_root * gain).astype(BF16)
            small = dot_nn(normed, w_small)
            bc, bct, gmat, gtmat, colp, cumt, kexp, lag = prep(small, segc, segr, bcp, hp, 2 * gb)
        chans = jnp.concatenate([chan, chan_got], axis=1)
        kexp = jnp.repeat(kexp[:, : 2 * hb], HEADDIM, axis=1)

        seq_args = (lag, bc, bct, gmat, colp, cumt, kexp)
        gain_in = chans[6]
        if direct:
            gates, xrs, ys, hidden, _, sts, partial_out, ir, c_full, w_out = scan_all(
                seqs(cotangent), out_proj, normed, w_gate, w_x, chans, *seq_args
            )
            dh, g_out, cf, sum3 = middle(c_full, w_out, hidden, ir, partial_out)
        else:
            w_out = [row_gather(w) for w in (out_proj, swap(out_proj))]
            c_full = gather_features(cotangent)
            gates, xrs, ys, gateds, sq, sts = scan(normed, w_gate, w_x, chans, *seq_args)
            dh = jnp.concatenate([dot_nn(c_full, w).astype(BF16) for w in w_out], axis=1)
            gate_sq = pair_sum(jnp.sum(sq, axis=1))
            inner_root = lax.rsqrt(gate_sq / inner + EPS)[:, None]
            gate_dot = jnp.sum(dh.astype(F32) * gateds.astype(F32) * gain_in, axis=1)
            gate_dot = pair_sum(gate_dot)[:, None]
            hidden = (gateds.astype(F32) * inner_root * gain_in).astype(BF16)
            partial_out = dot_nt(hidden[:, :cb], w_out[0]) + dot_nt(hidden[:, cb:], w_out[1])
            partial_out = partial_out.astype(BF16)
            ir = jnp.broadcast_to(inner_root, (length, 128))
            cf = jnp.broadcast_to(inner_root**3 / inner * gate_dot, (length, 128))
            g_out = [dot_tn(c_full, hidden[:, :cb]), dot_tn(c_full, hidden[:, cb:])]
            g_out = [row_scatter(g.astype(BF16)) for g in g_out]
            g_wout = g_out[0].astype(F32) + swap(g_out[1]).astype(F32)
            out_here = scatter_features(partial_out)

        grad_args = (
            gates, xrs, ys, dh, chans, lag, ir, cf, bc, bct, gtmat, colp, cumt, kexp, sts, segc, segr,
            small, hp, bcp,
        )
        if direct:
            (
                dgates, dxrs, chg, nd, d_small, pg, g_own, g_got, gate_own, gate_got, sum0, sum1, sum2,
            ) = scan_grad_all(g_out, partial_out, normed_t, *grad_args)
            g_wout = g_own + swap(g_got).astype(F32)
            own = lax.dynamic_index_in_dim(partial_out, here, 0, keepdims=False)
            away = sum1.astype(F32) + jnp.concatenate([sum3, sum2], axis=0).astype(F32)
            out_here = by_seq(own.astype(F32) + sum0.astype(F32), away)
        else:
            dgates, dxrs, chg, nd, d_small, pg = scan_grad(*grad_args)
        output = (out_here + seqs(tokens)).astype(BF16).reshape(tokens.shape)
        g_dtb, g_alog = pg[5, : 2 * hb], pg[6, : 2 * hb]
        g_bcs = pg[: KW + 1]
        dn, gg = back(dgates, dxrs, d_small, w_gate, w_x, w_small, normed)
        g_gain = gg[0] / gain

        if direct:
            rows = []
            for b in range(2):
                hs = slice(b * hb, (b + 1) * hb)
                heads = jnp.concatenate([g_dtb[hs], g_alog[hs]])
                rows += [chg[0:7, b * cb : (b + 1) * cb], jnp.pad(heads, (0, cb - 2 * hb))[None]]
            last = jnp.concatenate([g_gain, g_bcs.reshape(-1)])
            last = jnp.pad(last, (0, 8 * cb - last.shape[0])).reshape(8, cb)
            gz, thins, smalls, d_own, d_away, rowv = grad_all(
                dn, gate_own, normed_t, dxrs, d_small, jnp.concatenate(rows + [last], axis=0), nd, inv_root,
                gate_got,
            )
            d_here = by_seq(d_own, d_away.astype(F32))
            roots = by_seq(rowv[0, 1], rowv[1, 1])
            dots = by_seq(rowv[0, 0] + rowv[2, 0], rowv[1, 0] + rowv[3, 0])
            g_zx = jnp.transpose(gz, (1, 0, 2))
            g_bc = lax.dynamic_slice(thins, (0, ml * bcn), (thins.shape[0], bcn))
            g_dt = thins[:, 128 : 128 + hb] + thins[:, 256 + hb : 256 + 2 * hb]
            chg = smalls[0, 0:8] + smalls[1, 8:16]
            last = smalls[:, 16:].sum(0).reshape(-1)
            g_gain = lax.dynamic_slice(last, (here * feat,), (feat,))
            g_bcs = last[width : width + (KW + 1) * 2 * STATE].reshape(KW + 1, 2 * nl, bcn)
            g_bcs = lax.dynamic_index_in_dim(g_bcs, here, 1, keepdims=False)
            g_dtb, g_alog = chg[7, :hb], chg[7, hb : 2 * hb]
        else:
            d_here = scatter_features(jnp.moveaxis(dn, 0, 1).reshape(length, width))
            dots = pair_sum(jnp.sum(nd, axis=1))
            dots = by_seq(dots, swap(dots))
            roots = by_seq(inv_root[:, 0], swap(inv_root[:, 0]))

            def join(own, away):
                return own.astype(F32) + swap(away).astype(F32)

            halves = (slice(0, cb), slice(cb, 2 * cb))
            g_gate = [row_scatter(dot_tn(normed, dgates[:, n]).astype(BF16)) for n in halves]
            g_x = [row_scatter(dot_tn(normed, dxrs[:, n]).astype(BF16)) for n in halves]
            g_zx = jnp.stack([join(*g_gate), join(*g_x)], axis=1)
            thins = row_scatter(dot_tn(normed, d_small))
            g_bc = lax.psum(thins[:, : 2 * STATE], col).reshape(-1, 2 * nl, bcn)
            g_bc = lax.dynamic_index_in_dim(g_bc, here, 1, keepdims=False)
            g_dts = thins[:, 2 * STATE : 2 * STATE + 2 * hb].reshape(-1, 2, hb)
            g_dt = g_dts[:, 0] + swap(g_dts[:, 1])
            every = ("row", "zh", "zl")
            g_gain, g_bcs = lax.psum((g_gain, g_bcs), every)
            g_gain = lax.dynamic_slice(g_gain, (here * feat,), (feat,))
            g_bcs = g_bcs.reshape(KW + 1, 2 * nl, bcn)
            g_bcs = lax.dynamic_index_in_dim(g_bcs, here, 1, keepdims=False)
            chg = chg[:, :cb] + swap(chg[:, cb:])
            g_dtb = g_dtb[:hb] + swap(g_dtb[hb:])
            g_alog = g_alog[:hb] + swap(g_alog[hb:])
            chg, g_dtb, g_alog = lax.psum((chg, g_dtb, g_alog), "row")
        roots, dots = roots[..., None], dots[..., None]
        x32 = seqs(tokens).astype(F32)
        tokens_grad = seqs(cotangent) + roots * norm_gain * d_here - x32 * (roots * roots / width * dots)
        tokens_grad = tokens_grad.astype(BF16).reshape(tokens.shape)
        return (
            output,
            tokens_grad,
            g_gain,
            g_zx,
            g_dt,
            g_bc,
            chg[0:KW],
            chg[4],
            g_bcs[0:KW],
            g_bcs[KW],
            g_dtb,
            g_alog,
            chg[5].reshape(hb, HEADDIM).sum(1),
            chg[6],
            g_wout,
        )

    return per_device


def solution(mesh):
    nrow, ncol = mesh.shape["row"], mesh.shape["col"]
    nl = ncol // 2
    split = Mesh(mesh.devices.reshape(nrow, 2, nl), ("row", "zh", "zl"))
    col = ("zh", "zl")
    in_specs = (
        P("row", col), P("row", None), P(col), P("row", None, col), P("row", col), P("row", col),
        P(None, col), P(col), P(None, col), P(col), P(col), P(col), P(col), P(col),
        P("row", col), P("row", col),
    )
    out_specs = (
        P("row", col), P("row", col), P(col), P("row", None, col), P("row", col), P("row", col),
        P(None, col), P(col), P(None, col), P(col), P(col), P(col), P(col), P(col), P("row", col),
    )
    return jax.shard_map(
        build(nrow, nl), mesh=split, in_specs=in_specs, out_specs=out_specs, check_vma=False
    )
```

time: 915 us -> 604 us (0.66)
  waiting for transfers between devices: 200 us -> 0.01 us
  matrix products: 93.4 us -> 0 us
  Pallas kernels: 460 us -> 534 us
  starting transfers between devices: 35.9 us -> 1.4 us
  local copies, waits for them, and re-layouts: 63 us -> 34.8 us
  other arithmetic: 40 us -> 21.6 us
  between operations: 15.1 us -> 1.39 us
    ppermute x6 -> x1, waiting for transfers between devices: 134 us -> 0.01 us  [swap(): return lax.ppermute(v, 'zh', [(0, 1), (1, 0)])]
    dot_general x12 -> x0, matrix products: 93.4 us -> none  [the longest x7 56.7 us: dot_nn(): lax.dot_general(a, b, (((1,), (0,)), ((), ())), preferred_element_type=F32)]
    pallas_call x8 -> x6, Pallas kernels: 460 us -> 534 us  [the longest x1 133 us: gather_all(): pl.pallas_call(gather_kernel, in_specs=[anywhere] * 5 + [inside] * 2, out...]
    ppermute x9 -> x0, waiting for transfers between devices: 66.5 us -> none  [the longest x6 66.5 us: swap_zl(): return lax.ppermute(v, col, [(0, 1), (1, 0), (2, 3), (3, 2)])]
    ppermute x6 -> x1, starting transfers between devices: 27.1 us -> 1.4 us  [swap(): return lax.ppermute(v, 'zh', [(0, 1), (1, 0)])]
    reduce_sum x8 -> x0, other arithmetic: 9.47 us -> none  [the longest x1 4.28 us: shifted_silu(): v = v + taps[KW - 1 - j] * jnp.where(lag[:, None] >= j, earlier, 0.0)]
  transfers between devices with their start and end apart: 19 -> 1, of which waited for: 7 -> 0; matrix products, arithmetic and copies ran while one was open for 19% -> 5% of each run, Pallas kernels for 35% -> 26%
where the time goes in v3:
time: 604 us; the launch traced here: 593 us
  Pallas kernels  534 us (88%)
  local copies, waits for them, and re-layouts  34.8 us (6%)
  other arithmetic  21.6 us (4%)
    pallas_call x1, Pallas kernels, gather_all(): pl.pallas_call(gather_kernel, in_specs=[anywhere] * 5 + [inside] * 2, out...  133 us
    pallas_call x1, Pallas kernels, grad_all(): pl.pallas_call(grad_kernel, in_specs=[anywhere] * 2 + [inside] * 6 + [any...  124 us
    pallas_call x1, Pallas kernels, scan_grad_all(): pl.pallas_call(scan_grad_all_kernel, grid=(groups,), in_specs=[anywhere,...  112 us
    pallas_call x1, Pallas kernels, scan_all(): pl.pallas_call(scan_all_kernel, grid=(2 * groups,), in_specs=[anywhere] *...  100 us
    pallas_call x1, Pallas kernels, middle(): pl.pallas_call(mid_kernel, grid=(2, n), in_specs=[const((length, width)),...  37.7 us
    pallas_call x1, Pallas kernels, back(): pl.pallas_call(back_kernel, grid=(width // 256,), in_specs=[once(a.shape)...  27.9 us
  transfers between devices with their start and end apart: 1, of which 0 were waited for; matrix products, arithmetic and copies ran while one was open for 5% of the time, Pallas kernels for 26%

profile of v3, /device:TPU:0, one launch (start us, length us, event | category | flops | bytes accessed | tf_op | source)
XLA Modules:
  0.0 593.4 jit_solution(11055435166808359635)
XLA Ops:
  5.7 2.0 concatenate.54.par_ref
  9.4 3.4 fusion.9
  13.6 1.3 copy_bitcast_fusion
  15.6 1.0 broadcast_in_dim.52.segc_ref.refs_18_
  16.5 132.9 %gather_all.1 = (bf16[1024,2048]{1,0:T(8,128)(2,1)}, bf16[2,1024,1024]{2,1,0:T(8,128)(2,1)}, f32[1024,128]{1,0:T(8,128)}, f32[4,16,1024]{2,1,0:T(8,128)}, bf16[2...) custom-call(bf16[2,1024,512]{2,1,0:T(8,128)(2,1)} %bitcast.78, ...), custom_call_target="tpu_custom_call" | custom-call | tf_op jit(solution)/shard_map/gather_all/pallas_call | solution.py:806
  152.4 100.5 %scan_all.1 = (f32[1024,2048]{1,0:T(8,128)}, f32[1024,2048]{1,0:T(8,128)}, f32[1024,2048]{1,0:T(8,128)}, bf16[1024,2048]{1,0:T(8,128)(2,1)}, f32[1024,128]{1,0:T...) custom-call(bf16[2,1024,512]{2,1,0:T(8,128)(2,1)} %bitcast.77, ...), custom_call_target="tpu_custom_call" | custom-call | tf_op jit(solution)/shard_map/scan_all/pallas_call | solution.py:1326
  252.9 37.7 %middle.1 = (bf16[1024,2048]{1,0:T(8,128)(2,1)}, bf16[8,256,2048]{2,1,0:T(8,128)(2,1)}, f32[1024,128]{1,0:T(8,128)}, bf16[640,512]{1,0:T(8,128)(2,1)}) custom-call(bf16[1024,2048]{1,0:T(8,128)(2,1)} %get-tuple-element.79.cf_ref, bf16[2,2048,1024]{2,1,0:T(8,128)(2,1)} %get-tuple-element.80.wc_ref, bf16[1024,2048]{1,0:T(8,128)(2,1)} %get-tuple-element.81.hid_ref, ...), custom_call_target="tpu_custom_call" | custom-call | tf_op jit(solution)/shard_map/middle/pallas_call | solution.py:1429
  290.5 111.7 %scan_grad_all.1 = (bf16[1024,2048]{1,0:T(8,128)(2,1)}, bf16[1024,2048]{1,0:T(8,128)(2,1)}, f32[8,2048]{1,0:T(8,128)}, f32[1024,128]{1,0:T(8,128)}, bf16[1024,38...) custom-call(bf16[8,256,2048]{2,1,0:T(8,128)(2,1)} %get-tuple-element, ...), custom_call_target="tpu_custom_call" | custom-call | tf_op jit(solution)/shard_map/scan_grad_all/pallas_call | solution.py:1619
  402.3 1.4 collective-permute-start
  405.4 27.9 %back.1 = (bf16[4,1024,512]{2,1,0:T(8,128)(2,1)}, f32[8,2048]{1,0:T(8,128)}) custom-call(bf16[1024,2048]{1,0:T(8,128)(2,1)} %get-tuple-element.99.a0, bf16[1024,2048]{1,0:T(8,128)(2,1)} %get-tuple-element.100.a1.dx_ref, bf16[1024,384]{1,0:T(8,128)(2,1)} %get-tuple-element.101.a2.ds_ref, bf16[2,2048,1024]{2,1,0:T(8,128)(2,1)} %get-tuple-element.69.refs_4_.w0, ...), custom_call_target="tpu_custom_call" | custom-call | tf_op jit(solution)/shard_map/back/pallas_call | solution.py:543
  434.4 1.9 concatenate.60.small_ref
  436.2 123.6 %grad_all.1 = (f32[2,256,1024]{2,1,0:T(8,128)}, f32[256,384]{1,0:T(8,128)}, f32[4,24,1024]{2,1,0:T(8,128)}, f32[1024,512]{1,0:T(8,128)}, bf16[1024,512]{1,0:T(8,128)(2,1)}, /*index=5*/f32[4,8,1024]{2,1,0:T(8,128)}) custom-call(bf16[4,1024,512]{2,1,0:T(8,128)(2,1)} %get-tuple-element.103.dn_ref, bf16[2,4,256,1024]{3,2,1,0:T(8,128)(2,1)} %get-tuple-element.104.raw_ref, ...), custom_call_target="tpu_custom_call" | custom-call | tf_op jit(solution)/shard_map/grad_all/pallas_call | solution.py:1058
  561.6 1.4 fusion.12
  563.0 1.4 slice_bitcast_fusion.2
  566.5 1.6 fusion.4
  568.8 1.1 constant_dynamic-slice_fusion.2
  571.3 3.0 bitcast_convert_fusion
  574.2 2.9 copy.42
  577.2 1.3 dynamic_slice.25
  578.6 1.4 add_bitcast_fusion
  584.4 3.3 fusion.2
  587.7 1.2 fusion.8
  588.9 1.3 slice_bitcast_fusion.3
  590.8 2.2 convert_add_fusion.2
  (87 shorter events, 24.6 us)
Async XLA Ops:
  0.6 12.2 %copy-start = (s32[2,1024]{1,0:T(2,128)S(1)}, s32[2,1024]{1,0:T(2,128)}, u32[]{:S(2)}) copy-start(s32[2,1024]{1,0:T(2,128)} %param.17) | copy-start | bytes 24580
  402.3 188.6 %collective-permute-start = (bf16[256,1024]{1,0:T(8,128)(2,1)}, bf16[256,1024]{1,0:T(8,128)(2,1)}, u32[]{:S(2)}, u32[]{:S(2)}) collective-permute-start(bf16[256,1024]{1,0:T(8,128)(2,1)} %get-tuple-element.118), channel_id=1, source_target_pairs={{0,2},{2,0},{1,3},{3,1},{4,6},{6,4},{5,7},{7,5},{8,10},{10,8},{9,1... | collective-permute-start | bytes 1572872 | tf_op jit(solution)/shard_map/ppermute | solution.py:1674
  405.4 28.7 %copy-start.18 = (f32[8,256]{1,0:T(8,128)S(1)}, f32[8,256]{1,0:T(8,128)}, u32[]{:S(2)}) copy-start(f32[8,256]{1,0:T(8,128)} %get-tuple-element.106) | copy-start | bytes 24580
  405.4 28.8 %copy-start.14 = (f32[8,2048]{1,0:T(8,128)S(1)}, f32[8,2048]{1,0:T(8,128)}, u32[]{:S(2)}) copy-start(f32[8,2048]{1,0:T(8,128)} %get-tuple-element.105) | copy-start | bytes 196612
  436.2 130.2 %copy-start.7 = (bf16[1024,512]{1,0:T(8,128)(2,1)S(1)}, bf16[1024,512]{1,0:T(8,128)(2,1)}, u32[]{:S(2)}) copy-start(bf16[1024,512]{1,0:T(8,128)(2,1)} %get-tuple-element.95) | copy-start | bytes 3145732
  560.7 5.8 copy-start.12
  566.5 2.2 copy-start.17
  566.5 2.2 copy-start.11
  568.1 9.1 %copy-start.15 = (f32[1,1024,1]{1,2,0:T(1,128)S(1)}, f32[1,1024,1]{1,2,0:T(1,128)}, u32[]{:S(2)}) copy-start(f32[1,1024,1]{1,2,0:T(1,128)} %get-tuple-element.153) | copy-start | bytes 12292
  568.1 9.1 %copy-start.16 = (f32[1,1024,1]{1,2,0:T(1,128)S(1)}, f32[1,1024,1]{1,2,0:T(1,128)}, u32[]{:S(2)}) copy-start(f32[1,1024,1]{1,2,0:T(1,128)} %get-tuple-element.156) | copy-start | bytes 12292
  568.7 9.9 %copy-start.9 = (bf16[1024,512]{1,0:T(8,128)(2,1)S(1)}, bf16[1024,512]{1,0:T(8,128)(2,1)}, u32[]{:S(2)}) copy-start(bf16[1024,512]{1,0:T(8,128)(2,1)} %get-tuple-element.96) | copy-start | bytes 3145732
  571.3 3.0 copy-start.5
  571.3 7.3 %copy-start.10 = (bf16[384,512]{1,0:T(8,128)(2,1)S(1)}, bf16[384,512]{1,0:T(8,128)(2,1)}, u32[]{:S(2)}) copy-start(bf16[384,512]{1,0:T(8,128)(2,1)} %get-tuple-element.98) | copy-start | bytes 1179652
  580.0 1.6 copy-start.4
  580.0 2.2 copy-start.6
  582.2 1.6 copy-start.2
  582.2 2.2 copy-start.3
  582.2 2.2 copy-start.19
  584.4 5.8 copy-start.13
  584.4 6.4 %copy-start.8 = (f32[256,1024]{1,0:T(8,128)S(1)}, f32[256,1024]{1,0:T(8,128)}, u32[]{:S(2)}) copy-start(f32[256,1024]{1,0:T(8,128)} %get-tuple-element.117) | copy-start | bytes 3145732
  584.4 8.6 %copy-start.1 = (s32[2,1024]{1,0:T(2,128)S(1)}, s32[2,1024]{1,0:T(2,128)}, u32[]{:S(2)}) copy-start(s32[2,1024]{1,0:T(2,128)} %param.17) | copy-start | bytes 24580

commit v4 on v3

--- a/solution.py
+++ b/solution.py
@@ -66,54 +66,59 @@
     return ((lane >= h * HEADDIM) & (lane < (h + 1) * HEADDIM)).astype(F32).astype(BF16)
 
 
-def prep_kernel(
-    small_ref, segc_ref, segr_ref, bcp_ref, hp_ref,
-    bc_ref, bct_ref, g_ref, gt_ref, colp_ref, cumt_ref, kexp_ref, lag_ref,
-):
-    length = small_ref.shape[0]
-    blocks = length // SPAN
-    groups = colp_ref.shape[0]
+def prep_lags(segc_ref, kexp_ref, lag_ref):
     seg = segc_ref[...]
+    length = seg.shape[0]
     pos = lax.broadcasted_iota(jnp.int32, (length, 128), 0)
     lag = jnp.zeros((length, 128), F32)
     for j in range(1, KW):
         lag = lag + ((pltpu.roll(seg, j, 0) == seg) & (pos >= j)).astype(F32)
     lag_ref[0:length, :] = lag
     lag_ref[length:, :] = jnp.zeros((8, 128), F32)
-    lag2 = twice(lag)
-    raw = small_ref[:, 0:256]
+    kexp_ref[...] = jnp.zeros_like(kexp_ref)
+
+
+def prep_rows(
+    lo, hi, small_ref, segc_ref, segr_ref, bcp_ref, hp_ref,
+    bc_ref, bct_ref, g_ref, gt_ref, colp_ref, cumt_ref, kexp_ref, lag_ref,
+):
+    groups = colp_ref.shape[0]
+    some = slice(lo, hi)
+    lag2 = twice(lag_ref[some, :])
+    raw = small_ref[some, 0:256]
+    wide = raw if lo == 0 else small_ref[lo - 8 : hi, 0:256]
     v = bcp_ref[4:5, :] + bcp_ref[3:4, :] * raw
     for j in range(1, KW):
-        v = v + bcp_ref[3 - j : 4 - j, :] * jnp.where(lag2 >= j, pltpu.roll(raw, j, 0), 0.0)
-    act = v * jax.nn.sigmoid(v)
-    bc_ref[...] = act.astype(BF16)
-    bct_ref[...] = turned(act.astype(BF16))
-    z = small_ref[:, 256:384] + hp_ref[0:1, :]
+        earlier = pltpu.roll(wide, j, 0)[wide.shape[0] - (hi - lo) :]
+        v = v + bcp_ref[3 - j : 4 - j, :] * jnp.where(lag2 >= j, earlier, 0.0)
+    act = (v * jax.nn.sigmoid(v)).astype(BF16)
+    bc_ref[some, :] = act
+    bct_ref[:, some] = turned(act)
+    z = small_ref[some, 256:384] + hp_ref[0:1, :]
     dt = jnp.maximum(z, 0.0) + jnp.log1p(jnp.exp(-jnp.abs(z)))
     a = -dt * jnp.exp(hp_ref[1:2, :])
     tri_r = lax.broadcasted_iota(jnp.int32, (SPAN, SPAN), 0)
     tri_c = lax.broadcasted_iota(jnp.int32, (SPAN, SPAN), 1)
     lower = (tri_r >= tri_c).astype(F32)
     seg_row = segr_ref[0:1, :]
-    for c in range(blocks):
+    for c in range(lo // SPAN, hi // SPAN):
         r0 = c * SPAN
         rows = slice(r0, r0 + SPAN)
-        cum = dot_exact(lower, a[rows])
-        segb = seg[rows]
-        last = seg[r0 + SPAN - 1 : r0 + SPAN]
+        here = slice(r0 - lo, r0 - lo + SPAN)
+        cum = dot_exact(lower, a[here])
+        segb = segc_ref[rows, :]
+        last = segc_ref[r0 + SPAN - 1 : r0 + SPAN, :]
         tail = (segb == last).astype(F32)
         end = cum[SPAN - 1 : SPAN]
         q = jnp.exp(end - cum) * tail
         if c > 0:
-            prev = seg[r0 - 1 : r0]
+            prev = segc_ref[r0 - 1 : r0, :]
             p = jnp.exp(cum) * (segb == prev).astype(F32)
-            k = jnp.exp(end) * (last == prev).astype(F32)
+            kexp_ref[c : c + 1, :] = jnp.exp(end) * (last == prev).astype(F32)
         else:
             p = jnp.zeros_like(cum)
-            k = jnp.zeros_like(end)
-        kexp_ref[c : c + 1, :] = k
         cumt = jnp.transpose(cum)
-        dtb = dt[rows]
+        dtb = dt[here]
         for g in range(groups):
             hs = slice(PER * g, PER * g + PER)
             colp_ref[g, rows, 0:4] = cum[:, hs]
@@ -126,8 +131,11 @@
         same = across(segb) == seg_row[:, rows]
         g_ref[rows, :] = jnp.where(same & (tri_r >= tri_c), dot_nt(cc, bb), 0.0)
         gt_ref[rows, :] = jnp.where(same & (tri_r <= tri_c), dot_nt(bb, cc), 0.0)
-    if blocks < kexp_ref.shape[0]:
-        kexp_ref[blocks:, :] = jnp.zeros((kexp_ref.shape[0] - blocks, 128), F32)
+
+
+def prep_kernel(*refs):
+    prep_lags(refs[1], refs[-2], refs[-1])
+    prep_rows(0, refs[0].shape[0], *refs)
 
 
 def conv_rows(xr_ref, lag_ref, chan_ref, r0):
@@ -682,43 +690,23 @@
     def pass_x(p):
         x1[p].wait_recv()
         x3.append(start(xv.at[toks(p), cols(zhp)], xv.at[toks(p), cols(zhp)], zl))
-        send_x()
-
-    for q in range(3):
-        send_w(q)
-    x2 = start(x_ref.at[h], xv.at[:, cols(me)], zl)
-    for q in range(2):
-        deal(0, q)
-    for k in range(2):
-        keeps[3 + k].wait()
-        laid[k].start()
-    keeps[1].wait()
-    for copy in thins:
-        copy.wait_recv()
-    thin_go = [start(thin_v.at[r], thin_v.at[r], to) for to in (to_x, to_y, to_c)]
-    sib_thin.append(thin_go[2])
-    for q in range(2):
-        for n in range(2):
-            pass_on(0, q, n)
-    thin_go[0].wait_recv()
-    thin_d = start(thin_v.at[rx], thin_v.at[rx], to_y)
-    sib_thin.append(start(thin_v.at[rx], thin_v.at[rx], to_c))
-    thin_go[1].wait_recv()
-    sib_thin.append(start(thin_v.at[ry], thin_v.at[ry], to_c))
-
-    for copy in pars:
-        copy.wait_recv()
-    keeps[0].wait()
-    keeps[2].wait()
-    par_out[...] = parv[...]
-    bcp_ref[...] = jnp.zeros_like(bcp_ref)
-    bcp_ref[0:5, :] = sum(parv[b, 9:14, 0 : 2 * STATE] for b in range(4))
-    hp_ref[...] = jnp.zeros_like(hp_ref)
-    hp_ref[0:2, :] = parv[me, 14:16, 0:128] + pltpu.roll(parv[zhp, 14:16, 0:128], hb, 1)
+
+    x2 = {}
+
+    def send_own(k):
+        rows_k = pl.ds(k * 2 * step, 2 * step)
+        x2[k] = start(x_ref.at[h, rows_k], xv.at[rows_k, cols(me)], zl)
+
+    def thin_on(n):
+        row = (rx, ry, rd)[n]
+        thin_go[n].wait_recv()
+        if n == 0:
+            thin_go.append(start(thin_v.at[row], thin_v.at[row], to_y))
+        sib_thin.append(start(thin_v.at[row], thin_v.at[row], to_c))
 
     def norm(p):
-        if p == 0:
-            x2.wait_recv()
+        if p % 2 == 0:
+            x2[p // 2].wait_recv()
         x3[p].wait_recv()
         total = jnp.zeros((step, 1), F32)
         for b in range(4):
@@ -733,63 +721,111 @@
             nb_ref[toks(p), b * shard : (b + 1) * shard] = value
             nt_ref[b % 2, b // 2 * shard : (b // 2 + 1) * shard, toks(p)] = turned(value)
 
-    def narrow(p):
-        some = slice(p * (length // 2), (p + 1) * (length // 2))
-        small_ref[some, :] = dot_nn(nb_ref[some, :], ws_ref[...])
-
-    corner(0, 1)
-    deal(1, 0)
-    send_w(3)
-    deal(1, 1)
-    send_x()
-    deal(1, 2)
-    send_x()
-    thin_d.wait_recv()
-    sib_thin.append(start(thin_v.at[rd], thin_v.at[rd], to_c))
-    for copy in sib_thin:
-        copy.wait_recv()
-    ws_ref[...] = jnp.zeros_like(ws_ref)
-    for row in range(8):
-        at = slice(row * shard, (row + 1) * shard)
-        for b in range(4):
-            ws_ref[at, b * bcn : (b + 1) * bcn] = thin_v[row, b, :, 0:bcn]
-        ws_ref[at, 2 * STATE : 2 * STATE + hb] = thin_v[row, me, :, bcn : bcn + hb]
-        ws_ref[at, 2 * STATE + hb : 2 * STATE + 2 * hb] = thin_v[row, zhp, :, bcn : bcn + hb]
-    corner(0, 0)
-    for q in range(3):
-        pass_on(1, q, 0)
-    pass_x(0)
-    pass_x(1)
-    for q in range(3):
-        pass_on(1, q, 1)
-    corner(1, 1)
-    deal(1, 3)
-    send_x()
-    norm(0)
-    norm(1)
-    corner(1, 0)
-    corner(1, 2)
-    pass_x(2)
-    pass_x(3)
-    pass_on(1, 3, 0)
-    pass_on(1, 3, 1)
-    norm(2)
-    pass_x(4)
-    pass_x(5)
-    norm(3)
-    corner(1, 3)
-    narrow(0)
-    norm(4)
-    pass_x(6)
-    pass_x(7)
-    norm(5)
-    norm(6)
-    norm(7)
-    narrow(1)
-    prep_kernel(
+    prep_refs = (
         small_ref, segc_ref, segr_ref, bcp_ref, hp_ref,
         bc_ref, bct_ref, g_ref, gt_ref, colp_ref, cumt_ref, kexp_ref, lag_ref,
     )
+
+    def narrow(p):
+        lo, hi = p * (length // 2), (p + 1) * (length // 2)
+        small_ref[lo:hi, :] = dot_nn(nb_ref[lo:hi, :], ws_ref[...])
+        prep_rows(lo, hi, *prep_refs)
+
+    def parameters():
+        for copy in pars:
+            copy.wait_recv()
+        for n in range(3):
+            if n != 1:
+                keeps[n].wait()
+        par_out[...] = parv[...]
+        bcp_ref[...] = jnp.zeros_like(bcp_ref)
+        bcp_ref[0:5, :] = sum(parv[b, 9:14, 0 : 2 * STATE] for b in range(4))
+        hp_ref[...] = jnp.zeros_like(hp_ref)
+        hp_ref[0:2, :] = parv[me, 14:16, 0:128] + pltpu.roll(parv[zhp, 14:16, 0:128], hb, 1)
+        prep_lags(segc_ref, kexp_ref, lag_ref)
+
+    def narrow_weights():
+        for copy in sib_thin:
+            copy.wait_recv()
+        ws_ref[...] = jnp.zeros_like(ws_ref)
+        for row in range(8):
+            at = slice(row * shard, (row + 1) * shard)
+            for b in range(4):
+                ws_ref[at, b * bcn : (b + 1) * bcn] = thin_v[row, b, :, 0:bcn]
+            ws_ref[at, 2 * STATE : 2 * STATE + hb] = thin_v[row, me, :, bcn : bcn + hb]
+            ws_ref[at, 2 * STATE + hb : 2 * STATE + 2 * hb] = thin_v[row, zhp, :, bcn : bcn + hb]
+
+    send_w(0)
+    send_own(2)
+    send_x()
+    deal(0, 0)
+    send_own(3)
+    deal(0, 1)
+    send_x()
+    send_x()
+    for k in range(2):
+        keeps[3 + k].wait()
+        laid[k].start()
+    pass_on(0, 1, 1)
+    keeps[1].wait()
+    for copy in thins:
+        copy.wait_recv()
+    thin_go = [start(thin_v.at[r], thin_v.at[r], to) for to in (to_x, to_y, to_c)]
+    sib_thin.append(thin_go.pop())
+    parameters()
+    send_w(1)
+    send_own(1)
+    thin_on(0)
+    pass_on(0, 0, 0)
+    pass_x(0)
+    send_own(0)
+    send_w(2)
+    thin_on(1)
+    send_x()
+    thin_on(2)
+    pass_x(1)
+    pass_on(0, 0, 1)
+    send_w(3)
+    deal(1, 0)
+    pass_on(1, 0, 0)
+    corner(0, 1)
+    pass_x(2)
+    send_x()
+    deal(1, 1)
+    norm(0)
+    pass_x(3)
+    pass_on(1, 1, 1)
+    deal(1, 2)
+    pass_x(4)
+    send_x()
+    corner(0, 0)
+    narrow_weights()
+    deal(1, 3)
+    corner(1, 0)
+    norm(1)
+    norm(2)
+    send_x()
+    norm(3)
+    pass_x(5)
+    pass_on(1, 3, 1)
+    send_x()
+    norm(4)
+    corner(1, 1)
+    narrow(0)
+    pass_x(6)
+    pass_on(1, 2, 1)
+    pass_on(1, 3, 0)
+    pass_on(1, 1, 0)
+    pass_on(1, 2, 0)
+    norm(5)
+    pass_on(0, 1, 0)
+    pass_on(1, 0, 1)
+    pass_x(7)
+    corner(1, 2)
+    norm(6)
+    corner(1, 3)
+    norm(7)
+    narrow(1)
     for copy in sib:
         copy.wait_recv()
     for move in laid:
@@ -836,12 +872,13 @@
 
 
 GRAD_COPIES = 96
+HALVES = 2
 
 
 def grad_kernel(
-    dn_ref, raw_ref, nt_ref, dx_ref, ds_ref, small_ref, nd_ref, ir_ref, gate_ref,
+    raw_ref, wg_ref, wx_ref, ws_ref, nb_ref, gate_ref, nt_ref, dg_ref, dx_ref, ds_ref, small_ref, nd_ref, ir_ref,
     gz_ref, thin_out, small_out, own_out, away_out, row_out,
-    raw_v, pa, pr, ps, rowv, rowr, local, cs, cr, ts, tr, fs, fr, ss, sr, zs, zr, tfs, tfr, tss, tsr, tz, tzr,
+    raw_v, dn_v, wt, wst, nbt, ggv, tile_sem, pr, rowv, rowr, local, cs, cr, ts, tr, fs, fr, ss, sr, zs, zr, tfs, tfr, tss, tsr, tz, tzr,
     sbuf, srecv, szr, send, recv,
 ):
     h, l, r, c, x, y, rx, ry, rc = places()
@@ -867,54 +904,84 @@
 
         lax.fori_loop(0, width // wide, one, 0)
 
-    length, feat = ps.shape
-    piece = length // FINE
+    _, length, feat = dn_v.shape
+    piece = length // HALVES
+    strips = 4 * feat // 256
 
     def toks(p):
         return pl.ds(p * piece, piece)
 
-    raw_copy = pltpu.make_async_copy(raw_ref.at[1], raw_v, local.at[2])
+    raw_copy = pltpu.make_async_copy(raw_ref.at[1], raw_v, local.at[0])
     raw_copy.start()
-    near = [pltpu.make_async_copy(dn_ref.at[2 * k + l], pa.at[k], local.at[k]) for k in range(2)]
-    for move in near:
+
+    def loads(k, slot):
+        strip = pl.ds(pl.multiple_of(lax.rem(k, strips) * 256, 256), 256)
+        rows = pl.ds(pl.multiple_of(k // strips * piece, piece), piece)
+        return [
+            pltpu.make_async_copy(wg_ref.at[:, strip], wt.at[slot, 0], tile_sem.at[slot, 0]),
+            pltpu.make_async_copy(wx_ref.at[:, strip], wt.at[slot, 1], tile_sem.at[slot, 1]),
+            pltpu.make_async_copy(ws_ref.at[strip], wst.at[slot], tile_sem.at[slot, 2]),
+            pltpu.make_async_copy(nb_ref.at[rows, strip], nbt.at[slot], tile_sem.at[slot, 3]),
+        ]
+
+    for move in loads(0, 0):
         move.start()
-    pair, far = [], []
-
-    def give():
-        p = len(pair)
-        if p < FINE:
-            pair.append(
-                [start(dn_ref.at[2 * k + 1 - l, toks(p)], pr.at[k, toks(p)], zl) for k in range(2)]
-            )
+    ggv[...] = jnp.zeros_like(ggv)
+    pair, far, kept = [], [], []
+
+    def back(p):
+        def strip(n, carry):
+            k = p * strips + n
+            slot = lax.rem(k, 2)
+            for move in loads(k, slot):
+                move.wait()
+
+            @pl.when(k + 1 < HALVES * strips)
+            def _():
+                for move in loads(k + 1, 1 - slot):
+                    move.start()
+
+            value = dot_nt(ds_ref[toks(p), :], wst[slot])
+            for m, d_ref in enumerate((dg_ref, dx_ref)):
+                for b in range(2):
+                    value = value + dot_nt(d_ref[toks(p), b * ncol : (b + 1) * ncol], wt[slot, m, b])
+            lanes = pl.ds(pl.multiple_of(lax.rem(n, feat // 256) * 256, 256), 256)
+            dn_v[n // (feat // 256), toks(p), lanes] = value.astype(BF16)
+            ggv[pl.ds(n, 1), :] += jnp.sum(value * nbt[slot].astype(F32), axis=0, keepdims=True)
+            return carry
+
+        lax.fori_loop(0, strips, strip, 0)
+        pair.append([start(dn_v.at[2 * k + 1 - l, toks(p)], pr.at[k, toks(p)], zl) for k in range(2)])
 
     def pair_done(p):
-        if p == 0:
-            for move in near:
-                move.wait()
         for move in pair[p]:
             move.wait_recv()
-        give()
-        part = pa[1 - h, toks(p)].astype(F32) + pr[1 - h, toks(p)].astype(F32)
-        ps[toks(p)] = part.astype(BF16)
-        far.append(start(ps.at[toks(p)], away_out.at[toks(p)], zh))
-        own_out[toks(p)] = pa[h, toks(p)].astype(F32) + pr[h, toks(p)].astype(F32)
+        away, own = 2 * (1 - h) + l, 2 * h + l
+        value = dn_v[away, toks(p)].astype(F32) + pr[1 - h, toks(p)].astype(F32)
+        dn_v[away, toks(p)] = value.astype(BF16)
+        far.append(start(dn_v.at[away, toks(p)], away_out.at[toks(p)], zh))
+        value = dn_v[own, toks(p)].astype(F32) + pr[h, toks(p)].astype(F32)
+        dn_v[own, toks(p)] = value.astype(BF16)
+        kept.append(pltpu.make_async_copy(dn_v.at[own, toks(p)], own_out.at[toks(p)], local.at[1 + p]))
+        kept[p].start()
 
     z_copy = [start(gate_ref, zr.at[0], zh), None]
-    for _ in range(3):
-        give()
     rowv[...] = jnp.zeros_like(rowv)
     rowv[0:1, :] = jnp.sum(jnp.transpose(nd_ref[...]), axis=0, keepdims=True)
     rowv[1:2, :] = jnp.transpose(ir_ref[...])[0:1, :]
     row_copies = [start(rowv, rowr.at[n], to) for n, to in enumerate((zh, zl, zd))]
 
-    sbuf[0] = small_ref[...]
-    small_hops = [to_c, to_x, to_y]
-    small_copy = start(sbuf.at[0], srecv.at[0], to_c)
+    def begin_small():
+        sbuf[0] = small_ref[...]
+        for n in range(strips):
+            row, lanes = n // 4, slice(n % 4 * 256, n % 4 * 256 + 256)
+            sbuf[0, 16 + row : 17 + row, lanes] = ggv[n : n + 1, :] / small_ref[20 + row : 21 + row, lanes]
+        return start(sbuf.at[0], srecv.at[0], to_c)
 
     dx0, dx1 = dx_ref.at[:, 0:ncol], dx_ref.at[:, ncol : 2 * ncol]
     quarters = [
         dict(d=dx1, first=to_x, second=to_y, mine=x, along=y, swap=False),
-        dict(d=dx0, first=to_x, second=to_y, mine=x, along=y, swap=False),
+        dict(d=dx0, first=to_y, second=to_x, mine=y, along=x, swap=True),
         dict(first=to_y, second=to_x, mine=y, along=x, swap=True),
     ]
 
@@ -924,15 +991,27 @@
     def refs(i):
         if i == 4:
             return ts, tr, tfs, tfr, tss, tsr
-        return cs.at[i % 2], cr.at[i], fs.at[i], fr.at[i], ss.at[i], sr.at[i]
+        return cs, cr.at[i], fs.at[i // 2], fr.at[i], ss.at[i], sr.at[i]
 
     thin_q = dict(d=ds_ref, first=to_y, second=to_x, mine=y, along=x, swap=True)
+
+    def gone(i, name):
+        if i == 1:
+            earlier = quarters[0][name]
+            earlier.wait_send()
+            copies.open = [move for move in copies.open if move is not earlier]
+
+    def first_done(q):
+        if "seen" not in q:
+            q["f"].wait_recv()
+            q["seen"] = True
 
     def to_core(i, q):
         out, back = refs(i)[0:2]
         if i == 2:
             q["core"] = start(raw_ref.at[0], back, to_c)
             return
+        gone(i, "core")
 
         def body(at):
             value = product(1 - c, q["d"], at).astype(BF16)
@@ -958,16 +1037,16 @@
                     back[j, :, at] = part.astype(BF16)
 
             tiles(q["d"], body)
+        gone(i, "f")
         for n in range(2):
             fsend[n] = back[spot(q, 1 - q["mine"], n)]
         if after is not None:
-            after["f"].wait_recv()
+            first_done(after)
         q["f"] = start(fsend, frecv, q["first"])
 
     def to_second(i, q):
         _, back, _, frecv, ssend, srcv = refs(i)
-        if i != 0:
-            q["f"].wait_recv()
+        first_done(q)
         far = 1 - q["along"]
         kept = back[spot(q, q["mine"], far)].astype(F32)
         ssend[...] = (kept + frecv[far].astype(F32)).astype(BF16)
@@ -980,46 +1059,44 @@
         kept = back[spot(q, q["mine"], near)].astype(F32)
         return kept + frecv[near].astype(F32) + srcv[...].astype(F32)
 
+    def hop_small(n, to):
+        small_copy[0].wait_recv()
+        sbuf[n] = sbuf[n - 1] + srecv[n - 1]
+        if to is not None:
+            small_copy[0] = start(sbuf.at[n], srecv.at[n], to)
+
     to_core(2, quarters[2])
+    back(0)
     to_core(0, quarters[0])
     to_first(2, quarters[2])
     to_first(0, quarters[0])
+    back(1)
     pair_done(0)
     to_core(1, quarters[1])
-    pair_done(1)
+    to_second(0, quarters[0])
     to_core(4, thin_q)
-    pair_done(2)
-    small_copy.wait_recv()
-    sbuf[1] = sbuf[0] + srecv[0]
-    small_copy = start(sbuf.at[1], srecv.at[1], to_x)
-    pair_done(3)
-    to_second(2, quarters[2])
-    to_first(1, quarters[1], quarters[0])
-    to_second(0, quarters[0])
-    to_first(4, thin_q)
-    pair_done(4)
-    small_copy.wait_recv()
-    sbuf[2] = sbuf[1] + srecv[1]
-    small_copy = start(sbuf.at[2], srecv.at[2], to_y)
-    pair_done(5)
-    gz_ref[0] = settle(2, quarters[2])
+    small_copy = [begin_small()]
     zs[...] = settle(0, quarters[0]).astype(BF16)
     z_copy[1] = start(zs, zr.at[1], zh)
-    pair_done(6)
+    to_first(4, thin_q)
+    hop_small(1, to_x)
+    to_second(2, quarters[2])
+    to_first(1, quarters[1])
     to_second(4, thin_q)
-    small_copy.wait_recv()
-    sbuf[3] = sbuf[2] + srecv[2]
-    small_z = [
-        start(sbuf.at[3, lo:], szr.at[n, lo:], to) for n, (to, lo) in enumerate(((zh, 8), (zl, 16), (zd, 16)))
-    ]
-    pair_done(7)
-    to_second(1, quarters[1])
     tz[...] = settle(4, thin_q).astype(BF16)
     thin_z = []
     for n, (to, block) in enumerate(((zh, 2 * (1 - h) + l), (zl, 2 * h + 1 - l), (zd, 2 * (1 - h) + 1 - l))):
         lanes = pl.ds(pl.multiple_of(block // 2 * 128, 128), 128)
         thin_z.append(start(tz.at[:, lanes], tzr.at[n], to))
     thin_z.append(start(tz.at[:, 2 * STATE :], tzr.at[3], zh))
+    hop_small(2, to_y)
+    pair_done(1)
+    hop_small(3, None)
+    small_z = [
+        start(sbuf.at[3, lo:], szr.at[n, lo:], to) for n, (to, lo) in enumerate(((zh, 8), (zl, 16), (zd, 16)))
+    ]
+    to_second(1, quarters[1])
+    gz_ref[0] = settle(2, quarters[2])
     gz_ref[1] = settle(1, quarters[1])
     row_out[0] = rowv[...]
     for n in range(3):
@@ -1041,15 +1118,17 @@
         small_out[n + 1, lo:] = szr[n, lo:]
     for move in far:
         move.wait_recv()
+    for move in kept:
+        move.wait()
     for k in range(2):
         z_copy[k].wait_recv()
         gz_ref[k] += zr[k].astype(F32)
     copies.finish()
 
 
-def grad_all(dn, raw, nt, dxr, d_small, small, nd, ir, gate_got):
+def grad_all(raw, wg, wx, ws, nb, gate_got, nt, dgate, dxr, d_small, small, nd, ir):
     _, half, length = nt.shape
-    feat = dn.shape[2]
+    feat = half // 2
     shard, cb = half // 4, dxr.shape[1] // 2
     ns = d_small.shape[1]
     inside = pl.BlockSpec(memory_space=pltpu.VMEM)
@@ -1057,29 +1136,33 @@
     V = pltpu.VMEM
     return pl.pallas_call(
         grad_kernel,
-        in_specs=[anywhere] * 2 + [inside] * 6 + [anywhere],
-        out_specs=[inside] * 4 + [anywhere, inside],
+        in_specs=[anywhere] * 6 + [inside] * 7,
+        out_specs=[inside] * 3 + [anywhere, anywhere, inside],
         out_shape=(
             jax.ShapeDtypeStruct((2, shard, cb), F32),
             jax.ShapeDtypeStruct((shard, 384), F32),
             jax.ShapeDtypeStruct((4,) + small.shape, F32),
-            jax.ShapeDtypeStruct((length, feat), F32),
+            jax.ShapeDtypeStruct((length, feat), BF16),
             jax.ShapeDtypeStruct((length, feat), BF16),
             jax.ShapeDtypeStruct((4, 8, length), F32),
         ),
         scratch_shapes=[
             V((4, shard, cb), BF16),
+            V((4, length, feat), BF16),
+            V((2, 2, 2, 256, cb), BF16),
+            V((2, 256, ns), BF16),
+            V((2, length // HALVES, 256), BF16),
+            V((4 * feat // 256, 256), F32),
+            pltpu.SemaphoreType.DMA((2, 4)),
             V((2, length, feat), BF16),
-            V((2, length, feat), BF16),
-            V((length, feat), BF16),
             V((8, length), F32),
             V((3, 8, length), F32),
-            pltpu.SemaphoreType.DMA((3,)),
-            V((2, 4, shard, cb), BF16),
+            pltpu.SemaphoreType.DMA((1 + HALVES,)),
+            V((4, shard, cb), BF16),
             V((3, 4, shard, cb), BF16),
             V((4, shard, ns), BF16),
             V((4, shard, ns), BF16),
-            V((3, 2, shard, cb), BF16),
+            V((2, 2, shard, cb), BF16),
             V((3, 2, shard, cb), BF16),
             V((3, shard, cb), BF16),
             V((3, shard, cb), BF16),
@@ -1101,7 +1184,7 @@
             collective_id=1, has_side_effects=True, vmem_limit_bytes=VMEM_LIMIT
         ),
         name="grad_all",
-    )(dn, raw, nt, dxr, d_small, small, nd, ir, gate_got)
+    )(raw, wg, wx, ws, nb, gate_got, nt, dgate, dxr, d_small, small, nd, ir)
 
 
 def table(send, recv):
@@ -1149,8 +1232,8 @@
     def g1(p):
         return copy(p, cot_ref.at[1 - h, toks(p)], cf_ref.at[toks(p), cols(me)], zh)
 
-    def g2(p):
-        return copy(4 + p, cot_ref.at[h, toks(p)], cf_ref.at[toks(p), cols(me)], zl)
+    def g2():
+        return copy(4, cot_ref.at[h], cf_ref.at[:, cols(me)], zl)
 
     def g3(p):
         part = cf_ref.at[toks(p), cols(zhp)]
@@ -1196,34 +1279,33 @@
             load(n).start()
         for n in range(3):
             own(n).start()
-        for p in range(PIECES):
-            g2(p).start()
+        g2().start()
 
     def step1():
-        g1(0).start()
         for n in range(2):
             load(n).wait()
             keep(n).start()
+
+    def step2():
+        g1(0).start()
         for n in range(2):
             own(n).wait_recv()
         for n in range(2):
             diag(0, n).start()
             sib(0, n).start()
 
-    def step2():
+    def step3():
         g1(1).start()
+        wz().wait_recv()
+        for n in range(3):
+            got(n).start()
+
+    def step4():
+        g1(2).start()
+        g1(3).start()
         for n in range(2):
             diag(0, n).wait_recv()
         sib(0, 2).start()
-
-    def step3():
-        g1(2).start()
-        wz().wait_recv()
-        for n in range(3):
-            got(n).start()
-
-    def step4():
-        g1(3).start()
 
     def step5():
         for n in range(2):
@@ -1241,14 +1323,14 @@
     def step8():
         onward(1)
 
+    def step9():
+        onward(2)
+
     def step10():
-        onward(2)
-
-    def step12():
         onward(3)
 
     acts = {
-        0: step0, 1: step1, 2: step2, 3: step3, 4: step4, 5: step5, 6: step6, 8: step8, 10: step10, 12: step12,
+        0: step0, 1: step1, 2: step2, 3: step3, 4: step4, 5: step5, 6: step6, 8: step8, 9: step9, 10: step10,
     }
     for at, act in acts.items():
         pl.when(step == at)(act)
@@ -1294,7 +1376,7 @@
 
     @pl.when(step == 2 * groups - 1)
     def _():
-        late = [g2(p) for p in range(PIECES)] + [g3(p) for p in range(PIECES)]
+        late = [g2()] + [g3(p) for p in range(PIECES)]
         for move in late:
             move.wait_recv()
         keep(0).wait()
@@ -1470,9 +1552,9 @@
     (go_ref, po_ref, nt_ref), refs = refs[0:3], refs[3:]
     ins, refs = refs[0:20], refs[20:]
     outs, refs = refs[0:6], refs[6:]
-    own_out, got_out, raw_out, gate_out, sum0, sum1, sum2 = refs[0:7]
-    scratch, refs = refs[7:15], refs[15:]
-    gm, gr, gf, gfr, gs, gsr, tm, ts, tr, tf, tfr, tg, tgr, send, recv, local = refs
+    own_out, raw_out, gate_out, sum0, sum1, sum2 = refs[0:6]
+    scratch, refs = refs[6:14], refs[14:]
+    gm, gr, gf, gfr, gs, gsr, gz, gzr, tm, ts, tr, tf, tfr, tg, tgr, send, recv, local = refs
     h, l, _, c, x, y, rx, ry, rc = places()
     zh, zl, zd = {"zh": 1 - h}, {"zl": 1 - l}, {"zh": 1 - h, "zl": 1 - l}
     to_x, to_y, to_c = {"row": rx}, {"row": ry}, {"row": rc}
@@ -1498,6 +1580,14 @@
     def hop2(b):
         return copy(10 + b, gs.at[b], gsr.at[b], second[b])
 
+    def hop3():
+        return copy(18, gz, gzr, zh)
+
+    def settle(b):
+        hop2(b).wait_recv()
+        own = along[b]
+        return add(gm[b, spot(b, mine[b], own)], gfr[b, own]) + gsr[b].astype(F32)
+
     def out_sums():
         late = pl.ds(EARLY, po_ref.shape[1] - EARLY)
         return [
@@ -1531,7 +1621,7 @@
         for move in out_sums():
             move.start()
 
-    @pl.when(step == 2)
+    @pl.when(step == 1)
     def _():
         for b in range(2):
             for j in range(4):
@@ -1545,13 +1635,16 @@
                 j = spot(b, mine[b], s)
                 gm[b, j] = add(gm[b, j], gr[b, j]).astype(BF16)
 
-    @pl.when(step == 5)
+    @pl.when(step == 4)
     def _():
         for b in range(2):
             hop1(b).wait_recv()
             far = 1 - along[b]
             gs[b] = add(gm[b, spot(b, mine[b], far)], gfr[b, far]).astype(BF16)
             hop2(b).start()
+
+    @pl.when(step == 5)
+    def _():
         gate_core().wait_recv()
         for n in range(2):
             tf[n] = add(tm[spot(1, 1 - y, n)], tr[spot(1, 1 - y, n)]).astype(BF16)
@@ -1559,6 +1652,11 @@
         for n in range(2):
             tm[spot(1, y, n)] = add(tm[spot(1, y, n)], tr[spot(1, y, n)]).astype(BF16)
 
+    @pl.when(step == 6)
+    def _():
+        gz[...] = settle(1).astype(BF16)
+        hop3().start()
+
     @pl.when(step == groups - 1)
     def _():
         gate_hop1().wait_recv()
@@ -1588,11 +1686,9 @@
 
     @pl.when(step == groups - 1)
     def _():
-        for b, out in enumerate((own_out, got_out)):
-            hop2(b).wait_recv()
-            own = along[b]
-            total = add(gm[b, spot(b, mine[b], own)], gfr[b, own]) + gsr[b].astype(F32)
-            out[...] = total.astype(out.dtype)
+        own_out[...] = settle(0)
+        hop3().wait_recv()
+        own_out[...] += gzr[...].astype(F32)
         gate_hop2().wait_recv()
         total = add(tm[spot(1, y, x)], tfr[x]) + tgr[...].astype(F32)
         gate_out[...] = total.astype(BF16)
@@ -1601,7 +1697,7 @@
                 core(b, j).wait_send()
             hop1(b).wait_send()
             hop2(b).wait_send()
-        for move in (gate_core(), gate_hop1(), gate_hop2()):
+        for move in (gate_core(), gate_hop1(), gate_hop2(), hop3()):
             move.wait_send()
         for move in out_sums():
             move.wait()
@@ -1623,7 +1719,6 @@
         out_specs=outs
         + [
             once((shard, cb)),
-            once((shard, cb)),
             pl.BlockSpec((2, 4, shard, GROUP), lambda g: (0, 0, 0, jnp.maximum(g - groups // 2, 0))),
             once((shard, cb)),
             anywhere,
@@ -1633,7 +1728,6 @@
         out_shape=shapes
         + (
             jax.ShapeDtypeStruct((shard, cb), F32),
-            jax.ShapeDtypeStruct((shard, cb), BF16),
             jax.ShapeDtypeStruct((2, 4, shard, cb), BF16),
             jax.ShapeDtypeStruct((shard, cb), BF16),
             jax.ShapeDtypeStruct((length, feat), BF16),
@@ -1648,6 +1742,8 @@
             V((2, 2, shard, cb), BF16),
             V((2, shard, cb), BF16),
             V((2, shard, cb), BF16),
+            V((shard, cb), BF16),
+            V((shard, cb), BF16),
             V((4, shard, cb), BF16),
             V((4, shard, cb), BF16),
             V((4, shard, cb), BF16),
@@ -1712,6 +1808,11 @@
 
         def by_seq(own, away):
             return jnp.where(first_h, jnp.stack([own, away]), jnp.stack([away, own]))
+
+        def place(own, away):
+            both = jnp.zeros((2,) + own.shape, own.dtype)
+            both = lax.dynamic_update_slice(both, own[None], (mh, 0, 0))
+            return lax.dynamic_update_slice(both, away[None], (1 - mh, 0, 0)).reshape(-1, own.shape[1])
 
         def gather_features(v):
             own, away = mine(seqs(v)), other(seqs(v))
@@ -1811,19 +1912,23 @@
         )
         if direct:
             (
-                dgates, dxrs, chg, nd, d_small, pg, g_own, g_got, gate_own, gate_got, sum0, sum1, sum2,
+                dgates, dxrs, chg, nd, d_small, pg, g_wout, gate_own, gate_got, sum0, sum1, sum2,
             ) = scan_grad_all(g_out, partial_out, normed_t, *grad_args)
-            g_wout = g_own + swap(g_got).astype(F32)
-            own = lax.dynamic_index_in_dim(partial_out, here, 0, keepdims=False)
+            own = lax.dynamic_index_in_dim(partial_out, here, 0, keepdims=False).astype(F32)
+            own = own + sum0.astype(F32) + mine(seqs(tokens)).astype(F32)
             away = sum1.astype(F32) + jnp.concatenate([sum3, sum2], axis=0).astype(F32)
-            out_here = by_seq(own.astype(F32) + sum0.astype(F32), away)
+            away = away + other(seqs(tokens)).astype(F32)
+            output = place(own.astype(BF16), away.astype(BF16))
         else:
             dgates, dxrs, chg, nd, d_small, pg = scan_grad(*grad_args)
-        output = (out_here + seqs(tokens)).astype(BF16).reshape(tokens.shape)
+            output = (out_here + seqs(tokens)).astype(BF16).reshape(tokens.shape)
         g_dtb, g_alog = pg[5, : 2 * hb], pg[6, : 2 * hb]
         g_bcs = pg[: KW + 1]
-        dn, gg = back(dgates, dxrs, d_small, w_gate, w_x, w_small, normed)
-        g_gain = gg[0] / gain
+
+        def finish(pick, d, root, dot):
+            root, dot = root[:, None], dot[:, None]
+            grad = pick(seqs(cotangent)).astype(F32) + root * norm_gain * d
+            return (grad - pick(seqs(tokens)).astype(F32) * (root * root / width * dot)).astype(BF16)
 
         if direct:
             rows = []
@@ -1831,15 +1936,15 @@
                 hs = slice(b * hb, (b + 1) * hb)
                 heads = jnp.concatenate([g_dtb[hs], g_alog[hs]])
                 rows += [chg[0:7, b * cb : (b + 1) * cb], jnp.pad(heads, (0, cb - 2 * hb))[None]]
-            last = jnp.concatenate([g_gain, g_bcs.reshape(-1)])
-            last = jnp.pad(last, (0, 8 * cb - last.shape[0])).reshape(8, cb)
+            last = jnp.pad(g_bcs.reshape(-1), (0, width - g_bcs.size))
+            last = jnp.concatenate([jnp.zeros_like(gain), last, gain, jnp.zeros_like(gain)]).reshape(8, cb)
             gz, thins, smalls, d_own, d_away, rowv = grad_all(
-                dn, gate_own, normed_t, dxrs, d_small, jnp.concatenate(rows + [last], axis=0), nd, inv_root,
-                gate_got,
+                gate_own, w_gate, w_x, w_small, normed, gate_got, normed_t, dgates, dxrs, d_small,
+                jnp.concatenate(rows + [last], axis=0), nd, inv_root,
             )
-            d_here = by_seq(d_own, d_away.astype(F32))
-            roots = by_seq(rowv[0, 1], rowv[1, 1])
-            dots = by_seq(rowv[0, 0] + rowv[2, 0], rowv[1, 0] + rowv[3, 0])
+            own = finish(mine, d_own.astype(F32), rowv[0, 1], rowv[0, 0] + rowv[2, 0])
+            away = finish(other, d_away.astype(F32), rowv[1, 1], rowv[1, 0] + rowv[3, 0])
+            tokens_grad = place(own, away)
             g_zx = jnp.transpose(gz, (1, 0, 2))
             g_bc = lax.dynamic_slice(thins, (0, ml * bcn), (thins.shape[0], bcn))
             g_dt = thins[:, 128 : 128 + hb] + thins[:, 256 + hb : 256 + 2 * hb]
@@ -1850,10 +1955,13 @@
             g_bcs = lax.dynamic_index_in_dim(g_bcs, here, 1, keepdims=False)
             g_dtb, g_alog = chg[7, :hb], chg[7, hb : 2 * hb]
         else:
+            dn, gg = back(dgates, dxrs, d_small, w_gate, w_x, w_small, normed)
+            g_gain = gg[0] / gain
             d_here = scatter_features(jnp.moveaxis(dn, 0, 1).reshape(length, width))
             dots = pair_sum(jnp.sum(nd, axis=1))
-            dots = by_seq(dots, swap(dots))
-            roots = by_seq(inv_root[:, 0], swap(inv_root[:, 0]))
+            own = finish(mine, mine(d_here), inv_root[:, 0], dots)
+            away = finish(other, other(d_here), swap(inv_root[:, 0]), swap(dots))
+            tokens_grad = place(own, away)
 
             def join(own, away):
                 return own.astype(F32) + swap(away).astype(F32)
@@ -1876,10 +1984,6 @@
             g_dtb = g_dtb[:hb] + swap(g_dtb[hb:])
             g_alog = g_alog[:hb] + swap(g_alog[hb:])
             chg, g_dtb, g_alog = lax.psum((chg, g_dtb, g_alog), "row")
-        roots, dots = roots[..., None], dots[..., None]
-        x32 = seqs(tokens).astype(F32)
-        tokens_grad = seqs(cotangent) + roots * norm_gain * d_here - x32 * (roots * roots / width * dots)
-        tokens_grad = tokens_grad.astype(BF16).reshape(tokens.shape)
         return (
             output,
             tokens_grad,

time: 604 us -> 557 us (0.922)
  Pallas kernels: 534 us -> 501 us
  other arithmetic: 21.6 us -> 12.5 us
    pallas_call x1, Pallas kernels: 112 us -> 100 us  [scan_grad_all(): pl.pallas_call(scan_grad_all_kernel, grid=(groups,), in_specs=[anywhere,...]
    pallas_call x2 -> x1, Pallas kernels: 152 us -> 143 us  [grad_all(): pl.pallas_call(grad_kernel, in_specs=[anywhere] * 6 + [inside] * 7, out_s...]
    another operation x4 -> x0, other arithmetic: 7.39 us -> none  [by_seq(): return jnp.where(first_h, jnp.stack([own, away]), jnp.stack([away, own]))]
    dynamic_update_slice x0 -> x3, other arithmetic: none -> 7.09 us  [the longest x2 3.82 us: place(): lax.dynamic_update_slice(both, away[None], (1 - mh, 0, 0))]
    pallas_call x1, Pallas kernels: 133 us -> 127 us  [gather_all(): pl.pallas_call(gather_kernel, in_specs=[anywhere] * 5 + [inside] * 2, out...]
  transfers between devices with their start and end apart: 1 -> 0, of which waited for: 0 -> 0; matrix products, arithmetic and copies ran while one was open for 5% -> 0% of each run, Pallas kernels for 26% -> 0%
where the time goes in v4:
time: 557 us; the launch traced here: 546 us
  Pallas kernels  501 us (90%)
  local copies, waits for them, and re-layouts  31.8 us (6%)
  other arithmetic  12.5 us (2%)
    pallas_call x1, Pallas kernels, grad_all(): pl.pallas_call(grad_kernel, in_specs=[anywhere] * 6 + [inside] * 7, out_s...  143 us
    pallas_call x1, Pallas kernels, gather_all(): pl.pallas_call(gather_kernel, in_specs=[anywhere] * 5 + [inside] * 2, out...  127 us
    pallas_call x1, Pallas kernels, scan_grad_all(): pl.pallas_call(scan_grad_all_kernel, grid=(groups,), in_specs=[anywhere,...  100 us
    pallas_call x1, Pallas kernels, scan_all(): pl.pallas_call(scan_all_kernel, grid=(2 * groups,), in_specs=[anywhere] *...  97.5 us
    pallas_call x1, Pallas kernels, middle(): pl.pallas_call(mid_kernel, grid=(2, n), in_specs=[const((length, width)),...  33.6 us

profile of v4, /device:TPU:0, one launch (start us, length us, event | category | flops | bytes accessed | tf_op | source)
XLA Modules:
  0.0 546.2 jit_solution(10716963159033117733)
XLA Ops:
  4.3 0.7 select_maximum_fusion.2
  5.0 2.0 concatenate.44.par_ref
  7.0 1.0 broadcast_in_dim.65.segc_ref.refs_18_
  8.7 3.3 fusion.18
  12.0 1.3 copy_bitcast_fusion
  14.4 126.6 %gather_all.1 = (bf16[1024,2048]{1,0:T(8,128)(2,1)}, bf16[2,1024,1024]{2,1,0:T(8,128)(2,1)}, f32[1024,128]{1,0:T(8,128)}, f32[4,16,1024]{2,1,0:T(8,128)}, bf16[2...) custom-call(bf16[2,1024,512]{2,1,0:T(8,128)(2,1)} %bitcast.85, ...), custom_call_target="tpu_custom_call" | custom-call | tf_op jit(solution)/shard_map/gather_all/pallas_call | solution.py:842
  141.0 0.8 dynamic-slice_bitcast_fusion
  142.5 0.8 broadcast_in_dim.67
  144.0 97.5 %scan_all.1 = (f32[1024,2048]{1,0:T(8,128)}, f32[1024,2048]{1,0:T(8,128)}, f32[1024,2048]{1,0:T(8,128)}, bf16[1024,2048]{1,0:T(8,128)(2,1)}, f32[1024,128]{1,0:T...) custom-call(bf16[2,1024,512]{2,1,0:T(8,128)(2,1)} %bitcast.89, ...), custom_call_target="tpu_custom_call" | custom-call | tf_op jit(solution)/shard_map/scan_all/pallas_call | solution.py:1408
  241.5 33.6 %middle.1 = (bf16[1024,2048]{1,0:T(8,128)(2,1)}, bf16[8,256,2048]{2,1,0:T(8,128)(2,1)}, f32[1024,128]{1,0:T(8,128)}, bf16[640,512]{1,0:T(8,128)(2,1)}) custom-call(bf16[1024,2048]{1,0:T(8,128)(2,1)} %get-tuple-element.76.cf_ref, bf16[2,2048,1024]{2,1,0:T(8,128)(2,1)} %get-tuple-element.77.wc_ref, bf16[1024,2048]{1,0:T(8,128)(2,1)} %get-tuple-element.78.hid_ref, ...), custom_call_target="tpu_custom_call" | custom-call | tf_op jit(solution)/shard_map/middle/pallas_call | solution.py:1511
  275.1 100.5 %scan_grad_all.1 = (bf16[1024,2048]{1,0:T(8,128)(2,1)}, bf16[1024,2048]{1,0:T(8,128)(2,1)}, f32[8,2048]{1,0:T(8,128)}, f32[1024,128]{1,0:T(8,128)}, bf16[1024,38...) custom-call(bf16[8,256,2048]{2,1,0:T(8,128)(2,1)} %get-tuple-element, ...), custom_call_target="tpu_custom_call" | custom-call | tf_op jit(solution)/shard_map/scan_grad_all/pallas_call | solution.py:1715
  375.6 0.9 slice_bitcast_fusion.4
  376.6 0.8 fusion.20
  378.1 0.9 slice_reduce_fusion.1
  379.0 1.9 concatenate.52.small_ref
  380.9 142.6 %grad_all.1 = (f32[2,256,1024]{2,1,0:T(8,128)}, f32[256,384]{1,0:T(8,128)}, f32[4,24,1024]{2,1,0:T(8,128)}, bf16[1024,512]{1,0:T(8,128)(2,1)}, bf16[1024,512]{1,0:T(8,128)(2,1)}, /*index=5*/f32[4,8,1024]{2,1,0:T(8,128)}) custom-call(bf16[2,4,256,1024]{3,2,1,0:T(8,128)(2,1)} %get-tuple-element.96.raw_ref, ...), custom_call_target="tpu_custom_call" | custom-call | tf_op jit(solution)/shard_map/grad_all/pallas_call | solution.py:1137
  523.5 1.0 fusion.19
  524.5 1.5 broadcast.34.clone
  526.0 3.3 fusion.11
  529.4 1.4 copy-done.3
  530.9 3.3 fusion.7
  534.7 1.3 copy-done.5
  536.1 2.9 copy.42
  545.0 1.0 copy.59
  (80 shorter events, 14.2 us)
Async XLA Ops:
  0.6 6.4 %copy-start = (s32[2,1024]{1,0:T(2,128)S(1)}, s32[2,1024]{1,0:T(2,128)}, u32[]{:S(2)}) copy-start(s32[2,1024]{1,0:T(2,128)} %param.17) | copy-start | bytes 24580
  12.0 1.4 copy-start.14
  12.0 1.5 copy-start.18
  13.5 128.3 %copy-start.13 = (f32[4,1024]{1,0:T(4,128)S(1)}, f32[4,1024]{1,0:T(4,128)}, u32[]{:S(2)}) copy-start(f32[4,1024]{1,0:T(4,128)} %param.22) | copy-start | bytes 49156
  13.5 128.3 %copy-start.16 = (f32[1024]{0:T(1024)S(1)}, f32[1024]{0:T(1024)}, u32[]{:S(2)}) copy-start(f32[1024]{0:T(1024)} %param.23) | copy-start | bytes 12292
  13.5 128.3 %copy-start.17 = (f32[1024]{0:T(1024)S(1)}, f32[1024]{0:T(1024)}, u32[]{:S(2)}) copy-start(f32[1024]{0:T(1024)} %param.29) | copy-start | bytes 12292
  523.5 2.5 copy-start.2
  523.5 2.5 copy-start.15
  526.0 3.4 copy-start.7
  529.3 1.6 copy-start.3
  530.9 3.3 copy-start.6
  530.9 3.3 copy-start.9
  530.9 3.3 copy-start.10
  534.2 1.9 copy-start.5
  534.7 4.3 copy-start.4
  536.1 3.0 copy-start.11
  536.1 4.6 copy-start.12
  536.1 8.9 %copy-start.8 = (f32[256,1024]{1,0:T(8,128)S(1)}, f32[256,1024]{1,0:T(8,128)}, u32[]{:S(2)}) copy-start(f32[256,1024]{1,0:T(8,128)} %get-tuple-element.193) | copy-start | bytes 3145732
  536.1 9.9 %copy-start.1 = (s32[2,1024]{1,0:T(2,128)S(1)}, s32[2,1024]{1,0:T(2,128)}, u32[]{:S(2)}) copy-start(s32[2,1024]{1,0:T(2,128)} %param.17) | copy-start | bytes 24580
